TPU v7x, 32 devices: a whole 2x2x4 slice. The times are simulated.
32 devices in a mesh: batch: 4 (over x, core), seq: 8 (over z, y).
Axes of the slice: x: 2, y: 2, z: 4, core: 2. Of those that a mesh axis runs over, the one named last changes fastest.
Arguments:
- tokens: bfloat16 [4096, 2048], P(('batch', 'seq')), may hold values from -6 to 6
- ln1_gain: float32 [2048], replicated, may hold values from 0.5 to 1.5
- ln1_bias: float32 [2048], replicated, may hold values from -1 to 1
- w_qkv: bfloat16 [2048, 6144], P(('batch', 'seq')), may hold values from -0.125 to 0.125
- b_qkv: float32 [6144], replicated, may hold values from -1.5 to 1.5
- w_out: bfloat16 [2048, 2048], P(('batch', 'seq')), may hold values from -1 to 1
- b_out: float32 [2048], replicated, may hold values from -1 to 1
- ln2_gain: float32 [2048], replicated, may hold values from 0.5 to 1.5
- ln2_bias: float32 [2048], replicated, may hold values from -1 to 1
- w_gate: bfloat16 [2048, 5461], P(('batch', 'seq')), may hold values from -0.125 to 0.125
- b_gate: float32 [5461], replicated, may hold values from -1.5 to 1.5
- w_up: bfloat16 [2048, 5461], P(('batch', 'seq')), may hold values from -0.125 to 0.125
- b_up: float32 [5461], replicated, may hold values from -1.5 to 1.5
- w_down: bfloat16 [2048, 5461], P(('batch', 'seq')), may hold values from -0.078125 to 0.078125
- b_down: float32 [2048], replicated, may hold values from -1 to 1
- protein_lengths: int32 [4, 6], P('batch'), may hold values from 1 to 898, 1024 in all within a row
- prefix_lengths: int32 [4, 6], P('batch'), may hold values from 1 to 1024
- out_grad: bfloat16 [4096, 2048], P(('batch', 'seq')), may hold values from -6 to 6
Outputs:
- output: bfloat16 [4096, 2048], P(('batch', 'seq'))
- tokens_grad: bfloat16 [4096, 2048], P(('batch', 'seq'))
- ln1_gain_grad: float32 [2048], replicated
- ln1_bias_grad: float32 [2048], replicated
- w_qkv_grad: float32 [2048, 6144], P(('batch', 'seq'))
- b_qkv_grad: float32 [6144], replicated
- w_out_grad: float32 [2048, 2048], P(('batch', 'seq'))
- b_out_grad: float32 [2048], replicated
- ln2_gain_grad: float32 [2048], replicated
- ln2_bias_grad: float32 [2048], replicated
- w_gate_grad: float32 [2048, 5461], P(('batch', 'seq'))
- b_gate_grad: float32 [5461], replicated
- w_up_grad: float32 [2048, 5461], P(('batch', 'seq'))
- b_up_grad: float32 [5461], replicated
- w_down_grad: float32 [2048, 5461], P(('batch', 'seq'))
- b_down_grad: float32 [2048], replicated
Inputs may be any that keep to these rules, and one draw needn't show every extreme that they name: `protein_lengths`: each row holds the lengths of the 6 proteins packed in order into one group; a row sums to 1024, and its longest protein has exactly 898 tokens.
All inputs are finite; a program needn't handle non-finite values.
Results may differ from a plain program's by a relative error of at most 0.014.
Values may be sent and summed in bfloat16 or wider, within the bound.
No kernel may reach another device: no remote copies, remote signals or barrier semaphores. Data moves between devices by JAX's collectives and lax.ppermute only.
A program may use at most 704 MiB of HBM per device.

v0:
```python
import math

import jax
import jax.numpy as jnp
from jax import lax
from jax.sharding import PartitionSpec as P

HEADS = 16
HEAD = 128


epsilon = 1e-05
masked_value = -1000000000.0


def layer_norm(values, gain, bias):
    average = jnp.mean(values, axis=-1, keepdims=True)
    centered = values - average
    spread = jnp.mean(centered * centered, axis=-1, keepdims=True)
    return centered * lax.rsqrt(spread + epsilon) * gain + bias


def gelu_tanh(values):
    return (
        0.5
        * values
        * (1.0 + jnp.tanh(0.7978845608028654 * (values + 0.044715 * values * values * values)))
    )


def geglu(gate, upper):
    return gelu_tanh(gate) * upper


def group_layout(lengths, prefixes, count):
    ends = jnp.cumsum(lengths)
    starts = ends - lengths
    places = jnp.arange(count, dtype=jnp.int32)
    member = ((places[:, None] >= starts[None, :]) & (places[:, None] < ends[None, :])).astype(
        jnp.int32
    )
    numbers = jnp.arange(lengths.shape[0], dtype=jnp.int32)
    segment = jnp.sum(member * numbers[None, :], axis=1)
    first = jnp.sum(member * starts[None, :], axis=1)
    limits = starts + jnp.minimum(prefixes, lengths)
    bound = jnp.sum(member * limits[None, :], axis=1)
    return (segment, bound, places - first)


def rotary_tables(position):
    half_size = HEAD // 2
    rates = jnp.exp(jnp.arange(half_size, dtype=jnp.float32) * (-2.0 * math.log(10000.0) / HEAD))
    angles = position.astype(jnp.float32)[:, None] * rates[None, :]
    cosine = jnp.cos(angles)
    sine = jnp.sin(angles)
    return (jnp.concatenate([cosine, cosine], axis=1), jnp.concatenate([sine, sine], axis=1))


def rotate(values, cosine, sine):
    half_size = values.shape[-1] // 2
    turned = jnp.concatenate([-values[..., half_size:], values[..., :half_size]], axis=-1)
    return values * cosine[:, None, :] + turned * sine[:, None, :]


def allowed_keys(segment, bound, begin, block_rows):
    key_places = jnp.arange(segment.shape[0], dtype=jnp.int32)
    query_places = begin + jnp.arange(block_rows, dtype=jnp.int32)
    query_segment = lax.dynamic_slice_in_dim(segment, begin, block_rows, 0)
    query_bound = lax.dynamic_slice_in_dim(bound, begin, block_rows, 0)
    same = query_segment[:, None] == segment[None, :]
    return same & (
        (key_places[None, :] <= query_places[:, None])
        | (key_places[None, :] < query_bound[:, None])
    )


def contract_last(left, right):
    return lax.dot_general(
        left, right, (((1,), (1,)), ((), ())), preferred_element_type=jnp.float32
    )


def contract_first(left, right):
    return lax.dot_general(
        left, right, (((0,), (0,)), ((), ())), preferred_element_type=jnp.float32
    )


def masked_scores(packed, segment, bound, begin, block_rows):
    query_block = lax.dynamic_slice_in_dim(packed[:, 0], begin, block_rows, 0)
    scores = jnp.einsum(
        "bhe,khe->hbk", query_block, packed[:, 1], preferred_element_type=jnp.float32
    ) * HEAD ** (-0.5)
    allowed = allowed_keys(segment, bound, begin, block_rows)
    return (query_block, jnp.where(allowed[None], scores, masked_value))


def attend_forward(packed, segment, bound):
    count = packed.shape[0]
    block_rows = min(512, count)

    def one_block(block_index):
        begin = block_index * block_rows
        query_block, scores = masked_scores(packed, segment, bound, begin, block_rows)
        largest = jnp.max(scores, axis=-1, keepdims=True)
        powers = jnp.exp(scores - largest)
        totals = jnp.sum(powers, axis=-1, keepdims=True)
        probs = (powers / totals).astype(jnp.bfloat16)
        result = jnp.einsum("hbk,khe->bhe", probs, packed[:, 2], preferred_element_type=jnp.float32)
        return (result.astype(jnp.bfloat16), largest[..., 0] + jnp.log(totals[..., 0]))

    results, log_sums = lax.map(one_block, jnp.arange(count // block_rows, dtype=jnp.int32))
    return (results.reshape(count, packed.shape[2], packed.shape[3]), log_sums)


def attend_backward(packed, grad_heads, log_sums, segment, bound):
    count = packed.shape[0]
    block_rows = min(512, count)
    scale = HEAD ** (-0.5)
    keys_all = packed[:, 1]
    values_all = packed[:, 2]

    def one_block(carry, item):
        key_grad, value_grad = carry
        block_index, block_lse = item
        begin = block_index * block_rows
        query_block, scores = masked_scores(packed, segment, bound, begin, block_rows)
        probs = jnp.exp(scores - block_lse[..., None])
        low_probs = probs.astype(jnp.bfloat16)
        grad_block = lax.dynamic_slice_in_dim(grad_heads, begin, block_rows, 0)
        grad_probs = jnp.einsum(
            "bhe,khe->hbk", grad_block, values_all, preferred_element_type=jnp.float32
        )
        delta = jnp.sum(probs * grad_probs, axis=-1, keepdims=True)
        grad_scores = (probs * (grad_probs - delta)).astype(jnp.bfloat16)
        query_grad = (
            jnp.einsum("hbk,khe->bhe", grad_scores, keys_all, preferred_element_type=jnp.float32)
            * scale
        )
        key_grad = (
            key_grad
            + jnp.einsum(
                "hbk,bhe->khe", grad_scores, query_block, preferred_element_type=jnp.float32
            )
            * scale
        )
        value_grad = value_grad + jnp.einsum(
            "hbk,bhe->khe", low_probs, grad_block, preferred_element_type=jnp.float32
        )
        return ((key_grad, value_grad), query_grad)

    zeros_kv = jnp.zeros(keys_all.shape, jnp.float32)
    (key_grad, value_grad), query_grad = lax.scan(
        one_block,
        (zeros_kv, zeros_kv),
        (jnp.arange(count // block_rows, dtype=jnp.int32), log_sums),
    )
    query_grad = query_grad.reshape(keys_all.shape)
    return jnp.stack([query_grad, key_grad, value_grad], axis=1).astype(jnp.bfloat16)


def per_device(
    tokens,
    ln1_gain,
    ln1_bias,
    w_qkv,
    b_qkv,
    w_out,
    b_out,
    ln2_gain,
    ln2_bias,
    w_gate,
    b_gate,
    w_up,
    b_up,
    w_down,
    b_down,
    protein_lengths,
    prefix_lengths,
    out_grad,
):
    seq_count = lax.axis_size("seq")
    tok_rows = tokens.shape[0]
    width = tokens.shape[1]
    group_count = tok_rows * seq_count
    segment, bound, position = group_layout(protein_lengths[0], prefix_lengths[0], group_count)
    own_position = lax.dynamic_slice_in_dim(position, lax.axis_index("seq") * tok_rows, tok_rows, 0)
    cosine, sine = rotary_tables(own_position)
    inputs = tokens.astype(jnp.float32)
    qkv_full, out_full = (
        lax.all_gather(w_qkv, ("batch", "seq"), axis=0, tiled=True),
        lax.all_gather(w_out, ("batch", "seq"), axis=0, tiled=True),
    )
    normed = layer_norm(inputs, ln1_gain, ln1_bias).astype(jnp.bfloat16)
    raw = (jnp.dot(normed, qkv_full, preferred_element_type=jnp.float32) + b_qkv).reshape(
        tok_rows, 3, HEADS, HEAD
    )
    sent = jnp.stack(
        [rotate(raw[:, 0], cosine, sine), rotate(raw[:, 1], cosine, sine), raw[:, 2]], axis=1
    ).astype(jnp.bfloat16)
    packed = lax.all_to_all(sent, "seq", split_axis=2, concat_axis=0, tiled=True)
    head_result, log_sums = attend_forward(packed, segment, bound)
    attended = lax.all_to_all(head_result, "seq", split_axis=0, concat_axis=1, tiled=True).reshape(
        tok_rows, width
    )
    hidden_in = inputs + jnp.dot(attended, out_full, preferred_element_type=jnp.float32) + b_out
    gate_full, up_full, down_full = (
        lax.all_gather(w_gate, ("batch", "seq"), axis=0, tiled=True),
        lax.all_gather(w_up, ("batch", "seq"), axis=0, tiled=True),
        lax.all_gather(w_down, ("batch", "seq"), axis=0, tiled=True),
    )
    normed_two = layer_norm(hidden_in, ln2_gain, ln2_bias).astype(jnp.bfloat16)
    gate = jnp.dot(normed_two, gate_full, preferred_element_type=jnp.float32) + b_gate
    upper = jnp.dot(normed_two, up_full, preferred_element_type=jnp.float32) + b_up
    act = geglu(gate, upper).astype(jnp.bfloat16)
    ffn = contract_last(act, down_full) + b_down
    output = (hidden_in + ffn).astype(jnp.bfloat16)
    cotangent = out_grad.astype(jnp.float32)
    grad_act = jnp.dot(out_grad, down_full, preferred_element_type=jnp.float32)
    geglu_out, geglu_pull = jax.vjp(geglu, gate, upper)
    grad_gate, grad_up = geglu_pull(grad_act)
    grad_gate = grad_gate.astype(jnp.bfloat16)
    grad_up = grad_up.astype(jnp.bfloat16)
    grad_normed_two = contract_last(grad_gate, gate_full) + contract_last(grad_up, up_full)
    norm_two_out, norm_two_pull = jax.vjp(layer_norm, hidden_in, ln2_gain, ln2_bias)
    grad_ln_two, gain_two_grad, bias_two_grad = norm_two_pull(grad_normed_two)
    grad_hidden = cotangent + grad_ln_two
    left_cols = normed_two
    ffn_shares = lax.psum_scatter(
        jnp.concatenate(
            [
                contract_first(left_cols, grad_gate),
                contract_first(left_cols, grad_up),
                contract_first(out_grad, act),
            ],
            axis=1,
        ),
        ("batch", "seq"),
        scatter_dimension=0,
        tiled=True,
    )
    ffn_width = w_gate.shape[1]
    grad_attn = grad_hidden.astype(jnp.bfloat16)
    grad_attended = (
        contract_last(grad_attn, out_full).astype(jnp.bfloat16).reshape(tok_rows, HEADS, HEAD)
    )
    grad_heads = lax.all_to_all(grad_attended, "seq", split_axis=1, concat_axis=0, tiled=True)
    grad_packed = attend_backward(packed, grad_heads, log_sums, segment, bound)
    grad_sent = lax.all_to_all(grad_packed, "seq", split_axis=0, concat_axis=2, tiled=True).astype(
        jnp.float32
    )
    rotate_out, rotate_pull = jax.vjp(lambda values: rotate(values, cosine, sine), raw[:, 0])
    grad_query = rotate_pull(grad_sent[:, 0])[0]
    grad_key = rotate_pull(grad_sent[:, 1])[0]
    grad_raw = (
        jnp.stack([grad_query, grad_key, grad_sent[:, 2]], axis=1)
        .reshape(tok_rows, 3 * width)
        .astype(jnp.bfloat16)
    )
    grad_normed = contract_last(grad_raw, qkv_full)
    norm_one_out, norm_one_pull = jax.vjp(layer_norm, inputs, ln1_gain, ln1_bias)
    grad_ln_one, gain_one_grad, bias_one_grad = norm_one_pull(grad_normed)
    tokens_grad = (grad_hidden + grad_ln_one).astype(jnp.bfloat16)
    left_cols = normed
    attn_shares = lax.psum_scatter(
        jnp.concatenate(
            [contract_first(left_cols, grad_raw), contract_first(attended, grad_attn)], axis=1
        ),
        ("batch", "seq"),
        scatter_dimension=0,
        tiled=True,
    )
    small_terms = (
        gain_one_grad,
        bias_one_grad,
        jnp.sum(grad_raw.astype(jnp.float32), axis=0),
        jnp.sum(grad_attn.astype(jnp.float32), axis=0),
        gain_two_grad,
        bias_two_grad,
        jnp.sum(grad_gate.astype(jnp.float32), axis=0),
        jnp.sum(grad_up.astype(jnp.float32), axis=0),
        jnp.sum(cotangent, axis=0),
    )
    summed = lax.psum(
        (
            small_terms[0],
            small_terms[1],
            small_terms[2],
            small_terms[3],
            small_terms[4],
            small_terms[5],
            small_terms[6],
            small_terms[7],
            small_terms[8],
        ),
        ("batch", "seq"),
    )
    return (
        output,
        tokens_grad,
        summed[0],
        summed[1],
        attn_shares[:, : 3 * width],
        summed[2],
        attn_shares[:, 3 * width :],
        summed[3],
        summed[4],
        summed[5],
        ffn_shares[:, :ffn_width],
        summed[6],
        ffn_shares[:, ffn_width : 2 * ffn_width],
        summed[7],
        ffn_shares[:, 2 * ffn_width :],
        summed[8],
    )


def solution(mesh):
    in_specs = (
        P(("batch", "seq"), None),
        P(),
        P(),
        P(("batch", "seq"), None),
        P(),
        P(("batch", "seq"), None),
        P(),
        P(),
        P(),
        P(("batch", "seq"), None),
        P(),
        P(("batch", "seq"), None),
        P(),
        P(("batch", "seq"), None),
        P(),
        P("batch", None),
        P("batch", None),
        P(("batch", "seq"), None),
    )
    out_specs = (
        P(("batch", "seq"), None),
        P(("batch", "seq"), None),
        P(),
        P(),
        P(("batch", "seq"), None),
        P(),
        P(("batch", "seq"), None),
        P(),
        P(),
        P(),
        P(("batch", "seq"), None),
        P(),
        P(("batch", "seq"), None),
        P(),
        P(("batch", "seq"), None),
        P(),
    )
    return jax.shard_map(
        per_device, mesh=mesh, in_specs=in_specs, out_specs=out_specs, check_vma=False
    )
```

profile of v0, /device:TPU:0, one launch (start us, length us, event | category | flops | bytes accessed | tf_op | source)
XLA Modules:
  0.0 4554.7 jit_solution(7612719790226827556)
XLA Ops:
  12.0 156.4 %all-gather.6.cloned.1.call-done = bf16[2048,6144]{1,0:T(8,128)(2,1)} async-done(((bf16[64,6144]{1,0:T(8,128)(2,1)}), bf16[2048,6144]{1,0:T(8,128)(2,1)}) %all-gather.6.cloned.1.call-update) | async-done | bytes 25165840 | tf_op jit(solution)/shard_map/all_gather | solution.py:191
  168.4 10.1 fusion.62
  183.2 3.7 all-to-all-start
  186.9 49.0 %all-to-all-done = bf16[128,3,16,128]{3,0,1,2:T(8,128)(2,1)S(1)} async-done(((bf16[128,3,16,128]{3,0,1,2:T(8,128)(2,1)}), bf16[128,3,16,128]{3,0,1,2:T(8,128)(2,1)S(1)}, u32[]{:S(2)}, u32[]{:S(2)}) %all-to-all-start) | async-done | bytes 1572896 | tf_op jit(solution)/shard_map/all_to_all | solution.py:201
  237.2 17.7 while.27
  243.7 2.3 fusion.162
  252.6 2.3 fusion.162
  255.5 21.4 all_to_all.60
  277.4 4.9 fusion.102
  284.1 132.3 %all-gather.10.cloned.1.call-done = bf16[2048,5461]{1,0:T(8,128)(2,1)} async-done(((bf16[64,5461]{1,0:T(8,128)(2,1)}), bf16[2048,5461]{1,0:T(8,128)(2,1)}) %all-gather.10.cloned.1.call-update) | async-done | bytes 22368272 | tf_op jit(solution)/shard_map/all_gather | solution.py:208
  416.4 13.6 convolution_add_fusion.1
  430.0 129.3 %all-gather.12.cloned.1.call-done = bf16[2048,5461]{1,0:T(8,128)(2,1)} async-done(((bf16[64,5461]{1,0:T(8,128)(2,1)}), bf16[2048,5461]{1,0:T(8,128)(2,1)}) %all-gather.12.cloned.1.call-update) | async-done | bytes 22368272 | tf_op jit(solution)/shard_map/all_gather | solution.py:209
  559.4 13.7 convolution_add_fusion
  573.0 129.3 %all-gather.14.cloned.1.call-done = bf16[2048,5461]{1,0:T(8,128)(2,1)} async-done(((bf16[64,5461]{1,0:T(8,128)(2,1)}), bf16[2048,5461]{1,0:T(8,128)(2,1)}) %all-gather.14.cloned.1.call-update) | async-done | bytes 22368272 | tf_op jit(solution)/shard_map/all_gather | solution.py:210
  702.3 19.2 convert_reduce_fusion.1
  721.5 17.4 fusion.105
  738.9 17.6 fusion.106
  756.5 17.2 convolution_bitcast_fusion
  773.8 303.4 %concatenate.49 = f32[2048,16383]{0,1:T(8,128)} concatenate(f32[2048,5461]{0,1:T(8,128)} %fusion.105, f32[2048,5461]{0,1:T(8,128)} %fusion.106, f32[2048,5461]{0,1:T(8,128)} %convolution_bitcast_fusion), dimensions={1} | concatenate | bytes 268419072 | tf_op jit(solution)/shard_map/concatenate | solution.py:230
  1077.2 12.8 fusion.103
  1090.1 13.2 multiply_reduce_fusion.1
  1105.6 6.6 fusion.67
  1113.2 3.7 all-to-all-start.2
  1116.9 2.3 slice_bitcast_fusion.4
  1119.1 18.3 all-to-all-done.2
  1138.3 35.5 while.28
  1143.4 3.3 multiply_reduce_fusion.5
  1150.7 3.5 fusion.175
  1160.7 3.3 multiply_reduce_fusion.5
  1165.4 2.9 fusion.174
  1168.4 3.8 fusion.175
  1177.1 2.8 copy.172
  1179.8 4.5 all-to-all-start.3
  1184.6 8.7 fusion.104
  1193.3 45.8 %all-to-all-done.3 = bf16[1024,3,2,128]{3,2,1,0:T(2,128)(2,1)S(1)} async-done(((bf16[1024,3,2,128]{3,2,1,0:T(2,128)(2,1)}), bf16[1024,3,2,128]{3,2,1,0:T(2,128)(2,1)S(1)}, u32[]{:S(2)}, u32[]{:S(2)}) %all-to-all-start.3) | async-done | bytes 1572896 | tf_op jit(solution)/shard_map/all_to_all | solution.py:249
  1242.9 2.3 convert_reduce_fusion
  1247.1 20.4 fusion.90
  1267.6 45.9 %pad_maximum_fusion = f32[2048,8192]{1,0:T(8,128)} fusion(f32[2048,2048]{1,0:T(8,128)} %fusion.104, f32[2048,6144]{1,0:T(8,128)} %fusion.90), kind=kLoop, calls=%fused_computation.64 | loop fusion | flops 16777216 | bytes 134217728 | tf_op jit(solution)/shard_map/concatenate | solution.py:266
  1314.8 14.0 fusion.61
  1328.8 14.0 fusion.94
  1343.9 3.4 convert_reduce_fusion.4
  1347.3 1649.9 %all-reduce.9.cloned.1.call-done = f32[2048,16383]{0,1:T(8,128)} async-done(((f32[2048,16383]{0,1:T(8,128)}), f32[2048,16383]{0,1:T(8,128)}) %all-reduce.9.cloned.1.call-update) | async-done | bytes 134209552
  2997.2 8.3 fusion.98
  3005.5 3.1 copy.177
  3008.6 3.1 copy.178
  3013.8 1387.6 %reduce-scatter.3.cloned.1.call-done = f32[64,8192]{1,0:T(8,128)} async-done(((f32[2048,8192]{1,0:T(8,128)}), f32[64,8192]{1,0:T(8,128)}) %reduce-scatter.3.cloned.1.call-update) | async-done | bytes 2097168 | tf_op jit(solution)/shard_map/reduce_scatter | solution.py:265
  4401.4 2.7 slice.98
  4405.9 129.6 %all-reduce.11.cloned.1.call-done = (f32[2048]{0:T(1024)}, f32[2048]{0:T(1024)}, f32[6144]{0:T(1024)}, f32[2048]{0:T(1024)}, f32[2048]{0:T(1024)}, /*index=5*/f3...) async-done(((f32[2048]{0:T(1024)}, f32[2048]{0:T(1024)}, f32[6144]{0:T(1024)}, f32[2048]{0:T(1024)}, f32[2048]{0:T(1024)}, /*index=5*/f32[2048]{0:T(1024)}, ...) | async-done | bytes 117432 | tf_op jit(solution)/shard_map/psum | solution.py:284
  (252 shorter events, 73.3 us)
Async XLA Ops:
  7.2 4.3 copy-start.5
  7.2 161.2 %copy-start.41 = (f32[6144]{0:T(1024)S(1)}, f32[6144]{0:T(1024)}, u32[]{:S(2)}) copy-start(f32[6144]{0:T(1024)} %param.26) | copy-start | bytes 73732
  7.2 161.2 %copy-start.29 = (f32[2048]{0:T(1024)S(1)}, f32[2048]{0:T(1024)}, u32[]{:S(2)}) copy-start(f32[2048]{0:T(1024)} %param.24) | copy-start | bytes 24580
  7.2 161.2 %copy-start.23 = (f32[2048]{0:T(1024)S(1)}, f32[2048]{0:T(1024)}, u32[]{:S(2)}) copy-start(f32[2048]{0:T(1024)} %param.23) | copy-start | bytes 24580
  7.2 161.1 %all-gather.6.cloned.1.call-start = ((), (), s32[]{:S(2)}) async-start(), calls=%async_computation.5 | async-start | bytes 25952256 | tf_op jit(solution)/shard_map/all_gather | solution.py:191
  8.0 269.3 %all-gather.8.cloned.1.call-start = ((), (), s32[]{:S(2)}) async-start(), calls=%async_computation.6 | async-start | bytes 8650752 | tf_op jit(solution)/shard_map/all_gather | solution.py:192
  8.7 407.7 %all-gather.10.cloned.1.call-start = ((), (), s32[]{:S(2)}) async-start(), calls=%async_computation.7 | async-start | bytes 23248896 | tf_op jit(solution)/shard_map/all_gather | solution.py:208
  9.5 549.9 %all-gather.12.cloned.1.call-start = ((), (), s32[]{:S(2)}) async-start(), calls=%async_computation.8 | async-start | bytes 23248896 | tf_op jit(solution)/shard_map/all_gather | solution.py:209
  10.0 692.3 %all-gather.14.cloned.1.call-start = ((), (), s32[]{:S(2)}) async-start(), calls=%async_computation.9 | async-start | bytes 23248896 | tf_op jit(solution)/shard_map/all_gather | solution.py:210
  11.5 169.4 %copy-start.19 = (f32[128,128]{1,0:T(8,128)}, f32[128,128]{1,0:T(8,128)S(1)}, u32[]{:S(2)}) copy-start(f32[128,128]{1,0:T(8,128)S(1)} %get-tuple-element.381) | copy-start | bytes 196612
  11.5 169.4 %copy-start.21 = (f32[128,128]{1,0:T(8,128)}, f32[128,128]{1,0:T(8,128)S(1)}, u32[]{:S(2)}) copy-start(f32[128,128]{1,0:T(8,128)S(1)} %get-tuple-element.382) | copy-start | bytes 196612
  11.7 166.8 %copy-start.37 = (f32[128]{0:T(128)}, f32[128]{0:T(128)S(1)}, u32[]{:S(2)}) copy-start(f32[128]{0:T(128)S(1)} %broadcast_multiply_fusion.1) | copy-start | bytes 1540
  12.0 166.6 %copy-start.57 = (f32[128]{0:T(128)}, f32[128]{0:T(128)S(1)}, u32[]{:S(2)}) copy-start(f32[128]{0:T(128)S(1)} %fusion.73) | copy-start | bytes 1540
  12.0 166.6 %copy-start.39 = (f32[128]{0:T(128)}, f32[128]{0:T(128)S(1)}, u32[]{:S(2)}) copy-start(f32[128]{0:T(128)S(1)} %fusion.87) | copy-start | bytes 1540
  183.2 52.8 %all-to-all-start = ((bf16[128,3,16,128]{3,0,1,2:T(8,128)(2,1)}), bf16[128,3,16,128]{3,0,1,2:T(8,128)(2,1)S(1)}, u32[]{:S(2)}, u32[]{:S(2)}) async-start(bf16[128,3,16,128]{3,0,1,2:T(8,128)(2,1)} %pad_maximum_fusion.1), calls=%async_computation | async-start | bytes 3145728 | tf_op jit(solution)/shard_map/all_to_all | solution.py:201
  186.9 2810.3 %all-reduce.9.cloned.1.call-start = ((), (), s32[]{:S(2)}) async-start(), calls=%async_computation.11 | async-start | bytes 268435456
  254.9 27.4 copy-start.17
  254.9 27.4 copy-start.31
  255.0 27.3 copy-start.35
  255.0 22.4 copy-start.44
  277.3 5.0 copy-start.11
  277.3 6.5 copy-start.33
  277.3 6.5 copy-start.45
  277.4 139.0 %copy-start.42 = (f32[5461]{0:T(1024)S(1)}, f32[5461]{0:T(1024)}, u32[]{:S(2)}) copy-start(f32[5461]{0:T(1024)} %param.32) | copy-start | bytes 65536
  284.1 275.3 %copy-start.43 = (f32[5461]{0:T(1024)S(1)}, f32[5461]{0:T(1024)}, u32[]{:S(2)}) copy-start(f32[5461]{0:T(1024)} %param.34) | copy-start | bytes 65536
  721.5 35.0 copy-start.7
  721.5 17.4 copy-start.8
  738.9 17.6 copy-start.13
  1077.2 12.9 copy-start.3
  1077.2 12.9 copy-start.9
  1077.2 12.9 copy-start.34
  1077.2 12.9 copy-start.48
  1077.2 12.9 copy-start.50
  1090.1 13.2 copy-start.54
  1105.6 6.6 copy-start.15
  1112.2 26.1 copy-start.18
  1112.2 26.1 copy-start.32
  1112.2 26.0 copy-start.36
  1113.2 24.3 all-to-all-start.2
  1177.0 7.5 copy-start.12
  1177.1 7.5 copy-start.16
  1179.8 59.3 %all-to-all-start.3 = ((bf16[1024,3,2,128]{3,2,1,0:T(2,128)(2,1)}), bf16[1024,3,2,128]{3,2,1,0:T(2,128)(2,1)S(1)}, u32[]{:S(2)}, u32[]{:S(2)}) async-start(bf16[1024,3,2,128]{3,2,1,0:T(2,128)(2,1)} %copy.172), calls=%async_computation.3 | async-start | bytes 3145728 | tf_op jit(solution)/shard_map/all_to_all | solution.py:249
  1184.3 3217.1 %reduce-scatter.3.cloned.1.call-start = ((), (), s32[]{:S(2)}) async-start(), calls=%async_computation.10 | async-start | bytes 69206016 | tf_op jit(solution)/shard_map/reduce_scatter | solution.py:265
  1242.8 4.3 copy-start.6
  1242.9 4.3 copy-start.24
  1313.6 3222.0 %all-reduce.11.cloned.1.call-start = ((), (), s32[]{:S(2)}) async-start(), calls=%async_computation.12 | async-start | bytes 245760 | tf_op jit(solution)/shard_map/psum | solution.py:284
  1328.8 14.0 copy-start.58
  1328.8 15.1 copy-start.52
  (27 other events, 64.8 us)
Sparse Core Ops, SparseCore 0:
  11.0 157.3 all-gather.5
  171.4 98.9 all-gather.7
  273.2 143.1 all-gather.9
  419.1 140.2 all-gather.11
  562.1 140.2 all-gather.13
  1077.3 1919.8 all-reduce.8
  2999.5 1401.8 reduce-scatter.2
  4409.0 126.5 all-reduce.10
where the time goes:
time: 4570 us; the launch traced here: 4550 us
  waiting for transfers between devices  3830 us (84%)
  local copies, waits for them, and re-layouts  367 us (8%)
  matrix products  236 us (5%)
  other arithmetic  69 us (2%)
    unnamed x9, waiting for transfers between devices  1650 us
    reduce_scatter x1, waiting for transfers between devices, per_device(): lax.psum_scatter(jnp.concatenate([contract_first(left_cols, grad_raw), co...  1390 us
    concatenate x1, local copies, waits for them, and re-layouts, per_device(): jnp.concatenate([contract_first(left_cols, grad_gate), contract_first(lef...  303 us
    all_gather x1, waiting for transfers between devices, per_device(): lax.all_gather(w_qkv, ('batch', 'seq'), axis=0, tiled=True)  156 us
    all_gather x1, waiting for transfers between devices, per_device(): lax.all_gather(w_gate, ('batch', 'seq'), axis=0, tiled=True)  132 us
    psum x1, waiting for transfers between devices, per_device(): lax.psum((small_terms[0], small_terms[1], small_terms[2], small_terms[3],...  130 us
    all_gather x1, waiting for transfers between devices, per_device(): lax.all_gather(w_up, ('batch', 'seq'), axis=0, tiled=True)  129 us
    all_gather x1, waiting for transfers between devices, per_device(): lax.all_gather(w_down, ('batch', 'seq'), axis=0, tiled=True)  129 us
  transfers between devices with their start and end apart: 11, of which 10 were waited for; matrix products, arithmetic and copies ran while one was open for 6% of the time, Pallas kernels for 0%

commit v1 on v0

v1 whole, which is shorter than its diff:
```python
import math

import jax
import jax.numpy as jnp
from jax import lax
from jax.sharding import PartitionSpec as P

HEADS = 16
HEAD = 128
LANES = 128

epsilon = 1e-05
masked_value = -1000000000.0
bf16 = jnp.bfloat16
f32 = jnp.float32


def norm_parts(values):
    average = jnp.mean(values, axis=-1, keepdims=True)
    centered = values - average
    spread = jnp.mean(centered * centered, axis=-1, keepdims=True)
    inverse = lax.rsqrt(spread + epsilon)
    return (centered * inverse, inverse)


def layer_norm(values, gain, bias):
    unit, _ = norm_parts(values)
    return unit * gain + bias


def layer_norm_back(unit, inverse, gain, grad):
    scaled = grad * gain
    first = jnp.mean(scaled, axis=-1, keepdims=True)
    second = jnp.mean(scaled * unit, axis=-1, keepdims=True)
    return inverse * (scaled - first - unit * second)


def gelu_tanh(values):
    return (
        0.5
        * values
        * (1.0 + jnp.tanh(0.7978845608028654 * (values + 0.044715 * values * values * values)))
    )


def geglu(gate, upper):
    return gelu_tanh(gate) * upper


def group_layout(lengths, prefixes, count):
    ends = jnp.cumsum(lengths)
    starts = ends - lengths
    places = jnp.arange(count, dtype=jnp.int32)
    member = ((places[:, None] >= starts[None, :]) & (places[:, None] < ends[None, :])).astype(
        jnp.int32
    )
    numbers = jnp.arange(lengths.shape[0], dtype=jnp.int32)
    segment = jnp.sum(member * numbers[None, :], axis=1)
    first = jnp.sum(member * starts[None, :], axis=1)
    limits = starts + jnp.minimum(prefixes, lengths)
    bound = jnp.sum(member * limits[None, :], axis=1)
    return (segment, bound, places - first)


def rotary_tables(position):
    half_size = HEAD // 2
    rates = jnp.exp(jnp.arange(half_size, dtype=f32) * (-2.0 * math.log(10000.0) / HEAD))
    angles = position.astype(f32)[:, None] * rates[None, :]
    cosine = jnp.cos(angles)
    sine = jnp.sin(angles)
    return (jnp.concatenate([cosine, cosine], axis=1), jnp.concatenate([sine, sine], axis=1))


def rotate(values, cosine, sine):
    half_size = values.shape[-1] // 2
    turned = jnp.concatenate([-values[..., half_size:], values[..., :half_size]], axis=-1)
    return values * cosine[:, None, :] + turned * sine[:, None, :]


def rotate_back(values, cosine, sine):
    half_size = values.shape[-1] // 2
    wave = values * sine[:, None, :]
    turned = jnp.concatenate([wave[..., half_size:], -wave[..., :half_size]], axis=-1)
    return values * cosine[:, None, :] + turned


def dot_nn(left, right):
    return lax.dot_general(left, right, (((1,), (0,)), ((), ())), preferred_element_type=f32)


def dot_nt(left, right):
    return lax.dot_general(left, right, (((1,), (1,)), ((), ())), preferred_element_type=f32)


def dot_tn(left, right):
    return lax.dot_general(left, right, (((0,), (0,)), ((), ())), preferred_element_type=f32)


class Ring:
    def __init__(self, count):
        self.count = count
        rows = 4 if count % 4 == 0 else count
        columns = count // rows
        if columns == 2:
            order = [2 * z for z in range(rows)] + [2 * z + 1 for z in reversed(range(rows))]
        else:
            order = list(range(count))
        self.forward = [(order[i], order[(i + 1) % count]) for i in range(count)]
        self.backward = [(b, a) for a, b in self.forward]
        me = lax.axis_index("seq")
        if columns == 2:
            z, y = me // 2, me % 2
            place = jnp.where(y == 0, z, count - 1 - z)
        else:
            place = me
        self.me = me
        self.at = []
        for k in range(count):
            spot = lax.rem(place + k, count)
            if columns == 2:
                spot = jnp.where(spot < rows, 2 * spot, 2 * (count - 1 - spot) + 1)
            self.at.append(spot)

    def ahead(self, k):
        return self.at[k % self.count]

    def send(self, values, forward):
        return lax.ppermute(values, "seq", self.forward if forward else self.backward)

    def gather(self, block, axis=0):
        count, half_way = self.count, self.count // 2
        size = block.shape[axis]
        shape = list(block.shape)
        shape[axis] = size * count
        total = jnp.zeros(shape, block.dtype)
        half = block.shape[0] // 2

        def put(total, piece, owner, shift=0):
            start = [jnp.int32(0), jnp.int32(0)]
            start[axis] = owner * size
            if shift:
                start[0] = start[0] + shift
            return lax.dynamic_update_slice(total, piece, start)

        total = put(total, block, self.me)
        ahead = behind = block
        for k in range(1, half_way):
            behind = self.send(behind, True)
            ahead = self.send(ahead, False)
            total = put(total, behind, self.ahead(-k))
            total = put(total, ahead, self.ahead(k))
        behind = self.send(behind[:half], True)
        ahead = self.send(ahead[half:], False)
        total = put(total, behind, self.ahead(-half_way))
        total = put(total, ahead, self.ahead(half_way), half)
        return total

    def scatter(self, parts):
        count, half_way = self.count, self.count // 2
        rows, width = parts.shape[0] // count, parts.shape[1]
        half = rows // 2

        def piece(owner, start=0, size=rows):
            return lax.dynamic_slice(
                parts, (owner * rows + start, jnp.int32(0)), (size, width)
            ).astype(f32)

        low, high = piece(self.ahead(half_way), 0, half), piece(self.ahead(half_way), half, half)
        low = self.send(low.astype(bf16), True).astype(f32)
        high = self.send(high.astype(bf16), False).astype(f32)
        nothing = jnp.zeros_like(low)
        forward = jnp.concatenate([low, nothing], axis=0)
        backward = jnp.concatenate([nothing, high], axis=0)
        for k in range(half_way - 1, 0, -1):
            forward = forward + piece(self.ahead(k))
            backward = backward + piece(self.ahead(-k))
            forward = self.send(forward.astype(bf16), True).astype(f32)
            backward = self.send(backward.astype(bf16), False).astype(f32)
        return forward + backward + piece(self.me)


class Mates:
    def __init__(self, count):
        self.count = count
        self.chips = count // 2
        self.me = lax.axis_index("batch")
        self.chip, self.core = self.me // 2, self.me % 2
        self.swap = [(i, i ^ 1) for i in range(count)]

    def gather(self, block):
        rows, width = block.shape
        total = jnp.zeros((self.chips, 2, rows, width), block.dtype)
        zero = jnp.int32(0)

        def put(total, piece, chip, core):
            return lax.dynamic_update_slice(
                total, piece.reshape(1, 1, rows, width), (chip, core, zero, zero)
            )

        mine = [block]
        for step in range(1, self.chips):
            shift = [(i, (i + 2 * step) % self.count) for i in range(self.count)]
            mine.append(lax.ppermute(block, "batch", shift))
        for step, piece in enumerate(mine):
            chip = lax.rem(self.chip - step + self.chips, self.chips)
            total = put(total, piece, chip, self.core)
            total = put(total, lax.ppermute(piece, "batch", self.swap), chip, 1 - self.core)
        return total.reshape(self.count * rows, width)

    def scatter(self, parts):
        rows, width = parts.shape[0] // self.count, parts.shape[1]
        view = parts.reshape(self.chips, 2, rows, width)
        other = lax.dynamic_index_in_dim(view, 1 - self.core, 1, False).astype(bf16)
        kept = lax.dynamic_index_in_dim(view, self.core, 1, False).astype(f32)
        kept = kept + lax.ppermute(other, "batch", self.swap).astype(f32)
        total = lax.dynamic_index_in_dim(kept, self.chip, 0, False)
        for step in range(1, self.chips):
            shift = [(i, (i + 2 * step) % self.count) for i in range(self.count)]
            to = lax.rem(self.chip + step, self.chips)
            sent = lax.dynamic_index_in_dim(kept, to, 0, False).astype(bf16)
            total = total + lax.ppermute(sent, "batch", shift).astype(f32)
        return total


def sum_everywhere(values, batch_count, seq_count):
    for axis, count in (("batch", batch_count), ("seq", seq_count)):
        if count & (count - 1):
            values = lax.psum(values, axis)
            continue
        step = 1
        while step < count:
            values = values + lax.ppermute(values, axis, [(i, i ^ step) for i in range(count)])
            step *= 2
    return values


def allowed_keys(segment, bound):
    places = jnp.arange(segment.shape[0], dtype=jnp.int32)
    same = segment[:, None] == segment[None, :]
    return same & (
        (places[None, :] <= places[:, None]) | (places[None, :] < bound[:, None])
    )


def attend_forward(queries, keys, values, allowed):
    scores = jnp.einsum("qhe,khe->hqk", queries, keys, preferred_element_type=f32) * HEAD ** (-0.5)
    scores = jnp.where(allowed[None], scores, masked_value)
    largest = jnp.max(scores, axis=-1, keepdims=True)
    powers = jnp.exp(scores - largest)
    totals = jnp.sum(powers, axis=-1, keepdims=True)
    probs = (powers / totals).astype(bf16)
    result = jnp.einsum("hqk,khe->qhe", probs, values, preferred_element_type=f32)
    return (result.astype(bf16), largest + jnp.log(totals))


def attend_backward(queries, keys, values, grads, log_sums, allowed):
    scale = HEAD ** (-0.5)
    scores = jnp.einsum("qhe,khe->hqk", queries, keys, preferred_element_type=f32) * scale
    scores = jnp.where(allowed[None], scores, masked_value)
    probs = jnp.exp(scores - log_sums)
    low_probs = probs.astype(bf16)
    grad_probs = jnp.einsum("qhe,khe->hqk", grads, values, preferred_element_type=f32)
    delta = jnp.sum(probs * grad_probs, axis=-1, keepdims=True)
    grad_scores = (probs * (grad_probs - delta)).astype(bf16)
    query_grad = jnp.einsum("hqk,khe->qhe", grad_scores, keys, preferred_element_type=f32) * scale
    key_grad = jnp.einsum("hqk,qhe->khe", grad_scores, queries, preferred_element_type=f32) * scale
    value_grad = jnp.einsum("hqk,qhe->khe", low_probs, grads, preferred_element_type=f32)
    return (query_grad.astype(bf16), key_grad.astype(bf16), value_grad.astype(bf16))


def tile_split(width, count):
    tiles = -(-width // LANES)
    least, extra = divmod(tiles, count)
    sizes = [least + (1 if i < extra else 0) for i in range(count)]
    starts = [sum(sizes[:i]) for i in range(count)]
    return (starts, sizes, max(sizes))


def per_device(
    tokens,
    ln1_gain,
    ln1_bias,
    w_qkv,
    b_qkv,
    w_out,
    b_out,
    ln2_gain,
    ln2_bias,
    w_gate,
    b_gate,
    w_up,
    b_up,
    w_down,
    b_down,
    protein_lengths,
    prefix_lengths,
    out_grad,
):
    seq_count = lax.axis_size("seq")
    batch_count = lax.axis_size("batch")
    own_rows, width = tokens.shape
    weight_rows = w_qkv.shape[0]
    ffn_width = w_gate.shape[1]
    count = own_rows * seq_count
    own_heads = HEADS // seq_count
    own_width = own_heads * HEAD
    ring = Ring(seq_count)
    mates = Mates(batch_count)
    me = ring.me
    zero = jnp.int32(0)

    segment, bound, position = group_layout(protein_lengths[0], prefix_lengths[0], count)
    cosine, sine = rotary_tables(position)
    allowed = allowed_keys(segment, bound)

    def to_columns(blocks):
        moved = lax.all_to_all(blocks, "seq", split_axis=0, concat_axis=0, tiled=True)
        return moved.reshape(seq_count * weight_rows, blocks.shape[2])

    def to_rows(columns):
        blocks = columns.reshape(seq_count, weight_rows, columns.shape[1])
        return lax.all_to_all(blocks, "seq", split_axis=0, concat_axis=0, tiled=True)

    qkv_blocks = (
        w_qkv.reshape(weight_rows, 3, seq_count, own_width)
        .transpose(2, 0, 1, 3)
        .reshape(seq_count, weight_rows, 3 * own_width)
    )
    qkv_own = mates.gather(to_columns(qkv_blocks))
    tokens_all = ring.gather(tokens)
    out_all = mates.gather(ring.gather(w_out))

    starts, sizes, most = tile_split(ffn_width, seq_count)
    own_ffn = most * LANES
    padded = (starts[-1] + most) * LANES

    def ffn_blocks(weight, mask):
        whole = jnp.pad(weight, ((0, 0), (0, padded - ffn_width)))
        pieces = []
        for start, size in zip(starts, sizes):
            piece = whole[:, start * LANES : (start + most) * LANES]
            if mask and size < most:
                piece = jnp.pad(piece[:, : size * LANES], ((0, 0), (0, (most - size) * LANES)))
            pieces.append(piece)
        return jnp.stack(pieces)

    ffn_sent = jnp.concatenate(
        [ffn_blocks(w_gate, False), ffn_blocks(w_up, False), ffn_blocks(w_down, True)], axis=2
    )
    ffn_own = mates.gather(to_columns(ffn_sent))
    gate_up_own = ffn_own[:, : 2 * own_ffn]
    down_own = ffn_own[:, 2 * own_ffn :]
    first_tile = jnp.asarray(starts, jnp.int32)[me] * LANES

    def ffn_bias(bias):
        return lax.dynamic_slice(jnp.pad(bias, (0, padded - ffn_width)), (first_tile,), (own_ffn,))

    inputs = tokens_all.astype(f32)
    normed = layer_norm(inputs, ln1_gain, ln1_bias).astype(bf16)
    qkv_bias = lax.dynamic_slice(
        b_qkv.reshape(3, width), (zero, me * own_width), (3, own_width)
    ).reshape(3 * own_width)
    raw = (dot_nn(normed, qkv_own) + qkv_bias).reshape(count, 3, own_heads, HEAD)
    queries = rotate(raw[:, 0], cosine, sine).astype(bf16)
    keys = rotate(raw[:, 1], cosine, sine).astype(bf16)
    values = raw[:, 2].astype(bf16)
    head_result, log_sums = attend_forward(queries, keys, values, allowed)
    attended = ring.gather(head_result.reshape(count, own_width), axis=1)
    hidden_in = inputs + dot_nn(attended, out_all) + b_out
    hidden_own = lax.dynamic_slice(hidden_in, (me * own_rows, zero), (own_rows, width))

    normed_two = layer_norm(hidden_in, ln2_gain, ln2_bias).astype(bf16)
    gate_up = dot_nn(normed_two, gate_up_own)
    gate = gate_up[:, :own_ffn] + ffn_bias(b_gate)
    upper = gate_up[:, own_ffn:] + ffn_bias(b_up)
    act = geglu(gate, upper).astype(bf16)
    grad_out_all = ring.gather(out_grad)
    grad_act = dot_nn(grad_out_all, down_own)
    _, geglu_pull = jax.vjp(geglu, gate, upper)
    grad_gate, grad_up = geglu_pull(grad_act)
    grad_gate_up = jnp.concatenate([grad_gate.astype(bf16), grad_up.astype(bf16)], axis=1)
    grad_normed_two = ring.scatter(dot_nt(grad_gate_up, gate_up_own).astype(bf16))

    unit_two, inverse_two = norm_parts(hidden_own)
    cotangent = out_grad.astype(f32)
    grad_hidden = cotangent + layer_norm_back(unit_two, inverse_two, ln2_gain, grad_normed_two)
    gain_two_grad = jnp.sum(grad_normed_two * unit_two, axis=0)
    bias_two_grad = jnp.sum(grad_normed_two, axis=0)
    grad_attn = grad_hidden.astype(bf16)
    grad_attn_all = ring.gather(grad_attn)

    out_heads = lax.dynamic_slice(out_all, (me * own_width, zero), (own_width, width))
    grad_attended = dot_nt(grad_attn_all, out_heads).astype(bf16).reshape(count, own_heads, HEAD)
    grad_queries, grad_keys, grad_values = attend_backward(
        queries, keys, values, grad_attended, log_sums, allowed
    )
    grad_raw = jnp.stack(
        [
            rotate_back(grad_queries.astype(f32), cosine, sine).astype(bf16),
            rotate_back(grad_keys.astype(f32), cosine, sine).astype(bf16),
            grad_values,
        ],
        axis=1,
    ).reshape(count, 3 * own_width)
    grad_normed = ring.scatter(dot_nt(grad_raw, qkv_own).astype(bf16))
    unit_one, inverse_one = norm_parts(tokens.astype(f32))
    tokens_grad = (
        grad_hidden + layer_norm_back(unit_one, inverse_one, ln1_gain, grad_normed)
    ).astype(bf16)
    gain_one_grad = jnp.sum(grad_normed * unit_one, axis=0)
    bias_one_grad = jnp.sum(grad_normed, axis=0)

    ffn = ring.scatter(dot_nt(act, down_own).astype(bf16))
    output = (hidden_own + ffn + b_down).astype(bf16)

    ffn_share = mates.scatter(
        jnp.concatenate(
            [
                dot_tn(normed_two, grad_gate_up).astype(bf16),
                dot_tn(grad_out_all, act).astype(bf16),
            ],
            axis=1,
        )
    )
    ffn_rows = to_rows(ffn_share.astype(bf16))

    def ffn_grad(which):
        pieces = [
            ffn_rows[i, :, which * own_ffn : which * own_ffn + sizes[i] * LANES]
            for i in range(seq_count)
        ]
        return jnp.concatenate(pieces, axis=1)[:, :ffn_width].astype(f32)

    out_rows = jnp.concatenate(
        [
            lax.dynamic_slice(
                attended, (zero, (i * seq_count + me) * weight_rows), (count, weight_rows)
            )
            for i in range(batch_count)
        ],
        axis=1,
    )
    out_weight_grad = mates.scatter(dot_tn(out_rows, grad_attn_all).astype(bf16))
    qkv_share = mates.scatter(dot_tn(normed, grad_raw).astype(bf16))
    qkv_rows = to_rows(qkv_share.astype(bf16))
    qkv_weight_grad = (
        qkv_rows.reshape(seq_count, weight_rows, 3, own_width)
        .transpose(1, 2, 0, 3)
        .reshape(weight_rows, 3 * width)
        .astype(f32)
    )

    def spread(values, start, size):
        return lax.dynamic_update_slice(jnp.zeros((size,), f32), values, (start,))

    bias_gate_up = jnp.sum(grad_gate_up.astype(f32), axis=0)
    early = jnp.concatenate(
        [
            jnp.sum(cotangent, axis=0),
            jnp.sum(grad_attn.astype(f32), axis=0),
            gain_two_grad,
            bias_two_grad,
            spread(bias_gate_up[:own_ffn], first_tile, padded),
            spread(bias_gate_up[own_ffn:], first_tile, padded),
        ]
    )
    early = sum_everywhere(early, batch_count, seq_count)
    grad_bias_qkv = jnp.sum(grad_raw.astype(f32), axis=0)
    late = jnp.concatenate(
        [gain_one_grad, bias_one_grad]
        + [
            spread(grad_bias_qkv[i * own_width : (i + 1) * own_width], me * own_width, width)
            for i in range(3)
        ]
    )
    late = sum_everywhere(late, batch_count, seq_count)
    b_down_grad, b_out_grad, gain_two, bias_two = (
        early[i * width : (i + 1) * width] for i in range(4)
    )
    b_gate_grad = early[4 * width : 4 * width + ffn_width]
    b_up_grad = early[4 * width + padded : 4 * width + padded + ffn_width]
    return (
        output,
        tokens_grad,
        late[:width],
        late[width : 2 * width],
        qkv_weight_grad,
        late[2 * width :],
        out_weight_grad,
        b_out_grad,
        gain_two,
        bias_two,
        ffn_grad(0),
        b_gate_grad,
        ffn_grad(1),
        b_up_grad,
        ffn_grad(2),
        b_down_grad,
    )


def solution(mesh):
    rows = P(("batch", "seq"), None)
    in_specs = (
        rows, P(), P(), rows, P(), rows, P(), P(), P(), rows, P(), rows, P(), rows, P(),
        P("batch", None), P("batch", None), rows,
    )
    out_specs = (
        rows, rows, P(), P(), rows, P(), rows, P(), P(), P(), rows, P(), rows, P(), rows, P(),
    )
    return jax.shard_map(
        per_device, mesh=mesh, in_specs=in_specs, out_specs=out_specs, check_vma=False
    )
```

time: 4570 us -> 857 us (0.19)
  waiting for transfers between devices: 3830 us -> 301 us
  matrix products: 236 us -> 95.4 us
  local copies, waits for them, and re-layouts: 367 us -> 227 us
  starting transfers between devices: 12.6 us -> 152 us
    unnamed x9 -> x0, waiting for transfers between devices: 1650 us -> none
    reduce_scatter x1 -> x0, waiting for transfers between devices: 1390 us -> none  [per_device(): lax.psum_scatter(jnp.concatenate([contract_first(left_cols, grad_raw), co...]
    all_gather x5 -> x0, waiting for transfers between devices: 547 us -> none  [the longest x1 156 us: per_device(): lax.all_gather(w_qkv, ('batch', 'seq'), axis=0, tiled=True)]
    concatenate x1 -> x3, local copies, waits for them, and re-layouts: 303 us -> 1.01 us  [the longest x1 1 us: ffn_grad(): return jnp.concatenate(pieces, axis=1)[:, :ffn_width].astype(f32)]
    ppermute x0 -> x89, waiting for transfers between devices: none -> 289 us  [the longest x64 204 us: send(): lax.ppermute(values, 'seq', self.forward if forward else self.backward)]
    dot_general x29 -> x18, matrix products: 236 us -> 95.4 us  [the longest x4 40.4 us: dot_nn(): lax.dot_general(left, right, (((1,), (0,)), ((), ())), preferred_element_...]
    ppermute x0 -> x89, starting transfers between devices: none -> 133 us  [the longest x64 97.6 us: send(): lax.ppermute(values, 'seq', self.forward if forward else self.backward)]
    psum x1 -> x0, waiting for transfers between devices: 130 us -> none  [per_device(): lax.psum((small_terms[0], small_terms[1], small_terms[2], small_terms[3],...]
  transfers between devices with their start and end apart: 11 -> 93, of which waited for: 10 -> 44; matrix products, arithmetic and copies ran while one was open for 6% -> 40% of each run, Pallas kernels for 0% -> 0%
where the time goes in v1:
time: 857 us; the launch traced here: 846 us
  waiting for transfers between devices  301 us (35%)
  local copies, waits for them, and re-layouts  227 us (26%)
  starting transfers between devices  152 us (18%)
  matrix products  95.4 us (11%)
  other arithmetic  66.8 us (8%)
    ppermute x64, waiting for transfers between devices, send(): lax.ppermute(values, 'seq', self.forward if forward else self.backward)  204 us
    ppermute x64, starting transfers between devices, send(): lax.ppermute(values, 'seq', self.forward if forward else self.backward)  97.6 us
    unnamed x163, local copies, waits for them, and re-layouts  76.6 us
    ppermute x3, waiting for transfers between devices, scatter(): total = total + lax.ppermute(sent, 'batch', shift).astype(f32)  55.6 us
    dynamic_update_slice x45, local copies, waits for them, and re-layouts, put(): return lax.dynamic_update_slice(total, piece, start)  45.5 us
    dot_general x4, matrix products, dot_nn(): lax.dot_general(left, right, (((1,), (0,)), ((), ())), preferred_element_...  40.4 us
    ppermute x10, starting transfers between devices, sum_everywhere(): lax.ppermute(values, axis, [(i, i ^ step) for i in range(count)])  28.3 us
    dot_general x4, matrix products, dot_tn(): lax.dot_general(left, right, (((0,), (0,)), ((), ())), preferred_element_...  22.5 us
  transfers between devices with their start and end apart: 93, of which 44 were waited for; matrix products, arithmetic and copies ran while one was open for 40% of the time, Pallas kernels for 0%

profile of v1, /device:TPU:0, one launch (start us, length us, event | category | flops | bytes accessed | tf_op | source)
XLA Modules:
  0.0 845.8 jit_solution(2769751235960765886)
XLA Ops:
  9.3 6.3 all-to-all-start
  68.9 8.6 %collective-permute-done.22 = bf16[64,2048]{1,0:T(8,128)(2,1)S(1)} collective-permute-done((bf16[64,2048]{1,0:T(8,128)(2,1)}, bf16[64,2048]{1,0:T(8,128)(2,1)S(1)}, u32[]{:S(2)}, u32[]{:S(2)}) %collective-permute-start.22) | collective-permute-done | bytes 262176 | tf_op jit(solution)/shard_map/ppermute | solution.py:128
  86.9 7.5 collective-permute-done.24
  100.1 5.2 collective-permute-done.26
  106.0 4.4 broadcast_in_dim.23
  136.3 7.3 collective-permute-done.45
  145.5 5.6 collective-permute-start.6
  154.0 17.9 %collective-permute-done.46 = bf16[128,2048]{1,0:T(8,128)(2,1)S(1)} collective-permute-done((bf16[128,2048]{1,0:T(8,128)(2,1)S(1)}, bf16[128,2048]{1,0:T(8,128)(2,1)S(1)}, u32[]{:S(2)}, u32[]{:S(2)}) %collective-permute-start.46) | collective-permute-done | bytes 524320 | tf_op jit(solution)/shard_map/ppermute | solution.py:128
  172.0 10.1 %collective-permute-start.7 = (bf16[64,2048]{1,0:T(8,128)(2,1)S(1)}, bf16[64,2048]{1,0:T(8,128)(2,1)S(1)}, u32[]{:S(2)}, u32[]{:S(2)}) collective-permute-start(bf16[64,2048]{1,0:T(8,128)(2,1)S(1)} %slice.405), channel_id=1, source_target_pairs={{2,0},{4,2},{6,4},{7,6},{5,7},{3,5},{1,3},{0,1},{10,8},{12,10},{14... | collective-permute-start | bytes 786440 | tf_op jit(solution)/shard_map/ppermute | solution.py:128
  186.3 16.8 %collective-permute-done.7 = bf16[64,2048]{1,0:T(8,128)(2,1)S(1)} collective-permute-done((bf16[64,2048]{1,0:T(8,128)(2,1)S(1)}, bf16[64,2048]{1,0:T(8,128)(2,1)S(1)}, u32[]{:S(2)}, u32[]{:S(2)}) %collective-permute-start.7) | collective-permute-done | bytes 262176 | tf_op jit(solution)/shard_map/ppermute | solution.py:128
  212.4 4.6 collective-permute-start.48
  218.1 7.1 convolution_add_fusion
  243.3 6.6 collective-permute-done.11
  255.3 8.3 collective-permute-done.13
  277.8 4.3 broadcast_in_dim.25
  287.0 4.0 collective-permute-done.18
  297.5 13.4 %fusion.100 = (f32[1024]{0:T(1024)S(1)}, f32[1024,2048]{1,0:T(8,128)S(1)}) fusion(f32[2048]{0:T(1024)S(1)} %copy-done.51, bf16[1024,2048]{1,0:T(8,128)(2,1)} %constant_dynamic-update-slice_fusion.105, bf16[2048,2048]{1,0:T(8,128)(2,1)} %bitcast.23, bf16[1024,2048]{1,0:T(8,128)(2,1)} %constant_dynamic-update-slice_fusion.87), kind=kOutput, calls=%fused_computation.377 | convolution fusion | flops 8598322176 | bytes 25178112 | tf_op jit(solution)/shard_map/dot_general | solution.py:88
  311.3 17.0 %collective-permute-done.31 = bf16[512,2304]{1,0:T(8,128)(2,1)S(1)} collective-permute-done((bf16[512,2304]{1,0:T(8,128)(2,1)S(1)}, bf16[512,2304]{1,0:T(8,128)(2,1)S(1)}, u32[]{:S(2)}, u32[]{:S(2)}) %collective-permute-start.31) | collective-permute-done | bytes 2359328 | tf_op jit(solution)/shard_map/ppermute | solution.py:203
  334.4 9.7 %fusion.11 = f32[1024,1536]{1,0:T(8,128)S(1)} fusion(bf16[2048,2304]{1,0:T(8,128)(2,1)} %bitcast.53, f32[1024,2048]{1,0:T(8,128)S(1)} %get-tuple-element.129, f32[2048]{0:T(1024)S(1)} %copy-done.52, f32[2048]{0:T(1024)S(1)} %copy-done.35, f32[1024]{0:T(1024)S(1)} %add_rsqrt_fusion, f32[1024]{0:T(1024)S(1)} %broadcast_multiply_fusion.2), kind=kOutput, calls=%fused_computation.26 | convolution fusion | flops 6452936704 | bytes 20996096 | tf_op jit(solution)/shard_map/dot_general | solution.py:88
  344.0 10.2 %fusion.26 = (bf16[1024,768]{1,0:T(8,128)(2,1)S(1)}, bf16[1024,768]{1,0:T(8,128)(2,1)S(1)}, bf16[1024,768]{1,0:T(8,128)(2,1)S(1)}) fusion(f32[1024,1536]{1,0:T(8,128)S(1)} %fusion.11, f32[768]{0:T(1024)S(1)} %get-tuple-element.139, f32[768]{0:T(1024)S(1)} %get-tuple-element.140, bf16[1024,2048]{1,0:T(8,128)(2,1)} %constant_dynamic-update-slice_fusion.59, ...), kind=kOutput, calls=%fused_computation.50 | convolution fusion | flops 3246391296 | bytes 18356224 | tf_op jit(solution)/shard_map/dot_general | solution.py:88
  354.3 9.4 %fusion.20 = bf16[1024,2048]{1,0:T(8,128)(2,1)S(1)} fusion(bf16[2048,2304]{1,0:T(8,128)(2,1)} %bitcast.53, bf16[1024,768]{1,0:T(8,128)(2,1)S(1)} %get-tuple-element.35, bf16[1024,768]{1,0:T(8,128)(2,1)S(1)} %get-tuple-element.34), kind=kOutput, calls=%fused_computation.42 | convolution fusion | flops 6450839552 | bytes 13631488 | tf_op jit(solution)/shard_map/dot_general | solution.py:92
  365.8 5.6 convolution_convert_fusion.2
  376.3 4.4 collective-permute-done.33
  384.6 7.3 collective-permute-done.50
  396.2 7.0 collective-permute-done.34
  407.3 7.1 collective-permute-done.51
  418.6 7.0 collective-permute-done.35
  429.8 8.8 %collective-permute-done.56 = bf16[128,2048]{1,0:T(8,128)(2,1)S(1)} collective-permute-done((bf16[128,2048]{1,0:T(8,128)(2,1)S(1)}, bf16[128,2048]{1,0:T(8,128)(2,1)S(1)}, u32[]{:S(2)}, u32[]{:S(2)}) %collective-permute-start.56) | collective-permute-done | bytes 524320 | tf_op jit(solution)/shard_map/ppermute | solution.py:128
  439.2 8.9 %collective-permute-done.40 = bf16[128,2048]{1,0:T(8,128)(2,1)S(1)} collective-permute-done((bf16[128,2048]{1,0:T(8,128)(2,1)S(1)}, bf16[128,2048]{1,0:T(8,128)(2,1)S(1)}, u32[]{:S(2)}, u32[]{:S(2)}) %collective-permute-start.40) | collective-permute-done | bytes 524320 | tf_op jit(solution)/shard_map/ppermute | solution.py:128
  451.3 8.1 convolution_convert_fusion
  460.0 6.1 convolution_convert_fusion.3
  466.6 11.5 %pad_maximum_fusion = bf16[2048,2304]{0,1:T(8,128)(2,1)} fusion(bf16[2048,768]{0,1:T(8,128)(2,1)S(1)} %convolution_convert_fusion.3, bf16[2048,1536]{0,1:T(8,128)(2,1)S(1)} %convolution_convert_fusion), kind=kLoop, calls=%fused_computation.5 | loop fusion | flops 18874368 | bytes 18874368 | tf_op jit(solution)/shard_map/concatenate | solution.py:417
  478.1 16.1 %reshape.330 = bf16[2,2,512,2304]{2,1,0,3:T(2,128)(2,1)} reshape(bf16[2048,2304]{0,1:T(8,128)(2,1)} %pad_maximum_fusion) | data formatting | bytes 18874368 | tf_op jit(solution)/shard_map/reshape | solution.py:212
  497.7 22.4 %constant_dynamic-slice_fusion.1 = (bf16[2,1,512,2304]{2,1,0,3:T(2,128)(2,1)}, bf16[2,1,512,2304]{2,1,0,3:T(2,128)(2,1)}) fusion(bf16[2,2,512,2304]{2,1,0,3:T(2,128)(2,1)} %reshape.330, s32[]{:T(128)S(6)} %select_n.272, s32[]{:T(128)S(6)} %select_n.273), kind=kLoop, calls=%fused_computation.271 | loop fusion | bytes 18874376 | tf_op jit(solution)/shard_map/jit(dynamic_index_in_dim)/dynamic_slice | solution.py:214
  520.1 20.9 %copy.114 = bf16[2,1,512,2304]{3,2,0,1:T(8,128)(2,1)} copy(bf16[2,1,512,2304]{2,1,0,3:T(2,128)(2,1)} %get-tuple-element.37) | data formatting | bytes 9437184
  541.1 20.9 %copy.113 = bf16[2,1,512,2304]{3,2,0,1:T(8,128)(2,1)} copy(bf16[2,1,512,2304]{2,1,0,3:T(2,128)(2,1)} %get-tuple-element.36) | data formatting | bytes 9437184
  570.3 7.1 collective-permute-done.59
  580.9 11.4 %collective-permute-done.61 = bf16[128,2048]{1,0:T(8,128)(2,1)S(1)} collective-permute-done((bf16[128,2048]{1,0:T(8,128)(2,1)S(1)}, bf16[128,2048]{1,0:T(8,128)(2,1)S(1)}, u32[]{:S(2)}, u32[]{:S(2)}) %collective-permute-start.61) | collective-permute-done | bytes 524320 | tf_op jit(solution)/shard_map/ppermute | solution.py:128
  595.4 5.8 collective-permute-done.63
  623.2 6.8 convolution_convert_fusion.4
  651.9 55.6 %collective-permute-done.79 = bf16[512,768]{1,0:T(8,128)(2,1)S(1)} collective-permute-done((bf16[512,768]{1,0:T(8,128)(2,1)S(1)}, bf16[512,768]{1,0:T(8,128)(2,1)S(1)}, u32[]{:S(2)}, u32[]{:S(2)}) %collective-permute-start.79) | collective-permute-done | bytes 786464 | tf_op jit(solution)/shard_map/ppermute | solution.py:221
  708.5 5.0 all-to-all-start.2
  718.3 4.9 fusion.13
  723.2 11.7 %all-to-all-done.2 = bf16[8,64,768]{2,1,0:T(8,128)(2,1)S(1)} async-done(((bf16[8,64,768]{2,1,0:T(8,128)(2,1)}), bf16[8,64,768]{2,1,0:T(8,128)(2,1)S(1)}, u32[]{:S(2)}, u32[]{:S(2)}) %all-to-all-start.2) | async-done | bytes 786464 | tf_op jit(solution)/shard_map/all_to_all | solution.py:322
  743.6 9.3 %collective-permute-start.68 = (bf16[128,2048]{1,0:T(8,128)(2,1)S(1)}, bf16[128,2048]{1,0:T(8,128)(2,1)S(1)}, u32[]{:S(2)}, u32[]{:S(2)}) collective-permute-start(bf16[128,2048]{1,0:T(8,128)(2,1)S(1)} %get-tuple-element.44), channel_id=1, source_target_pairs={{0,2},{2,4},{4,6},{6,7},{7,5},{5,3},{3,1},{1,0},{8,10},{10,12},{12... | collective-permute-start | bytes 1572872 | tf_op jit(solution)/shard_map/ppermute | solution.py:128
  755.7 20.8 %collective-permute-done.72 = bf16[128,2048]{1,0:T(8,128)(2,1)S(1)} collective-permute-done((bf16[128,2048]{1,0:T(8,128)(2,1)S(1)}, bf16[128,2048]{1,0:T(8,128)(2,1)S(1)}, u32[]{:S(2)}, u32[]{:S(2)}) %collective-permute-start.72) | collective-permute-done | bytes 524320 | tf_op jit(solution)/shard_map/ppermute | solution.py:128
  776.5 10.5 %collective-permute-done.68 = bf16[128,2048]{1,0:T(8,128)(2,1)S(1)} collective-permute-done((bf16[128,2048]{1,0:T(8,128)(2,1)S(1)}, bf16[128,2048]{1,0:T(8,128)(2,1)S(1)}, u32[]{:S(2)}, u32[]{:S(2)}) %collective-permute-start.68) | collective-permute-done | bytes 524320 | tf_op jit(solution)/shard_map/ppermute | solution.py:128
  798.0 19.5 %collective-permute-start.76 = (f32[10240]{0:T(1024)S(1)}, f32[10240]{0:T(1024)S(1)}, u32[]{:S(2)}, u32[]{:S(2)}) collective-permute-start(f32[10240]{0:T(1024)S(1)} %add.681), channel_id=1, source_target_pairs={{0,2},{1,3},{2,0},{3,1},{4,6},{5,7},{6,4},{7,5},{8,10},{9,11},{10,... | collective-permute-start | bytes 122888 | tf_op jit(solution)/shard_map/ppermute | solution.py:232
  (509 shorter events, 327.3 us)
Async XLA Ops:
  0.6 61.6 %collective-permute-start = (bf16[128,2048]{1,0:T(8,128)(2,1)}, bf16[128,2048]{1,0:T(8,128)(2,1)}, u32[]{:S(2)}, u32[]{:S(2)}) collective-permute-start(bf16[128,2048]{1,0:T(8,128)(2,1)} %param.19), channel_id=1, source_target_pairs={{0,2},{2,4},{4,6},{6,7},{7,5},{5,3},{3,1},{1,0},{8,10},{10,12},{12... | collective-permute-start | bytes 1572872 | tf_op jit(solution)/shard_map/ppermute | solution.py:128
  3.7 60.5 %collective-permute-start.1 = (bf16[128,2048]{1,0:T(8,128)(2,1)}, bf16[128,2048]{1,0:T(8,128)(2,1)}, u32[]{:S(2)}, u32[]{:S(2)}) collective-permute-start(bf16[128,2048]{1,0:T(8,128)(2,1)} %param.19), channel_id=1, source_target_pairs={{2,0},{4,2},{6,4},{7,6},{5,7},{3,5},{1,3},{0,1},{10,8},{12,10},{14... | collective-permute-start | bytes 1572872 | tf_op jit(solution)/shard_map/ppermute | solution.py:128
  3.7 53.1 %collective-permute-start.19 = (bf16[64,2048]{1,0:T(8,128)(2,1)}, bf16[64,2048]{1,0:T(8,128)(2,1)}, u32[]{:S(2)}, u32[]{:S(2)}) collective-permute-start(bf16[64,2048]{1,0:T(8,128)(2,1)} %param.24), channel_id=1, source_target_pairs={{0,2},{2,4},{4,6},{6,7},{7,5},{5,3},{3,1},{1,0},{8,10},{10,12},{12... | collective-permute-start | bytes 786440 | tf_op jit(solution)/shard_map/ppermute | solution.py:128
  5.8 52.9 %collective-permute-start.20 = (bf16[64,2048]{1,0:T(8,128)(2,1)}, bf16[64,2048]{1,0:T(8,128)(2,1)}, u32[]{:S(2)}, u32[]{:S(2)}) collective-permute-start(bf16[64,2048]{1,0:T(8,128)(2,1)} %param.24), channel_id=1, source_target_pairs={{2,0},{4,2},{6,4},{7,6},{5,7},{3,5},{1,3},{0,1},{10,8},{12,10},{14... | collective-permute-start | bytes 786440 | tf_op jit(solution)/shard_map/ppermute | solution.py:128
  9.3 115.8 %all-to-all-start = ((bf16[8,64,768]{2,1,0:T(8,128)(2,1)}), bf16[8,64,768]{2,1,0:T(8,128)(2,1)S(1)}, u32[]{:S(2)}, u32[]{:S(2)}) async-start(bf16[8,64,768]{2,1,0:T(8,128)(2,1)} %reshape.304), calls=%async_computation | async-start | bytes 1572864 | tf_op jit(solution)/shard_map/all_to_all | solution.py:317
  15.5 63.5 %collective-permute-start.41 = (bf16[128,2048]{1,0:T(8,128)(2,1)}, bf16[128,2048]{1,0:T(8,128)(2,1)}, u32[]{:S(2)}, u32[]{:S(2)}) collective-permute-start(bf16[128,2048]{1,0:T(8,128)(2,1)} %param.36), channel_id=1, source_target_pairs={{0,2},{2,4},{4,6},{6,7},{7,5},{5,3},{3,1},{1,0},{8,10},{10,12},{12... | collective-permute-start | bytes 1572872 | tf_op jit(solution)/shard_map/ppermute | solution.py:128
  56.8 25.4 %collective-permute-start.42 = (bf16[128,2048]{1,0:T(8,128)(2,1)}, bf16[128,2048]{1,0:T(8,128)(2,1)S(1)}, u32[]{:S(2)}, u32[]{:S(2)}) collective-permute-start(bf16[128,2048]{1,0:T(8,128)(2,1)} %param.36), channel_id=1, source_target_pairs={{2,0},{4,2},{6,4},{7,6},{5,7},{3,5},{1,3},{0,1},{10,8},{12,10},{14... | collective-permute-start | bytes 1572872 | tf_op jit(solution)/shard_map/ppermute | solution.py:128
  64.2 49.3 %collective-permute-start.2 = (bf16[128,2048]{1,0:T(8,128)(2,1)}, bf16[128,2048]{1,0:T(8,128)(2,1)}, u32[]{:S(2)}, u32[]{:S(2)}) collective-permute-start(bf16[128,2048]{1,0:T(8,128)(2,1)} %collective-permute-done), channel_id=1, source_target_pairs={{0,2},{2,4},{4,6},{6,7},{7,5},{5,3},{3,1},{1,0},{8,10},{10,12},{12... | collective-permute-start | bytes 1572872 | tf_op jit(solution)/shard_map/ppermute | solution.py:128
  68.1 48.8 %collective-permute-start.3 = (bf16[128,2048]{1,0:T(8,128)(2,1)}, bf16[128,2048]{1,0:T(8,128)(2,1)}, u32[]{:S(2)}, u32[]{:S(2)}) collective-permute-start(bf16[128,2048]{1,0:T(8,128)(2,1)} %collective-permute-done.1), channel_id=1, source_target_pairs={{2,0},{4,2},{6,4},{7,6},{5,7},{3,5},{1,3},{0,1},{10,8},{12,10},{14... | collective-permute-start | bytes 1572872 | tf_op jit(solution)/shard_map/ppermute | solution.py:128
  82.2 38.1 %collective-permute-start.43 = (bf16[128,2048]{1,0:T(8,128)(2,1)}, bf16[128,2048]{1,0:T(8,128)(2,1)}, u32[]{:S(2)}, u32[]{:S(2)}) collective-permute-start(bf16[128,2048]{1,0:T(8,128)(2,1)} %collective-permute-done.41), channel_id=1, source_target_pairs={{0,2},{2,4},{4,6},{6,7},{7,5},{5,3},{3,1},{1,0},{8,10},{10,12},{12... | collective-permute-start | bytes 1572872 | tf_op jit(solution)/shard_map/ppermute | solution.py:128
  86.8 35.9 %collective-permute-start.44 = (bf16[128,2048]{1,0:T(8,128)(2,1)S(1)}, bf16[128,2048]{1,0:T(8,128)(2,1)S(1)}, u32[]{:S(2)}, u32[]{:S(2)}) collective-permute-start(bf16[128,2048]{1,0:T(8,128)(2,1)S(1)} %collective-permute-done.42), channel_id=1, source_target_pairs={{2,0},{4,2},{6,4},{7,6},{5,7},{3,5},{1,3},{0,1},{10,8},{12,10},{14... | collective-permute-start | bytes 1572872 | tf_op jit(solution)/shard_map/ppermute | solution.py:128
  106.0 146.1 %collective-permute-start.27 = (bf16[512,2048]{1,0:T(8,128)(2,1)}, bf16[512,2048]{1,0:T(8,128)(2,1)}, u32[]{:S(2)}, u32[]{:S(2)}) collective-permute-start(bf16[512,2048]{1,0:T(8,128)(2,1)} %constant_dynamic-update-slice_fusion.69), channel_id=1, source_target_pairs={{0,8},{8,0},{16,24},{24,16},{1,9},{9,1},{17,25},{25,17},{2,10},{10... | collective-permute-start | bytes 6291464 | tf_op jit(solution)/shard_map/ppermute | solution.py:207
  113.5 129.8 %collective-permute-start.28 = (bf16[512,2048]{1,0:T(8,128)(2,1)}, bf16[512,2048]{1,0:T(8,128)(2,1)}, u32[]{:S(2)}, u32[]{:S(2)}) collective-permute-start(bf16[512,2048]{1,0:T(8,128)(2,1)} %constant_dynamic-update-slice_fusion.69), channel_id=1, source_target_pairs={{0,16},{8,24},{16,0},{24,8},{1,17},{9,25},{17,1},{25,9},{2,18},{10... | collective-permute-start | bytes 6291464 | tf_op jit(solution)/shard_map/ppermute | solution.py:203
  120.3 25.3 %collective-permute-start.5 = (bf16[128,2048]{1,0:T(8,128)(2,1)}, bf16[128,2048]{1,0:T(8,128)(2,1)}, u32[]{:S(2)}, u32[]{:S(2)}) collective-permute-start(bf16[128,2048]{1,0:T(8,128)(2,1)} %collective-permute-done.3), channel_id=1, source_target_pairs={{2,0},{4,2},{6,4},{7,6},{5,7},{3,5},{1,3},{0,1},{10,8},{12,10},{14... | collective-permute-start | bytes 1572872 | tf_op jit(solution)/shard_map/ppermute | solution.py:128
  122.7 20.9 %collective-permute-start.45 = (bf16[128,2048]{1,0:T(8,128)(2,1)}, bf16[128,2048]{1,0:T(8,128)(2,1)}, u32[]{:S(2)}, u32[]{:S(2)}) collective-permute-start(bf16[128,2048]{1,0:T(8,128)(2,1)} %collective-permute-done.43), channel_id=1, source_target_pairs={{0,2},{2,4},{4,6},{6,7},{7,5},{5,3},{3,1},{1,0},{8,10},{10,12},{12... | collective-permute-start | bytes 1572872 | tf_op jit(solution)/shard_map/ppermute | solution.py:128
  125.9 148.7 %all-to-all-start.1 = ((bf16[8,64,2304]{2,1,0:T(8,128)(2,1)}), bf16[8,64,2304]{2,1,0:T(8,128)(2,1)S(1)}, u32[]{:S(2)}, u32[]{:S(2)}) async-start(bf16[8,64,2304]{2,1,0:T(8,128)(2,1)} %pad_maximum_fusion.2), calls=%async_computation.1 | async-start | bytes 4718592 | tf_op jit(solution)/shard_map/all_to_all | solution.py:317
  131.9 40.0 %collective-permute-start.46 = (bf16[128,2048]{1,0:T(8,128)(2,1)S(1)}, bf16[128,2048]{1,0:T(8,128)(2,1)S(1)}, u32[]{:S(2)}, u32[]{:S(2)}) collective-permute-start(bf16[128,2048]{1,0:T(8,128)(2,1)S(1)} %copy-done.30), channel_id=1, source_target_pairs={{2,0},{4,2},{6,4},{7,6},{5,7},{3,5},{1,3},{0,1},{10,8},{12,10},{14... | collective-permute-start | bytes 1572872 | tf_op jit(solution)/shard_map/ppermute | solution.py:128
  143.6 74.2 %collective-permute-start.8 = (bf16[512,768]{1,0:T(8,128)(2,1)S(1)}, bf16[512,768]{1,0:T(8,128)(2,1)S(1)}, u32[]{:S(2)}, u32[]{:S(2)}) collective-permute-start(bf16[512,768]{1,0:T(8,128)(2,1)S(1)} %bitcast.319), channel_id=1, source_target_pairs={{0,8},{8,0},{16,24},{24,16},{1,9},{9,1},{17,25},{25,17},{2,10},{10... | collective-permute-start | bytes 2359304 | tf_op jit(solution)/shard_map/ppermute | solution.py:207
  145.5 39.6 %collective-permute-start.6 = (bf16[64,2048]{1,0:T(8,128)(2,1)S(1)}, bf16[64,2048]{1,0:T(8,128)(2,1)S(1)}, u32[]{:S(2)}, u32[]{:S(2)}) collective-permute-start(bf16[64,2048]{1,0:T(8,128)(2,1)S(1)} %slice.404), channel_id=1, source_target_pairs={{0,2},{2,4},{4,6},{6,7},{7,5},{5,3},{3,1},{1,0},{8,10},{10,12},{12... | collective-permute-start | bytes 786440 | tf_op jit(solution)/shard_map/ppermute | solution.py:128
  172.0 31.1 %collective-permute-start.7 = (bf16[64,2048]{1,0:T(8,128)(2,1)S(1)}, bf16[64,2048]{1,0:T(8,128)(2,1)S(1)}, u32[]{:S(2)}, u32[]{:S(2)}) collective-permute-start(bf16[64,2048]{1,0:T(8,128)(2,1)S(1)} %slice.405), channel_id=1, source_target_pairs={{2,0},{4,2},{6,4},{7,6},{5,7},{3,5},{1,3},{0,1},{10,8},{12,10},{14... | collective-permute-start | bytes 786440 | tf_op jit(solution)/shard_map/ppermute | solution.py:128
  185.1 27.2 %collective-permute-start.9 = (bf16[512,768]{1,0:T(8,128)(2,1)S(1)}, bf16[512,768]{1,0:T(8,128)(2,1)S(1)}, u32[]{:S(2)}, u32[]{:S(2)}) collective-permute-start(bf16[512,768]{1,0:T(8,128)(2,1)S(1)} %bitcast.320), channel_id=1, source_target_pairs={{0,16},{8,24},{16,0},{24,8},{1,17},{9,25},{17,1},{25,9},{2,18},{10... | collective-permute-start | bytes 2359304 | tf_op jit(solution)/shard_map/ppermute | solution.py:203
  212.4 25.6 %collective-permute-start.48 = (bf16[64,2048]{1,0:T(8,128)(2,1)}, bf16[64,2048]{1,0:T(8,128)(2,1)}, u32[]{:S(2)}, u32[]{:S(2)}) collective-permute-start(bf16[64,2048]{1,0:T(8,128)(2,1)} %slice.422), channel_id=1, source_target_pairs={{2,0},{4,2},{6,4},{7,6},{5,7},{3,5},{1,3},{0,1},{10,8},{12,10},{14... | collective-permute-start | bytes 786440 | tf_op jit(solution)/shard_map/ppermute | solution.py:128
  243.2 51.0 %collective-permute-start.29 = (bf16[512,2048]{1,0:T(8,128)(2,1)}, bf16[512,2048]{1,0:T(8,128)(2,1)}, u32[]{:S(2)}, u32[]{:S(2)}) collective-permute-start(bf16[512,2048]{1,0:T(8,128)(2,1)} %collective-permute-done.28), channel_id=1, source_target_pairs={{0,8},{8,0},{16,24},{24,16},{1,9},{9,1},{17,25},{25,17},{2,10},{10... | collective-permute-start | bytes 6291464 | tf_op jit(solution)/shard_map/ppermute | solution.py:207
  274.6 54.6 %collective-permute-start.30 = (bf16[512,2304]{1,0:T(8,128)(2,1)S(1)}, bf16[512,2304]{1,0:T(8,128)(2,1)S(1)}, u32[]{:S(2)}, u32[]{:S(2)}) collective-permute-start(bf16[512,2304]{1,0:T(8,128)(2,1)S(1)} %bitcast.304), channel_id=1, source_target_pairs={{0,8},{8,0},{16,24},{24,16},{1,9},{9,1},{17,25},{25,17},{2,10},{10... | collective-permute-start | bytes 7077896 | tf_op jit(solution)/shard_map/ppermute | solution.py:207
  274.6 53.7 %collective-permute-start.31 = (bf16[512,2304]{1,0:T(8,128)(2,1)S(1)}, bf16[512,2304]{1,0:T(8,128)(2,1)S(1)}, u32[]{:S(2)}, u32[]{:S(2)}) collective-permute-start(bf16[512,2304]{1,0:T(8,128)(2,1)S(1)} %bitcast.305), channel_id=1, source_target_pairs={{0,16},{8,24},{16,0},{24,8},{1,17},{9,25},{17,1},{25,9},{2,18},{10... | collective-permute-start | bytes 7077896 | tf_op jit(solution)/shard_map/ppermute | solution.py:203
  382.6 20.6 %collective-permute-start.34 = (bf16[128,2048]{1,0:T(8,128)(2,1)S(1)}, bf16[128,2048]{1,0:T(8,128)(2,1)S(1)}, u32[]{:S(2)}, u32[]{:S(2)}) collective-permute-start(bf16[128,2048]{1,0:T(8,128)(2,1)S(1)} %get-tuple-element.64), channel_id=1, source_target_pairs={{0,2},{2,4},{4,6},{6,7},{7,5},{5,3},{3,1},{1,0},{8,10},{10,12},{12... | collective-permute-start | bytes 1572872 | tf_op jit(solution)/shard_map/ppermute | solution.py:128
  416.4 22.1 %collective-permute-start.56 = (bf16[128,2048]{1,0:T(8,128)(2,1)S(1)}, bf16[128,2048]{1,0:T(8,128)(2,1)S(1)}, u32[]{:S(2)}, u32[]{:S(2)}) collective-permute-start(bf16[128,2048]{1,0:T(8,128)(2,1)S(1)} %get-tuple-element.53), channel_id=1, source_target_pairs={{2,0},{4,2},{6,4},{7,6},{5,7},{3,5},{1,3},{0,1},{10,8},{12,10},{14... | collective-permute-start | bytes 1572872 | tf_op jit(solution)/shard_map/ppermute | solution.py:128
  416.9 21.7 %collective-permute-start.52 = (bf16[128,2048]{1,0:T(8,128)(2,1)S(1)}, bf16[128,2048]{1,0:T(8,128)(2,1)S(1)}, u32[]{:S(2)}, u32[]{:S(2)}) collective-permute-start(bf16[128,2048]{1,0:T(8,128)(2,1)S(1)} %get-tuple-element.52), channel_id=1, source_target_pairs={{0,2},{2,4},{4,6},{6,7},{7,5},{5,3},{3,1},{1,0},{8,10},{10,12},{12... | collective-permute-start | bytes 1572872 | tf_op jit(solution)/shard_map/ppermute | solution.py:128
  466.2 30.0 %collective-permute-start.84 = (f32[19456]{0:T(1024)S(1)}, f32[19456]{0:T(1024)S(1)}, u32[]{:S(2)}, u32[]{:S(2)}) collective-permute-start(f32[19456]{0:T(1024)S(1)} %add.693), channel_id=1, source_target_pairs={{0,1},{1,0},{2,3},{3,2},{4,5},{5,4},{6,7},{7,6},{8,9},{9,8},{10,11... | collective-permute-start | bytes 233480 | tf_op jit(solution)/shard_map/ppermute | solution.py:232
  494.2 69.1 %collective-permute-start.57 = (bf16[128,2048]{1,0:T(8,128)(2,1)S(1)}, bf16[128,2048]{1,0:T(8,128)(2,1)S(1)}, u32[]{:S(2)}, u32[]{:S(2)}) collective-permute-start(bf16[128,2048]{1,0:T(8,128)(2,1)S(1)} %get-tuple-element.28), channel_id=1, source_target_pairs={{0,2},{2,4},{4,6},{6,7},{7,5},{5,3},{3,1},{1,0},{8,10},{10,12},{12... | collective-permute-start | bytes 1572872 | tf_op jit(solution)/shard_map/ppermute | solution.py:128
  495.6 69.0 %collective-permute-start.58 = (bf16[128,2048]{1,0:T(8,128)(2,1)S(1)}, bf16[128,2048]{1,0:T(8,128)(2,1)S(1)}, u32[]{:S(2)}, u32[]{:S(2)}) collective-permute-start(bf16[128,2048]{1,0:T(8,128)(2,1)S(1)} %get-tuple-element.28), channel_id=1, source_target_pairs={{2,0},{4,2},{6,4},{7,6},{5,7},{3,5},{1,3},{0,1},{10,8},{12,10},{14... | collective-permute-start | bytes 1572872 | tf_op jit(solution)/shard_map/ppermute | solution.py:128
  496.3 65.7 %collective-permute-start.85 = (f32[19456]{0:T(1024)S(1)}, f32[19456]{0:T(1024)S(1)}, u32[]{:S(2)}, u32[]{:S(2)}) collective-permute-start(f32[19456]{0:T(1024)S(1)} %add.694), channel_id=1, source_target_pairs={{0,2},{1,3},{2,0},{3,1},{4,6},{5,7},{6,4},{7,5},{8,10},{9,11},{10,... | collective-permute-start | bytes 233480 | tf_op jit(solution)/shard_map/ppermute | solution.py:232
  541.1 91.1 %collective-permute-start.87 = (bf16[2,512,2304]{2,1,0:T(8,128)(2,1)}, bf16[2,512,2304]{2,1,0:T(8,128)(2,1)}, u32[]{:S(2)}, u32[]{:S(2)}) collective-permute-start(bf16[2,512,2304]{2,1,0:T(8,128)(2,1)} %bitcast.313), channel_id=1, source_target_pairs={{0,8},{8,0},{16,24},{24,16},{1,9},{9,1},{17,25},{25,17},{2,10},{10... | collective-permute-start | bytes 14155784 | tf_op jit(solution)/shard_map/ppermute | solution.py:215
  621.0 26.7 %collective-permute-start.65 = (bf16[64,2048]{1,0:T(8,128)(2,1)}, bf16[64,2048]{1,0:T(8,128)(2,1)S(1)}, u32[]{:S(2)}, u32[]{:S(2)}) collective-permute-start(bf16[64,2048]{1,0:T(8,128)(2,1)} %get-tuple-element.50), channel_id=1, source_target_pairs={{0,2},{2,4},{4,6},{6,7},{7,5},{5,3},{3,1},{1,0},{8,10},{10,12},{12... | collective-permute-start | bytes 786440 | tf_op jit(solution)/shard_map/ppermute | solution.py:128
  622.7 25.0 %collective-permute-start.69 = (bf16[64,2048]{1,0:T(8,128)(2,1)}, bf16[64,2048]{1,0:T(8,128)(2,1)}, u32[]{:S(2)}, u32[]{:S(2)}) collective-permute-start(bf16[64,2048]{1,0:T(8,128)(2,1)} %get-tuple-element.51), channel_id=1, source_target_pairs={{2,0},{4,2},{6,4},{7,6},{5,7},{3,5},{1,3},{0,1},{10,8},{12,10},{14... | collective-permute-start | bytes 786440 | tf_op jit(solution)/shard_map/ppermute | solution.py:128
  637.4 80.9 %collective-permute-start.88 = (bf16[512,2304]{1,0:T(8,128)(2,1)}, bf16[512,2304]{1,0:T(8,128)(2,1)}, u32[]{:S(2)}, u32[]{:S(2)}) collective-permute-start(bf16[512,2304]{1,0:T(8,128)(2,1)} %fusion.32), channel_id=1, source_target_pairs={{0,16},{8,24},{16,0},{24,8},{1,17},{9,25},{17,1},{25,9},{2,18},{10... | collective-permute-start | bytes 7077896 | tf_op jit(solution)/shard_map/ppermute | solution.py:221
  643.8 63.7 %collective-permute-start.79 = (bf16[512,768]{1,0:T(8,128)(2,1)S(1)}, bf16[512,768]{1,0:T(8,128)(2,1)S(1)}, u32[]{:S(2)}, u32[]{:S(2)}) collective-permute-start(bf16[512,768]{1,0:T(8,128)(2,1)S(1)} %fusion.66), channel_id=1, source_target_pairs={{0,16},{8,24},{16,0},{24,8},{1,17},{9,25},{17,1},{25,9},{2,18},{10... | collective-permute-start | bytes 2359304 | tf_op jit(solution)/shard_map/ppermute | solution.py:221
  649.8 63.9 %collective-permute-start.66 = (bf16[128,2048]{1,0:T(8,128)(2,1)}, bf16[128,2048]{1,0:T(8,128)(2,1)S(1)}, u32[]{:S(2)}, u32[]{:S(2)}) collective-permute-start(bf16[128,2048]{1,0:T(8,128)(2,1)} %get-tuple-element.48), channel_id=1, source_target_pairs={{0,2},{2,4},{4,6},{6,7},{7,5},{5,3},{3,1},{1,0},{8,10},{10,12},{12... | collective-permute-start | bytes 1572872 | tf_op jit(solution)/shard_map/ppermute | solution.py:128
  651.5 62.2 %collective-permute-start.70 = (bf16[128,2048]{1,0:T(8,128)(2,1)}, bf16[128,2048]{1,0:T(8,128)(2,1)S(1)}, u32[]{:S(2)}, u32[]{:S(2)}) collective-permute-start(bf16[128,2048]{1,0:T(8,128)(2,1)} %get-tuple-element.49), channel_id=1, source_target_pairs={{2,0},{4,2},{6,4},{7,6},{5,7},{3,5},{1,3},{0,1},{10,8},{12,10},{14... | collective-permute-start | bytes 1572872 | tf_op jit(solution)/shard_map/ppermute | solution.py:128
  708.5 26.4 %all-to-all-start.2 = ((bf16[8,64,768]{2,1,0:T(8,128)(2,1)}), bf16[8,64,768]{2,1,0:T(8,128)(2,1)S(1)}, u32[]{:S(2)}, u32[]{:S(2)}) async-start(bf16[8,64,768]{2,1,0:T(8,128)(2,1)} %bitcast.71), calls=%async_computation.2 | async-start | bytes 1572864 | tf_op jit(solution)/shard_map/all_to_all | solution.py:322
  713.7 39.2 %collective-permute-start.80 = (bf16[2,64,2048]{2,1,0:T(8,128)(2,1)}, bf16[2,64,2048]{2,1,0:T(8,128)(2,1)S(1)}, u32[]{:S(2)}, u32[]{:S(2)}) collective-permute-start(bf16[2,64,2048]{2,1,0:T(8,128)(2,1)} %dynamic-slice_bitcast_fusion.1), channel_id=1, source_target_pairs={{0,8},{8,0},{16,24},{24,16},{1,9},{9,1},{17,25},{25,17},{2,10},{10... | collective-permute-start | bytes 1572872 | tf_op jit(solution)/shard_map/ppermute | solution.py:215
  716.3 23.5 %collective-permute-start.67 = (bf16[128,2048]{1,0:T(8,128)(2,1)}, bf16[128,2048]{1,0:T(8,128)(2,1)}, u32[]{:S(2)}, u32[]{:S(2)}) collective-permute-start(bf16[128,2048]{1,0:T(8,128)(2,1)} %get-tuple-element.46), channel_id=1, source_target_pairs={{0,2},{2,4},{4,6},{6,7},{7,5},{5,3},{3,1},{1,0},{8,10},{10,12},{12... | collective-permute-start | bytes 1572872 | tf_op jit(solution)/shard_map/ppermute | solution.py:128
  718.3 21.5 %collective-permute-start.71 = (bf16[128,2048]{1,0:T(8,128)(2,1)}, bf16[128,2048]{1,0:T(8,128)(2,1)}, u32[]{:S(2)}, u32[]{:S(2)}) collective-permute-start(bf16[128,2048]{1,0:T(8,128)(2,1)} %get-tuple-element.47), channel_id=1, source_target_pairs={{2,0},{4,2},{6,4},{7,6},{5,7},{3,5},{1,3},{0,1},{10,8},{12,10},{14... | collective-permute-start | bytes 1572872 | tf_op jit(solution)/shard_map/ppermute | solution.py:128
  735.9 97.5 %all-to-all-start.3 = ((bf16[8,64,2304]{2,1,0:T(8,128)(2,1)}), bf16[8,64,2304]{2,1,0:T(8,128)(2,1)S(1)}, u32[]{:S(2)}, u32[]{:S(2)}) async-start(bf16[8,64,2304]{2,1,0:T(8,128)(2,1)} %bitcast.82), calls=%async_computation.3 | async-start | bytes 4718592 | tf_op jit(solution)/shard_map/all_to_all | solution.py:322
  741.7 34.8 %collective-permute-start.72 = (bf16[128,2048]{1,0:T(8,128)(2,1)S(1)}, bf16[128,2048]{1,0:T(8,128)(2,1)S(1)}, u32[]{:S(2)}, u32[]{:S(2)}) collective-permute-start(bf16[128,2048]{1,0:T(8,128)(2,1)S(1)} %get-tuple-element.45), channel_id=1, source_target_pairs={{2,0},{4,2},{6,4},{7,6},{5,7},{3,5},{1,3},{0,1},{10,8},{12,10},{14... | collective-permute-start | bytes 1572872 | tf_op jit(solution)/shard_map/ppermute | solution.py:128
  743.6 43.3 %collective-permute-start.68 = (bf16[128,2048]{1,0:T(8,128)(2,1)S(1)}, bf16[128,2048]{1,0:T(8,128)(2,1)S(1)}, u32[]{:S(2)}, u32[]{:S(2)}) collective-permute-start(bf16[128,2048]{1,0:T(8,128)(2,1)S(1)} %get-tuple-element.44), channel_id=1, source_target_pairs={{0,2},{2,4},{4,6},{6,7},{7,5},{5,3},{3,1},{1,0},{8,10},{10,12},{12... | collective-permute-start | bytes 1572872 | tf_op jit(solution)/shard_map/ppermute | solution.py:128
  754.1 37.4 %collective-permute-start.81 = (bf16[64,2048]{1,0:T(8,128)(2,1)S(1)}, bf16[64,2048]{1,0:T(8,128)(2,1)S(1)}, u32[]{:S(2)}, u32[]{:S(2)}) collective-permute-start(bf16[64,2048]{1,0:T(8,128)(2,1)S(1)} %fusion.77), channel_id=1, source_target_pairs={{0,16},{8,24},{16,0},{24,8},{1,17},{9,25},{17,1},{25,9},{2,18},{10... | collective-permute-start | bytes 786440 | tf_op jit(solution)/shard_map/ppermute | solution.py:221
  798.0 21.5 %collective-permute-start.76 = (f32[10240]{0:T(1024)S(1)}, f32[10240]{0:T(1024)S(1)}, u32[]{:S(2)}, u32[]{:S(2)}) collective-permute-start(f32[10240]{0:T(1024)S(1)} %add.681), channel_id=1, source_target_pairs={{0,2},{1,3},{2,0},{3,1},{4,6},{5,7},{6,4},{7,5},{8,10},{9,11},{10,... | collective-permute-start | bytes 122888 | tf_op jit(solution)/shard_map/ppermute | solution.py:232
  (106 other events, 1661.0 us)

commit v2 on v1

v2 whole, which is shorter than its diff:
```python
import math

import jax
import jax.numpy as jnp
from jax import lax
from jax.experimental import pallas as pl
from jax.experimental.pallas import tpu as pltpu
from jax.sharding import Mesh
from jax.sharding import PartitionSpec as P

HEADS = 16
HEAD = 128
LANES = 128

epsilon = 1e-05
masked_value = -1000000000.0
log2_e = math.log2(math.e)
bf16 = jnp.bfloat16
f32 = jnp.float32

EVERY = ("x", "core", "z", "y")
GROUP = ("z", "y")
TEAM = ("core", "z")


def norm_parts(values):
    average = jnp.mean(values, axis=-1, keepdims=True)
    centered = values - average
    spread = jnp.mean(centered * centered, axis=-1, keepdims=True)
    inverse = lax.rsqrt(spread + epsilon)
    return (centered * inverse, inverse)


def layer_norm(values, gain, bias):
    unit, _ = norm_parts(values)
    return unit * gain + bias


def layer_norm_back(unit, inverse, gain, grad):
    scaled = grad * gain
    first = jnp.mean(scaled, axis=-1, keepdims=True)
    second = jnp.mean(scaled * unit, axis=-1, keepdims=True)
    return inverse * (scaled - first - unit * second)


def gelu_tanh(values):
    return (
        0.5
        * values
        * (1.0 + jnp.tanh(0.7978845608028654 * (values + 0.044715 * values * values * values)))
    )


def geglu(gate, upper):
    return gelu_tanh(gate) * upper


def group_layout(lengths, prefixes, count):
    ends = jnp.cumsum(lengths)
    starts = ends - lengths
    places = jnp.arange(count, dtype=jnp.int32)
    member = ((places[:, None] >= starts[None, :]) & (places[:, None] < ends[None, :])).astype(
        jnp.int32
    )
    first = jnp.sum(member * starts[None, :], axis=1)
    limits = starts + jnp.minimum(prefixes, lengths)
    bound = jnp.sum(member * limits[None, :], axis=1)
    return (places - first, first, jnp.maximum(places + 1, bound))


def rotary_tables(position):
    half_size = HEAD // 2
    rates = jnp.exp(jnp.arange(half_size, dtype=f32) * (-2.0 * math.log(10000.0) / HEAD))
    angles = position.astype(f32)[:, None] * rates[None, :]
    cosine = jnp.cos(angles)
    sine = jnp.sin(angles)
    return (jnp.concatenate([cosine, cosine], axis=1), jnp.concatenate([-sine, sine], axis=1))


def swap_halves(values):
    half_size = HEAD // 2
    return jnp.concatenate([values[:, half_size:], values[:, :half_size]], axis=1)


def rotate(values, cosine, sine):
    return values * cosine + swap_halves(values) * sine


def rotate_back(values, cosine, sine):
    return values * cosine + swap_halves(values * sine)


def dot_nn(left, right):
    return lax.dot_general(left, right, (((1,), (0,)), ((), ())), preferred_element_type=f32)


def dot_nt(left, right):
    return lax.dot_general(left, right, (((1,), (1,)), ((), ())), preferred_element_type=f32)


def dot_tn(left, right):
    return lax.dot_general(left, right, (((0,), (0,)), ((), ())), preferred_element_type=f32)


def put(total, piece, where):
    return lax.dynamic_update_slice(total, piece, [jnp.int32(i) for i in where])


def cut(values, where, sizes):
    return lax.dynamic_slice(values, [jnp.int32(i) for i in where], sizes)


class Clock:
    def __init__(self):
        self.last = None

    def hold(self, *values):
        if self.last is None:
            return values if len(values) > 1 else values[0]
        held = lax.optimization_barrier((*values, self.last))[:-1]
        return held if len(values) > 1 else held[0]

    def run(self, step, *values):
        held = self.hold(*values)
        out = step(*held) if len(values) > 1 else step(held)
        return self(*out) if isinstance(out, (tuple, list)) else self(out)

    def __call__(self, *values):
        given = values if self.last is None else (*values, self.last)
        out = lax.optimization_barrier(given)
        self.last = out[0]
        out = out[: len(values)]
        return out if len(values) > 1 else out[0]


class Task:
    def __init__(self, name, steps):
        self.name, self.steps = name, steps
        self.result = None
        self.step()

    def step(self):
        with jax.named_scope(self.name):
            try:
                next(self.steps)
            except StopIteration as end:
                self.steps, self.result = None, end.value
        return self

    def finish(self):
        while self.steps is not None:
            self.step()
        return self.result


class Ring:
    def __init__(self, rows, columns, clock):
        count = rows * columns
        self.count = count
        self.clock = clock
        if columns == 2:
            order = [2 * z for z in range(rows)] + [2 * z + 1 for z in reversed(range(rows))]
        else:
            order = list(range(count))
        self.forward = [(order[i], order[(i + 1) % count]) for i in range(count)]
        self.backward = [(b, a) for a, b in self.forward]
        me = lax.axis_index(GROUP)
        if columns == 2:
            place = jnp.where(me % 2 == 0, me // 2, count - 1 - me // 2)
        else:
            place = me
        self.me = me
        self.at = []
        for k in range(count):
            spot = lax.rem(place + k, count)
            if columns == 2:
                spot = jnp.where(spot < rows, 2 * spot, 2 * (count - 1 - spot) + 1)
            self.at.append(spot)

    def ahead(self, k):
        return self.at[k % self.count]

    def send(self, values, forward):
        return lax.ppermute(values, GROUP, self.forward if forward else self.backward)

    def gather(self, block):
        half_way = self.count // 2
        rows, width = block.shape
        half = rows // 2
        block = self.clock.hold(block)
        total = jnp.zeros((self.count * rows, width), block.dtype)
        total = put(total, block, (self.me * rows, 0))
        ahead = behind = block
        for k in range(1, half_way):
            behind, ahead = self.send(behind, True), self.send(ahead, False)
            yield
            behind, ahead = self.clock(behind, ahead)
            total = put(total, behind, (self.ahead(-k) * rows, 0))
            total = put(total, ahead, (self.ahead(k) * rows, 0))
        behind, ahead = self.send(behind[:half], True), self.send(ahead[half:], False)
        yield
        behind, ahead = self.clock(behind, ahead)
        total = put(total, behind, (self.ahead(half_way) * rows, 0))
        return put(total, ahead, (self.ahead(half_way) * rows + half, 0))

    def scatter(self, parts):
        half_way = self.count // 2
        rows, width = parts.shape[0] // self.count, parts.shape[1]
        half = rows // 2
        parts = self.clock.hold(parts)

        def piece(owner, start=0, size=rows):
            return cut(parts, (owner * rows + start, 0), (size, width)).astype(f32)

        low, high = piece(self.ahead(half_way), 0, half), piece(self.ahead(half_way), half, half)
        low, high = self.clock(low.astype(bf16), high.astype(bf16))
        low, high = self.send(low, True), self.send(high, False)
        yield
        low, high = self.clock(low, high)
        nothing = jnp.zeros_like(low)
        forward = jnp.concatenate([low, nothing], axis=0)
        backward = jnp.concatenate([nothing, high], axis=0)
        for k in range(half_way - 1, 0, -1):
            forward = (forward.astype(f32) + piece(self.ahead(k))).astype(bf16)
            backward = (backward.astype(f32) + piece(self.ahead(-k))).astype(bf16)
            forward, backward = self.clock(forward, backward)
            forward, backward = self.send(forward, True), self.send(backward, False)
            yield
            forward, backward = self.clock(forward, backward)
        return forward, backward, piece(self.me)


class Line:
    def __init__(self, count, clock):
        self.count = count
        self.clock = clock
        self.me = lax.axis_index("z")

    def up(self, values, low, high):
        return lax.ppermute(values, "z", [(i, i + 1) for i in range(low, high)])

    def down(self, values, low, high):
        return lax.ppermute(values, "z", [(i + 1, i) for i in range(low, high)])

    def gather(self, block, axis):
        last = self.count - 1
        size = block.shape[axis]
        shape = list(block.shape)
        shape[axis] = size * (self.count + 1)
        block = self.clock.hold(block)
        total = jnp.zeros(shape, block.dtype)

        def put_at(total, piece, owner):
            owner = jnp.where((owner < 0) | (owner > last), self.count, owner)
            return put(total, piece, [owner * size if d == axis else 0 for d in range(2)])

        total = put_at(total, block, self.me)
        below = above = block
        for k in range(last):
            below, above = self.up(below, k, last), self.down(above, 0, last - k)
            yield
            below, above = self.clock(below, above)
            total = put_at(total, below, self.me - k - 1)
            total = put_at(total, above, self.me + k + 1)
        return total

    def scatter(self, parts, before=None):
        last = self.count - 1
        rows, width = parts.shape[0] // self.count, parts.shape[1]
        parts = self.clock.hold(parts)

        def piece(owner):
            return cut(parts, (owner * rows, 0), (rows, width)).astype(f32)

        below = above = None
        for k in range(last, 0, -1):
            upward, downward = piece(self.me + k), piece(self.me - k)
            if below is not None:
                upward, downward = upward + below.astype(f32), downward + above.astype(f32)
            upward, downward = self.clock(upward.astype(bf16), downward.astype(bf16))
            below = self.up(upward, 0, last - k + 1)
            above = self.down(downward, k - 1, last)
            yield
            below, above = self.clock(below, above)
        return below, above, piece(self.me)


def shifts(count):
    return [[(i, (i + step) % count) for i in range(count)] for step in range(1, count)]


def from_axis(value, axis, count):
    me = lax.axis_index(axis)
    return [
        (lax.ppermute(value, axis, pairs), lax.rem(me - step + count, count))
        for step, pairs in enumerate(shifts(count), 1)
    ]


def to_axis(values, axis, count, dim):
    me = lax.axis_index(axis)
    return [
        lax.ppermute(
            lax.dynamic_index_in_dim(values, lax.rem(me + step, count), dim, False), axis, pairs
        )
        for step, pairs in enumerate(shifts(count), 1)
    ]


def in_order(found, axis, count, dim):
    me = lax.axis_index(axis)
    wide = jnp.stack((found[::-1] * 2)[:-1], axis=dim)
    where, sizes = [0] * wide.ndim, list(wide.shape)
    where[dim], sizes[dim] = count - 1 - me, count
    return cut(wide, where, sizes)


def exchange(values, axis, count, dim, clock):
    arrived = to_axis(values, axis, count, dim)
    yield
    found = [own_part(values, axis, dim)] + [clock(value) for value in arrived]
    return in_order(found, axis, count, dim)


def team_exchange(values, nz, clock):
    values = clock.hold(values).reshape(2, nz, *values.shape[1:])
    both = yield from exchange(values, "core", 2, 0, clock)
    out = yield from exchange(both, "z", nz, 1, clock)
    return out.reshape(2 * nz, *values.shape[2:])


def own_part(values, axis, dim):
    return lax.dynamic_index_in_dim(values, lax.axis_index(axis), dim, False)


def add_up(own, others):
    total = own.astype(f32)
    for other in others:
        total = total + other.astype(f32)
    return total.astype(bf16)


class Grid:
    def __init__(self, nx, ny, clock):
        self.nx, self.ny, self.clock = nx, ny, clock
        self.x, self.y = lax.axis_index("x"), lax.axis_index("y")

    def gather(self, block):
        half = block.shape[2] // 2 // LANES * LANES
        block = self.clock.hold(block)
        along_x, along_y = from_axis(block, "x", self.nx), from_axis(block, "y", self.ny)
        yield
        values = self.clock(*[v for v, _ in along_x + along_y])
        along_x, along_y = values[: self.nx - 1], values[self.nx - 1 :]
        left = [[w for w, _ in from_axis(v[..., :half], "y", self.ny)] for v in along_x]
        right = [[w for w, _ in from_axis(v[..., half:], "x", self.nx)] for v in along_y]
        own = in_order([block, *along_y], "y", self.ny, 1)
        yield
        found = [own]
        for i, value in enumerate(along_x):
            corners = [
                jnp.concatenate(self.clock(left[i][j], right[j][i]), axis=2)
                for j in range(self.ny - 1)
            ]
            found.append(in_order([value, *corners], "y", self.ny, 1))
        return [value.reshape(-1, value.shape[-1]) for value in found]

    def place(self, k):
        return lax.rem(self.x - k + self.nx, self.nx)

    def turn(self, values):
        half = values.shape[1] // self.nx
        wide = jnp.concatenate([values, values], axis=1)
        found = [
            cut(wide, (0, self.place(k) * half), (values.shape[0], half)) for k in range(self.nx)
        ]
        return jnp.concatenate(found, axis=1)

    def turn_back(self, values):
        return self.turn(values)

    def scatter(self, x_first, y_first, rows):
        nx, ny = self.nx, self.ny
        count = len(x_first)
        values = self.clock.hold(*x_first, *y_first)
        values = [v.reshape(nx, rows, ny, -1, v.shape[1]) for v in values]
        one, two = values[:count], values[count:]

        def send_x(values):
            return [
                lax.ppermute(values[k], "x", [(i, (i - k) % nx) for i in range(nx)])
                for k in range(1, nx)
            ]

        sent = [send_x(v) for v in one] + [to_axis(v, "y", ny, 2) for v in two]
        yield
        sent = [[self.clock(v) for v in group] for group in sent]
        one = [add_up(v[0], group) for v, group in zip(one, sent)]
        two = [add_up(own_part(v, "y", 2), group) for v, group in zip(two, sent[count:])]
        values = self.clock(*one, *two)
        one, two = values[:count], values[count:]
        sent = [to_axis(v, "y", ny, 1) for v in one] + [send_x(v) for v in two]
        yield
        sent = [[self.clock(v) for v in group] for group in sent]
        one = [add_up(own_part(v, "y", 1), group) for v, group in zip(one, sent)]
        two = [add_up(v[0], group) for v, group in zip(two, sent[count:])]
        return jnp.concatenate([*one, *two], axis=2)


def sum_everywhere(values, sizes, clock):
    values = clock.hold(values)
    for axis, count in sizes:
        if count & (count - 1):
            values = lax.psum(values, axis)
            continue
        step = 1
        while step < count:
            other = lax.ppermute(values, axis, [(i, i ^ step) for i in range(count)])
            yield
            values = values + clock(other)
            step *= 2
    return values


def allowed_keys(low_ref, high_ref, shape):
    places = lax.broadcasted_iota(jnp.int32, shape, 1)
    return (places >= low_ref[...]) & (places < high_ref[...])


def forward_kernel(q_ref, k_ref, v_ref, low_ref, high_ref, out_ref, lse_ref):
    scores = dot_nt(q_ref[...], k_ref[...]) * (HEAD**-0.5 * log2_e)
    allowed = allowed_keys(low_ref, high_ref, scores.shape)
    scores = jnp.where(allowed, scores, masked_value)
    largest = jnp.max(scores, axis=1, keepdims=True)
    powers = jnp.exp2(scores - largest)
    totals = jnp.sum(powers, axis=1, keepdims=True)
    probs = (powers * (1.0 / totals)).astype(bf16)
    out_ref[...] = dot_nn(probs, v_ref[...]).astype(bf16)
    lse_ref[0] = largest + jnp.log2(totals)


def backward_kernel(
    q_ref, k_ref, v_ref, g_ref, low_ref, high_ref, lse_ref, cos_ref, sin_ref, all_cos_ref, all_sin_ref,
    gq_ref, gk_ref, gv_ref, k_sum, v_sum,
):
    scale = HEAD**-0.5
    step = pl.program_id(1)

    @pl.when(step == 0)
    def _():
        k_sum[...] = jnp.zeros_like(k_sum)
        v_sum[...] = jnp.zeros_like(v_sum)

    scores = dot_nt(q_ref[...], k_ref[...]) * (scale * log2_e)
    allowed = allowed_keys(low_ref, high_ref, scores.shape)
    probs = jnp.where(allowed, jnp.exp2(scores - lse_ref[0]), 0.0)
    grad_probs = dot_nt(g_ref[...], v_ref[...])
    delta = jnp.sum(probs * grad_probs, axis=1, keepdims=True)
    grad_scores = (probs * (grad_probs - delta)).astype(bf16)
    grad_q = (dot_nn(grad_scores, k_ref[...]) * scale).astype(bf16).astype(f32)
    gq_ref[...] = rotate_back(grad_q, cos_ref[...], sin_ref[...]).astype(bf16)
    k_sum[...] += dot_tn(grad_scores, q_ref[...])
    v_sum[...] += dot_tn(probs.astype(bf16), g_ref[...])

    @pl.when(step == pl.num_programs(1) - 1)
    def _():
        grad_k = (k_sum[...] * scale).astype(bf16).astype(f32)
        gk_ref[...] = rotate_back(grad_k, all_cos_ref[...], all_sin_ref[...]).astype(bf16)
        gv_ref[...] = v_sum[...].astype(bf16)


params = pltpu.CompilerParams(vmem_limit_bytes=56 * 2**20)
cost = pl.CostEstimate(flops=0, bytes_accessed=0, transcendentals=0)


def attention_specs(count, heads, block):
    def one(column):
        return pl.BlockSpec((block, HEAD), lambda h, i: (i, column + h))

    def whole(column):
        return pl.BlockSpec((count, HEAD), lambda h, i: (0, column + h))

    edge = pl.BlockSpec((block, 1), lambda h, i: (i, 0))
    lse = pl.BlockSpec((1, block, 1), lambda h, i: (h, i, 0))
    return (one, whole, edge, lse)


def attend_forward(packed, low, high):
    count, heads = packed.shape[0], packed.shape[1] // (3 * HEAD)
    block = min(256, count)
    one, whole, edge, lse = attention_specs(count, heads, block)
    return pl.pallas_call(
        forward_kernel,
        grid=(heads, count // block),
        in_specs=[one(0), whole(heads), whole(2 * heads), edge, edge],
        out_specs=[one(0), lse],
        out_shape=[
            jax.ShapeDtypeStruct((count, heads * HEAD), bf16),
            jax.ShapeDtypeStruct((heads, count, 1), f32),
        ],
        compiler_params=params,
        cost_estimate=cost,
        name="attend_forward",
    )(packed, packed, packed, low, high)


def attend_backward(packed, grads, low, high, log_sums, cosine, sine):
    count, heads = packed.shape[0], packed.shape[1] // (3 * HEAD)
    block = min(256, count)
    one, whole, edge, lse = attention_specs(count, heads, block)
    shape = jax.ShapeDtypeStruct((count, heads * HEAD), bf16)
    turn = pl.BlockSpec((block, HEAD), lambda h, i: (i, 0))
    turn_all = pl.BlockSpec((count, HEAD), lambda h, i: (0, 0))
    return pl.pallas_call(
        backward_kernel,
        grid=(heads, count // block),
        in_specs=[one(0), whole(heads), whole(2 * heads), one(0), edge, edge, lse]
        + [turn, turn, turn_all, turn_all],
        out_specs=[one(0), whole(0), whole(0)],
        out_shape=[shape, shape, shape],
        scratch_shapes=[pltpu.VMEM((count, HEAD), f32), pltpu.VMEM((count, HEAD), f32)],
        compiler_params=params,
        cost_estimate=cost,
        name="attend_backward",
    )(packed, packed, packed, grads, low, high, log_sums, cosine, sine, cosine, sine)


def over_rows(name, body, block, rows, whole, outs, sums=(), places=None, scratch=()):
    count = rows[-1].shape[0]
    places = jnp.zeros((1,), jnp.int32) if places is None else places

    def kernel(places_ref, *refs):
        n, m, k = len(rows), len(rows) + len(whole), len(rows) + len(whole) + len(outs)
        if sums:

            @pl.when(pl.program_id(0) == 0)
            def _():
                for ref in refs[k : k + len(sums)]:
                    ref[...] = jnp.zeros_like(ref)

        body(refs[:n], refs[n:m], places_ref, refs[m:k], refs[k:])

    room = [pltpu.VMEM((block, width), kind) for width, kind in scratch]

    def by_row(i, places):
        return (i, 0)

    def fixed(i, places):
        return (0, 0)

    return pl.pallas_call(
        kernel,
        grid_spec=pltpu.PrefetchScalarGridSpec(
            num_scalar_prefetch=1,
            grid=(count // block,),
            in_specs=[
                pl.BlockSpec((block, a.shape[1]), by_row) for a in rows
            ]
            + [pl.BlockSpec(a.shape, fixed) for a in whole],
            out_specs=[pl.BlockSpec((block, width), by_row) for width, _ in outs]
            + [pl.BlockSpec((1, width), fixed) for width in sums],
            scratch_shapes=room,
        ),
        out_shape=[jax.ShapeDtypeStruct((count, width), kind) for width, kind in outs]
        + [jax.ShapeDtypeStruct((1, width), f32) for width in sums],
        compiler_params=params,
        cost_estimate=cost,
        name=name,
    )(places, *rows, *whole)


def columns_of(ref, place, width):
    return ref.at[:, pl.ds(pl.multiple_of(place * width, width), width)]


def project_pieces(left_ref, pieces, places_ref):
    total = None
    for i, piece in enumerate(pieces):
        depth = piece.shape[0]
        term = dot_nn(columns_of(left_ref, places_ref[i], depth)[...], piece[...])
        total = term if total is None else total + term
    return total


def transposed_sums(name, lefts, rights, block=256):
    rights = [r if isinstance(r, (tuple, list)) else [r] for r in rights]
    depth = lefts[0].shape[1]
    block = min(block, depth)
    width = sum(r.shape[1] for r in rights[0])
    flat = [r for group in rights for r in group]

    def kernel(*refs):
        left_refs, right_refs, out_ref = refs[: len(lefts)], refs[len(lefts) : -1], refs[-1]
        per = len(rights[0])
        start = 0
        for j in range(per):
            size = rights[0][j].shape[1]
            total = None
            for i, left in enumerate(left_refs):
                term = dot_tn(left[...], right_refs[i * per + j][...])
                total = term if total is None else total + term
            out_ref[:, start : start + size] = total.astype(bf16)
            start += size

    return pl.pallas_call(
        kernel,
        grid=(depth // block,),
        in_specs=[pl.BlockSpec((a.shape[0], block), lambda i: (0, i)) for a in lefts]
        + [pl.BlockSpec(a.shape, lambda i: (0, 0)) for a in flat],
        out_specs=pl.BlockSpec((block, width), lambda i: (i, 0)),
        out_shape=jax.ShapeDtypeStruct((depth, width), bf16),
        compiler_params=params,
        cost_estimate=cost,
        name=name,
    )(*lefts, *flat)


def times_transposed(name, left, pieces, places, width):
    def body(rows, whole, places_ref, outs, sums):
        for i, piece in enumerate(whole):
            part = dot_nt(rows[0][...], piece[...]).astype(bf16)
            columns_of(outs[0], places_ref[i], piece.shape[0])[...] = part

    (out,) = over_rows(
        name, body, min(256, left.shape[0]), [left], pieces, [(width, bf16)], places=places
    )
    return out


def tile_split(width, count):
    tiles = -(-width // LANES)
    least, extra = divmod(tiles, count)
    sizes = [least + (1 if i < extra else 0) for i in range(count)]
    starts = [sum(sizes[:i]) for i in range(count)]
    return (starts, sizes, max(sizes))


def per_device(
    tokens,
    ln1_gain,
    ln1_bias,
    w_qkv,
    b_qkv,
    w_out,
    b_out,
    ln2_gain,
    ln2_bias,
    w_gate,
    b_gate,
    w_up,
    b_up,
    w_down,
    b_down,
    protein_lengths,
    prefix_lengths,
    out_grad,
):
    nx, nz, ny = (lax.axis_size(axis) for axis in ("x", "z", "y"))
    x, core, z, y = (lax.axis_index(axis) for axis in EVERY)
    sizes_of = (("core", 2), ("x", nx), ("y", ny), ("z", nz))
    own_rows, width = tokens.shape
    weight_rows = w_qkv.shape[0]
    ffn_width = w_gate.shape[1]
    seq_count, team_count = nz * ny, 2 * nz
    count = own_rows * seq_count
    line_rows = nz * own_rows
    own_heads = HEADS // seq_count
    own_width = own_heads * HEAD
    clock = Clock()
    ring = Ring(nz, ny, clock)
    line = Line(nz, clock)
    grid = Grid(nx, ny, clock)
    me = ring.me

    def all_to_all(values, axes):
        return lax.all_to_all(values, axes, split_axis=0, concat_axis=0, tiled=True)

    def other_core(values):
        return lax.ppermute(values, "core", [(0, 1), (1, 0)])

    token_task = Task("tokens", ring.gather(tokens))
    qkv_blocks = (
        w_qkv.reshape(weight_rows, 3, seq_count, own_width)
        .transpose(2, 0, 1, 3)
        .reshape(seq_count, weight_rows, 3 * own_width)
    )
    qkv_moved = all_to_all(qkv_blocks, GROUP)

    starts, sizes, most = tile_split(ffn_width, team_count)
    own_ffn = most * LANES
    padded = (starts[-1] + most) * LANES
    first_tile = jnp.asarray(starts, jnp.int32)[core * nz + z] * LANES

    def ffn_blocks(weight, mask):
        whole = jnp.pad(weight, ((0, 0), (0, padded - ffn_width)))
        pieces = []
        for start, size in zip(starts, sizes):
            piece = whole[:, start * LANES : (start + most) * LANES]
            if mask and size < most:
                piece = jnp.pad(piece[:, : size * LANES], ((0, 0), (0, (most - size) * LANES)))
            pieces.append(piece)
        return jnp.stack(pieces)

    def ffn_bias(bias):
        return cut(jnp.pad(bias, (0, padded - ffn_width)), (first_tile,), (own_ffn,))

    half_places = jnp.stack([lax.rem(x - k + nx, nx) for k in range(nx)])
    places = jnp.concatenate([half_places * 2 + core, half_places * 2 + 1 - core])

    row = lambda values: values.reshape(1, -1)
    token_task.step()
    gate_up_blocks = clock.run(
        lambda gate, up: jnp.concatenate([ffn_blocks(gate, False), ffn_blocks(up, False)], axis=2),
        w_gate,
        w_up,
    )
    token_task.step()
    down_blocks = clock.run(lambda down: ffn_blocks(down, True), w_down)
    qkv_rows = clock(qkv_moved).reshape(seq_count * weight_rows, 3 * own_width)
    from_x = from_axis(qkv_rows, "x", nx)
    out_moved = all_to_all(
        clock.hold(jnp.broadcast_to(w_out[None], (nz, weight_rows, width))), "z"
    )
    token_task.step()

    def tables(lengths, prefixes):
        position, low, high = group_layout(lengths[0], prefixes[0], count)
        return (*rotary_tables(position), low[:, None], high[:, None])

    cosine, sine, low, high = clock.run(tables, protein_lengths, prefix_lengths)
    arrived = [clock(value) for value, _ in from_x]
    qkv_pieces = [qkv_rows, *arrived]
    from_core = [other_core(value) for value in qkv_pieces]
    tokens_all = clock(token_task.finish())
    out_task = Task("w_out", grid.gather(clock(out_moved)))
    gate_up_moved = all_to_all(clock.hold(gate_up_blocks), TEAM)
    qkv_pieces += [clock(value) for value in from_core]
    qkv_bias = cut(b_qkv.reshape(3, width), (0, me * own_width), (3, own_width))

    def first_kernel(rows, whole, places_ref, outs, sums):
        tokens_ref, cos_ref, sin_ref = rows
        gain, bias, qkv_bias, *pieces = whole
        normed_ref, packed_ref = outs
        normed = layer_norm(tokens_ref[...].astype(f32), gain[...], bias[...])
        normed_ref[...] = normed.astype(bf16)
        raw = project_pieces(normed_ref, pieces, places_ref) + qkv_bias[...]
        for i in range(3 * own_heads):
            piece = raw[:, i * HEAD : (i + 1) * HEAD]
            if i < 2 * own_heads:
                piece = rotate(piece, cos_ref[...], sin_ref[...])
            packed_ref[:, i * HEAD : (i + 1) * HEAD] = piece.astype(bf16)

    normed, packed = clock.run(
        lambda tokens_all, *pieces: over_rows(
            "project",
            first_kernel,
            256,
            [tokens_all, cosine, sine],
            [row(ln1_gain), row(ln1_bias), row(qkv_bias), *pieces],
            [(width, bf16), (3 * own_width, bf16)],
            places=places,
        ),
        tokens_all,
        *qkv_pieces,
    )
    head_result, log_sums = clock.run(lambda values: attend_forward(values, low, high), packed)

    head_result = head_result.reshape(nz, ny, own_rows, own_width)
    moved_task = Task("to_y", exchange(head_result, "y", ny, 1, clock))
    moved = moved_task.finish().transpose(0, 2, 1, 3).reshape(line_rows, ny * own_width)
    attended_task = Task("attended", line.gather(clock(moved), 1))
    out_task.step()
    attended_task.step()
    gate_up_moved = clock(gate_up_moved)
    out_pieces = list(clock(*out_task.finish()))
    from_core = [other_core(piece) for piece in out_pieces]
    attended_task.step()
    gate_up_task = Task("gate_up", grid.gather(gate_up_moved))
    down_moved = all_to_all(clock.hold(down_blocks), TEAM)
    inputs_line, out_grad_turned = clock.run(
        lambda values, grads: (
            lax.dynamic_index_in_dim(
                values.reshape(nz, ny, own_rows, width), y, 1, False
            ).reshape(line_rows, width),
            grid.turn(grads),
        ),
        tokens_all,
        out_grad,
    )
    out_pieces = out_pieces + [clock(value) for value in from_core]
    attended = clock(attended_task.finish())
    grad_out_task = Task("out_grad", line.gather(out_grad_turned, 0))

    def second_kernel(rows, whole, places_ref, outs, more):
        tokens_ref, attended_ref = rows
        gain, bias, out_bias, *pieces = whole
        attn = project_pieces(attended_ref, pieces, places_ref) + out_bias[...]
        hidden = tokens_ref[...].astype(f32) + attn
        outs[1][...] = hidden
        (normed_ref,) = more
        normed_ref[...] = layer_norm(hidden, gain[...], bias[...]).astype(bf16)
        part = width // nx
        for k in range(nx):
            place = places_ref[2 * nx + k]
            outs[0][:, k * part : (k + 1) * part] = columns_of(normed_ref, place, part)[...]

    normed_two, hidden_in = clock.run(
        lambda tokens, attended, *pieces: over_rows(
            "second_norm",
            second_kernel,
            min(256, line_rows),
            [tokens, attended],
            [row(ln2_gain), row(ln2_bias), row(b_out), *pieces],
            [(width, bf16), (width, f32)],
            places=jnp.concatenate([places, half_places]),
            scratch=[(width, bf16)],
        ),
        inputs_line,
        attended,
        *out_pieces,
    )
    hidden_own = cut(hidden_in, (z * own_rows, 0), (own_rows, width))
    grad_out_task.step()
    normed_other = other_core(normed_two)
    gate_up_task.step()
    down_moved = clock(down_moved)
    grad_out_task.step()
    gate_up_own = clock(jnp.concatenate(gate_up_task.finish(), axis=0))
    down_task = Task("down", grid.gather(down_moved))
    normed_two = jnp.concatenate([normed_two, clock(normed_other)], axis=0)
    grad_out_line = clock(grad_out_task.finish())[:line_rows]
    grad_out_other = other_core(grad_out_line)

    def first_half(values, weight):
        gate_up = dot_nn(values, weight)
        gate = gate_up[:, :own_ffn] + ffn_bias(b_gate)
        upper = gate_up[:, own_ffn:] + ffn_bias(b_up)
        return gate, upper

    gate, upper = clock.run(first_half, normed_two, gate_up_own)
    down_task.step()
    grad_out_all = clock(jnp.concatenate([grad_out_line, clock(grad_out_other)], axis=0))
    down_own = clock(jnp.concatenate(down_task.finish(), axis=0))

    def first_half_back(grads, weight, gate, upper):
        grad_act = dot_nn(grads, weight)
        act, pull = jax.vjp(geglu, gate, upper)
        return jnp.concatenate([g.astype(bf16) for g in pull(grad_act)], axis=1), act.astype(bf16)

    grad_gate_up, act = clock.run(first_half_back, grad_out_all, down_own, gate, upper)

    def low_nt(left, right):
        return dot_nt(left, right).astype(bf16)

    def low_tn(left, right):
        return dot_tn(left, right).astype(bf16)

    def both_parts(grads, gate_up, act, down):
        return jnp.concatenate([low_nt(grads, gate_up), low_nt(act, down)], axis=1)

    other_parts = other_core(
        clock.run(both_parts, grad_gate_up[line_rows:], gate_up_own, act[line_rows:], down_own)
    )
    own_parts = clock.run(
        both_parts, grad_gate_up[:line_rows], gate_up_own, act[:line_rows], down_own
    )
    parts_task = Task("second_half", line.scatter(clock(add_up(own_parts, [clock(other_parts)]))))
    split = 3 * own_ffn // 2 // LANES * LANES
    first_share = clock.run(low_tn, normed_two, grad_gate_up[:, :split])
    second_share, third_share = clock.run(
        lambda a, b, c, d: (low_tn(a, b[:, split:]), low_tn(c, d)),
        normed_two,
        grad_gate_up,
        grad_out_all,
        act,
    )
    ffn_grad_task = Task(
        "ffn_grad", grid.scatter([first_share], [second_share, third_share], team_count)
    )
    parts_task.step()
    bias_gate_up = clock.run(
        lambda grads: jnp.sum(grads.astype(f32), axis=0), grad_gate_up
    )
    parts_task.step()
    ffn_grad_task.step()
    two_parts = parts_task.finish()

    def second_back_kernel(rows, whole, places_ref, outs, more):
        *sums, _ = more
        more = more[-1:]
        below, above, own, hidden, out_grad_ref = rows
        gain, *pieces = whole
        turned = below[:, :width].astype(f32) + above[:, :width].astype(f32) + own[:, :width]
        (grads_ref,) = more
        part = width // nx
        for k in range(nx):
            columns_of(grads_ref, places_ref[2 * nx + k], part)[...] = turned[:, k * part : (k + 1) * part]
        grads = grads_ref[...]
        unit, inverse = norm_parts(hidden[...])
        cotangent = out_grad_ref[...].astype(f32)
        total = cotangent + layer_norm_back(unit, inverse, gain[...], grads)
        low = total.astype(bf16)
        outs[0][...] = total
        outs[1][...] = low
        for i, piece in enumerate(pieces):
            part = dot_nt(low, piece[...]).astype(bf16)
            columns_of(outs[2], places_ref[i], piece.shape[0])[...] = part
        for ref, values in zip(sums, (grads * unit, grads, low.astype(f32), cotangent)):
            ref[...] += jnp.sum(values, axis=0, keepdims=True)

    grad_hidden, grad_attn, grad_attended, *second_sums = clock.run(
        lambda *values: over_rows(
            "second_norm_back",
            second_back_kernel,
            own_rows,
            values[:5],
            [row(ln2_gain), *values[5:]],
            [(width, f32), (width, bf16), (width, bf16)],
            [width] * 4,
            places=jnp.concatenate([places, half_places]),
            scratch=[(width, f32)],
        ),
        *two_parts,
        hidden_own,
        out_grad,
        *out_pieces,
    )

    grad_heads = all_to_all(
        grad_attended.reshape(own_rows, seq_count, own_width).transpose(1, 0, 2), GROUP
    )
    grad_heads = clock(grad_heads).reshape(count, own_width)
    ffn_share = clock(ffn_grad_task.finish())
    ffn_back = all_to_all(ffn_share, TEAM)
    grad_parts = clock.run(
        lambda *values: attend_backward(*values, low, high, log_sums, cosine, sine),
        packed,
        grad_heads,
    )

    def first_back_kernel(rows, whole, places_ref, outs, more):
        *sums, part_ref = more
        grads, tokens_ref = rows[:3], rows[3]
        unit, _ = norm_parts(tokens_ref[...].astype(f32))
        for i, piece in enumerate(whole):
            part = None
            for j, grad in enumerate(grads):
                term = dot_nt(grad[...], piece[:, j * own_width : (j + 1) * own_width])
                part = term if part is None else part + term
            depth = piece.shape[0]
            columns_of(outs[0], places_ref[i], depth)[...] = part.astype(bf16)
            columns_of(part_ref, places_ref[i], depth)[...] = part
        part = part_ref[...]
        sums[0][...] += jnp.sum(part * unit, axis=0, keepdims=True)
        sums[1][...] += jnp.sum(part, axis=0, keepdims=True)
        for j, grad in enumerate(grads):
            total = jnp.sum(grad[...].astype(f32), axis=0, keepdims=True)
            sums[2][:, j * own_width : (j + 1) * own_width] += total

    normed_part, *first_sums = clock.run(
        lambda *values: over_rows(
            "first_norm_back",
            first_back_kernel,
            256,
            values[:4],
            values[4:],
            [(width, bf16)],
            [width, width, 3 * own_width],
            places=places,
            scratch=[(width, f32)],
        ),
        *grad_parts,
        tokens_all,
        *qkv_pieces,
    )
    one_task = Task("grad_normed", ring.scatter(normed_part))

    def spread(values, start, size):
        return put(jnp.zeros((size,), f32), values, (start,))

    def gather_small(bias_gate_up, *sums):
        bias_qkv = sums[-1][0]
        small = [value[0] for value in sums[:-1]]
        small += [
            spread(bias_qkv[i * own_width : (i + 1) * own_width], me * own_width, width)
            for i in range(3)
        ]
        small += [
            spread(bias_gate_up[:own_ffn], first_tile, padded),
            spread(bias_gate_up[own_ffn:], first_tile, padded),
        ]
        return jnp.concatenate(small)

    small = clock.run(gather_small, bias_gate_up, *second_sums, *first_sums)
    small_task = Task("small", sum_everywhere(small, sizes_of, clock))
    qkv_share = clock.run(
        lambda a, b, c, d: low_tn(a, jnp.concatenate([b, c, d], axis=1)), normed, *grad_parts
    )
    qkv_share = qkv_share.reshape(nx, 2, seq_count * weight_rows, 3 * own_width)
    qkv_core = to_axis(qkv_share, "core", 2, 1)
    ffn_back = clock(ffn_back)
    one_task.step()
    grad_attn_task = Task(
        "grad_attn",
        exchange(grad_attn.reshape(own_rows, nz, width // nz).transpose(1, 0, 2), "z", nz, 0, clock),
    )
    qkv_share = clock(add_up(own_part(qkv_share, "core", 1), [clock(v) for v in qkv_core]))
    qkv_x = to_axis(qkv_share, "x", nx, 0)
    small_task.step()
    one_task.step()
    grad_attn_block = clock(grad_attn_task.finish()).reshape(line_rows, width // nz)
    out_share = clock.run(lambda a, b: low_tn(a[:, :width], b), attended, grad_attn_block)
    out_share = out_share.reshape(nx, 2, nz, ny, weight_rows, width // nz)
    out_core = to_axis(out_share, "core", 2, 1)
    small_task.step()
    qkv_share = clock(add_up(own_part(qkv_share, "x", 0), [clock(v) for v in qkv_x]))
    qkv_back = all_to_all(qkv_share.reshape(seq_count, weight_rows, 3 * own_width), GROUP)
    out_share = clock(add_up(own_part(out_share, "core", 1), [clock(v) for v in out_core]))
    out_x = to_axis(out_share, "x", nx, 0)
    one_task.step()
    small_task.step()
    output = clock.run(
        lambda below, above, own, hidden: (
            grid.turn_back(
                below[:, width:].astype(f32) + above[:, width:].astype(f32) + own[:, width:]
            )
            + hidden
            + b_down
        ).astype(bf16),
        *two_parts,
        hidden_own,
    )
    out_share = clock(add_up(own_part(out_share, "x", 0), [clock(v) for v in out_x]))
    out_y = to_axis(out_share, "y", ny, 1)
    one_parts = one_task.finish()
    small_task.step()
    out_share = clock(add_up(own_part(out_share, "y", 1), [clock(v) for v in out_y]))
    out_back = Task("out_grad", exchange(out_share, "z", nz, 0, clock))

    def last_kernel(rows, whole, places_ref, outs, sums):
        below, above, own, tokens_ref, hidden_grad = rows
        grads = below[...].astype(f32) + above[...].astype(f32) + own[...]
        unit, inverse = norm_parts(tokens_ref[...].astype(f32))
        total = hidden_grad[...] + layer_norm_back(unit, inverse, whole[0][...], grads)
        outs[0][...] = total.astype(bf16)

    tokens_grad = clock.run(
        lambda *values: over_rows(
            "first_norm_tokens",
            last_kernel,
            own_rows,
            values,
            [row(ln1_gain)],
            [(width, bf16)],
        )[0],
        *one_parts,
        tokens,
        grad_hidden,
    )
    small = small_task.finish()
    out_back = out_back.finish()

    def ffn_rows(moved, begin):
        pieces = [moved[i, :, begin : begin + sizes[i] * LANES] for i in range(team_count)]
        return jnp.concatenate(pieces, axis=1)[:, :ffn_width].astype(f32)

    out_weight_grad = (
        out_back.transpose(1, 0, 2).reshape(weight_rows, width).astype(f32)
    )
    qkv_weight_grad = (
        clock(qkv_back)
        .reshape(seq_count, weight_rows, 3, own_width)
        .transpose(1, 2, 0, 3)
        .reshape(weight_rows, 3 * width)
        .astype(f32)
    )
    gain_two, bias_two, b_out_grad, b_down_grad, gain_one, bias_one = (
        small[i * width : (i + 1) * width] for i in range(6)
    )
    b_qkv_grad = small[6 * width : 9 * width]
    b_gate_grad = small[9 * width : 9 * width + ffn_width]
    b_up_grad = small[9 * width + padded : 9 * width + padded + ffn_width]
    return (
        output,
        tokens_grad,
        gain_one,
        bias_one,
        qkv_weight_grad,
        b_qkv_grad,
        out_weight_grad,
        b_out_grad,
        gain_two,
        bias_two,
        ffn_rows(ffn_back, 0),
        b_gate_grad,
        ffn_rows(ffn_back, own_ffn),
        b_up_grad,
        ffn_rows(ffn_back, 2 * own_ffn),
        b_down_grad,
    )


def solution(mesh):
    nx, seq_count = mesh.shape["batch"] // 2, mesh.shape["seq"]
    nz = 4 if seq_count % 4 == 0 else seq_count
    grid = Mesh(mesh.devices.reshape(nx, 2, nz, seq_count // nz), EVERY)
    rows = P(EVERY, None)
    lengths = P(("x", "core"), None)
    in_specs = (
        rows, P(), P(), rows, P(), rows, P(), P(), P(), rows, P(), rows, P(), rows, P(),
        lengths, lengths, rows,
    )
    out_specs = (
        rows, rows, P(), P(), rows, P(), rows, P(), P(), P(), rows, P(), rows, P(), rows, P(),
    )
    return jax.shard_map(
        per_device, mesh=grid, in_specs=in_specs, out_specs=out_specs, check_vma=False
    )
```

time: 857 us -> 654 us (0.76)
  waiting for transfers between devices: 301 us -> 179 us
  local copies, waits for them, and re-layouts: 227 us -> 118 us
  Pallas kernels: 0 us -> 72.6 us
  matrix products: 95.4 us -> 50 us
    ppermute x89 -> x77, waiting for transfers between devices: 289 us -> 166 us  [the longest x16 41.7 us: send(): lax.ppermute(values, GROUP, self.forward if forward else self.backward)]
    pallas_call x0 -> x7, Pallas kernels: none -> 72.6 us  [the longest x5 49.7 us: over_rows(): pl.pallas_call(kernel, grid_spec=pltpu.PrefetchScalarGridSpec(num_scalar_...]
    unnamed x163 -> x179, local copies, waits for them, and re-layouts: 76.6 us -> 24.4 us
    dynamic_update_slice x62 -> x28, local copies, waits for them, and re-layouts: 66.6 us -> 35.2 us  [put(): return lax.dynamic_update_slice(total, piece, [jnp.int32(i) for i in where])]
    dot_general x4 -> x2, matrix products: 40.4 us -> 13.3 us  [dot_nn(): lax.dot_general(left, right, (((1,), (0,)), ((), ())), preferred_element_...]
    ppermute x89 -> x77, starting transfers between devices: 133 us -> 108 us  [the longest x9 31.6 us: up(): return lax.ppermute(values, 'z', [(i, i + 1) for i in range(low, high)])]
    all_to_all x4 -> x7, starting transfers between devices: 18.9 us -> 37.9 us  [all_to_all(): return lax.all_to_all(values, axes, split_axis=0, concat_axis=0, tiled=True)]
    dynamic_slice x8 -> x10, local copies, waits for them, and re-layouts: 26.7 us -> 8.56 us  [the longest x8 4.79 us: cut(): return lax.dynamic_slice(values, [jnp.int32(i) for i in where], sizes)]
  transfers between devices with their start and end apart: 93 -> 84, of which waited for: 44 -> 33; matrix products, arithmetic and copies ran while one was open for 40% -> 31% of each run, Pallas kernels for 0% -> 11%
where the time goes in v2:
time: 654 us; the launch traced here: 643 us
  waiting for transfers between devices  179 us (27%)
  starting transfers between devices  146 us (22%)
  local copies, waits for them, and re-layouts  118 us (18%)
  other arithmetic  74.5 us (11%)
  Pallas kernels  72.6 us (11%)
  matrix products  50 us (8%)
    pallas_call x5, Pallas kernels, over_rows(): pl.pallas_call(kernel, grid_spec=pltpu.PrefetchScalarGridSpec(num_scalar_...  49.7 us
    ppermute x16, waiting for transfers between devices, send(): lax.ppermute(values, GROUP, self.forward if forward else self.backward)  41.7 us
    all_to_all x7, starting transfers between devices, all_to_all(): return lax.all_to_all(values, axes, split_axis=0, concat_axis=0, tiled=True)  37.9 us
    ppermute x15, waiting for transfers between devices, to_axis(): lax.ppermute(lax.dynamic_index_in_dim(values, lax.rem(me + step, count),...  37.9 us
    dynamic_update_slice x28, local copies, waits for them, and re-layouts, put(): return lax.dynamic_update_slice(total, piece, [jnp.int32(i) for i in where])  35.2 us
    ppermute x9, starting transfers between devices, up(): return lax.ppermute(values, 'z', [(i, i + 1) for i in range(low, high)])  31.6 us
    ppermute x9, waiting for transfers between devices, down(): return lax.ppermute(values, 'z', [(i + 1, i) for i in range(low, high)])  28.7 us
    unnamed x179, local copies, waits for them, and re-layouts  24.4 us
  transfers between devices with their start and end apart: 84, of which 33 were waited for; matrix products, arithmetic and copies ran while one was open for 31% of the time, Pallas kernels for 11%

profile of v2, /device:TPU:0, one launch (start us, length us, event | category | flops | bytes accessed | tf_op | source)
XLA Modules:
  0.0 643.5 jit_solution(6804216428134671202)
XLA Ops:
  7.1 6.3 all-to-all-start
  24.0 17.3 %collective-permute-done.3 = bf16[128,2048]{1,0:T(8,128)(2,1)} collective-permute-done((bf16[128,2048]{1,0:T(8,128)(2,1)S(1)}, bf16[128,2048]{1,0:T(8,128)(2,1)}, u32[]{:S(2)}, u32[]{:S(2)}) %collective-permute-start.3) | collective-permute-done | bytes 524320 | tf_op jit(solution)/shard_map/tokens/ppermute | solution.py:184
  41.3 5.8 collective-permute-start.4
  57.5 6.0 collective-permute-done.5
  84.0 7.9 %all-to-all-start.2 = ((bf16[8,64,1536]{2,1,0:T(8,128)(2,1)}), bf16[8,64,1536]{2,1,0:T(8,128)(2,1)}, u32[]{:S(2)}, u32[]{:S(2)}) async-start(bf16[8,64,1536]{2,1,0:T(8,128)(2,1)} %pad_maximum_fusion.7), calls=%async_computation.2 | async-start | bytes 3145728 | tf_op jit(solution)/shard_map/all_to_all | solution.py:676
  98.9 12.0 %project.1 = (bf16[1024,2048]{1,0:T(8,128)(2,1)}, bf16[1024,768]{1,0:T(8,128)(2,1)}) custom-call(s32[4]{0:T(128)} %pad_add_fusion.places_ref, bf16[1024,2048]{1,0:T(8,128)(2,1)} %constant_dynamic-update-slice_fusion.81.refs_0_.refs_3_, f32[1024,128]{1,0:T(8,128)} %pad_maximum_fusion.8.refs_1_.cos_ref.all_cos_ref, ...), custom_call_target="tpu_custom_call" | custom-call | tf_op jit(solution)/shard_map/project/pallas_call | solution.py:551
  110.9 9.7 %attend_forward.1 = (bf16[1024,256]{1,0:T(8,128)(2,1)}, f32[2,1024,1]{2,1,0:T(8,128)}) custom-call(bf16[1024,768]{1,0:T(8,128)(2,1)} %get-tuple-element.474.q_ref.k_ref.v_ref, bf16[1024,768]{1,0:T(8,128)(2,1)} %get-tuple-element.474.q_ref.k_ref.v_ref, bf16[1024,768]{1,0:T(8,128)(2,1)} %get-tuple-element.474.q_ref.k_ref.v_ref, s32[1024,1]{1,0:T(8,128)} %copy.98.low_ref, ...), custom_call_target="tpu_custom_call" | custom-call | tf_op jit(solution)/shard_map/attend_forward/pallas_call | solution.py:492
  122.2 7.6 %collective-permute-done.11 = bf16[4,128,256]{2,1,0:T(8,128)(2,1)S(1)} collective-permute-done((bf16[4,128,256]{2,1,0:T(8,128)(2,1)S(1)}, bf16[4,128,256]{2,1,0:T(8,128)(2,1)S(1)}, u32[]{:S(2)}, u32[]{:S(2)}) %collective-permute-start.11) | collective-permute-done | bytes 262176 | tf_op jit(solution)/shard_map/to_y/ppermute | solution.py:303
  132.1 5.5 collective-permute-start.12
  142.2 3.6 collective-permute-done.13
  149.4 4.0 collective-permute-done.18
  155.0 3.7 fusion.15
  169.7 5.5 collective-permute-done.17
  177.8 7.1 %all-to-all-start.3 = ((bf16[8,64,768]{2,1,0:T(8,128)(2,1)}), bf16[8,64,768]{2,1,0:T(8,128)(2,1)}, u32[]{:S(2)}, u32[]{:S(2)}) async-start(bf16[8,64,768]{2,1,0:T(8,128)(2,1)} %copy-done.39), calls=%async_computation.3 | async-start | bytes 1572864 | tf_op jit(solution)/shard_map/all_to_all | solution.py:676
  193.4 18.6 %collective-permute-done.21 = bf16[512,512]{1,0:T(8,128)(2,1)S(1)} collective-permute-done((bf16[512,512]{1,0:T(8,128)(2,1)}, bf16[512,512]{1,0:T(8,128)(2,1)S(1)}, u32[]{:S(2)}, u32[]{:S(2)}) %collective-permute-start.21) | collective-permute-done | bytes 524320 | tf_op jit(solution)/shard_map/attended/ppermute | solution.py:243
  215.0 5.4 collective-permute-start.24
  220.9 12.0 %second_norm.1 = (bf16[512,2048]{1,0:T(8,128)(2,1)}, f32[512,2048]{1,0:T(8,128)}) custom-call(s32[6]{0:T(128)} %pad_add_fusion.1.places_ref, bf16[512,2048]{1,0:T(8,128)(2,1)} %bitcast.325, bf16[512,2560]{1,0:T(8,128)(2,1)} %constant_dynamic-update-slice_fusion.74.refs_1_, f32[1,2048]{1,0:T(1,128)} %bitcast.364, f32[1,2048]{1,0:T(1,128)} %bitcast.375, ...), custom_call_target="tpu_custom_call" | custom-call | tf_op jit(solution)/shard_map/second_norm/pallas_call | solution.py:551
  280.6 6.6 %fusion.56 = f32[1024,1536]{1,0:T(8,128)S(1)} fusion(bf16[1024,2048]{1,0:T(8,128)(2,1)S(1)} %constant_dynamic-update-slice_fusion.26, bf16[2048,1536]{1,0:T(8,128)(2,1)S(1)} %pad_maximum_fusion), kind=kOutput, calls=%fused_computation.302 | convolution fusion | flops 6442450944 | bytes 16777216 | tf_op jit(solution)/shard_map/dot_general | solution.py:94
  295.6 3.9 collective-permute-done.38
  301.9 6.6 %multiply_convert_fusion = (bf16[1024,768]{1,0:T(8,128)(2,1)S(1)}, bf16[1024,768]{1,0:T(8,128)(2,1)S(1)}, bf16[1024,768]{1,0:T(8,128)(2,1)S(1)}) fusion(f32[1024,768]{1,0:T(8,128)S(1)} %get-tuple-element.398, f32[1024,768]{1,0:T(8,128)S(1)} %get-tuple-element.395, bf16[1024,2048]{1,0:T(8,128)(2,1)S(1)} %pad_maximum_fusion.1, ...), kind=kOutput, calls=%fused_computation.45 | convolution fusion | flops 3244818432 | bytes 18350080 | tf_op jit(solution)/shard_map/dot_general | solution.py:94
  312.4 3.7 convolution_convert_fusion.7
  320.3 4.1 convolution_convert_fusion.4
  324.7 3.7 convolution_convert_fusion.5
  328.7 3.7 add_convert_fusion
  334.1 4.6 collective-permute-start.41
  339.5 6.1 convolution_convert_fusion
  345.6 5.0 convolution_convert_fusion.2
  365.5 5.1 collective-permute-start.43
  376.1 16.1 %collective-permute-done.43 = bf16[128,4096]{1,0:T(8,128)(2,1)} collective-permute-done((bf16[128,4096]{1,0:T(8,128)(2,1)}, bf16[128,4096]{1,0:T(8,128)(2,1)}, u32[]{:S(2)}, u32[]{:S(2)}) %collective-permute-start.43) | collective-permute-done | bytes 1048608 | tf_op jit(solution)/shard_map/second_half/ppermute | solution.py:240
  395.8 5.5 collective-permute-start.45
  401.3 9.9 %collective-permute-done.47 = bf16[8,2,64,1152]{3,2,0,1:T(8,128)(2,1)} collective-permute-done((bf16[8,2,64,1152]{3,2,0,1:T(8,128)(2,1)}, bf16[8,2,64,1152]{3,2,0,1:T(8,128)(2,1)}, u32[]{:S(2)}, u32[]{:S(2)}) %collective-permute-start.47) | collective-permute-done | bytes 2359328 | tf_op jit(solution)/shard_map/ffn_grad/ppermute | solution.py:391
  413.7 10.8 %collective-permute-done.49 = bf16[2,8,64,768]{3,2,1,0:T(8,128)(2,1)S(1)} collective-permute-done((bf16[2,8,64,768]{3,2,1,0:T(8,128)(2,1)S(1)}, bf16[2,8,64,768]{3,2,1,0:T(8,128)(2,1)S(1)}, u32[]{:S(2)}, u32[]{:S(2)}) %collective-permute-start.49) | collective-permute-done | bytes 1572896 | tf_op jit(solution)/shard_map/ffn_grad/ppermute | solution.py:303
  431.9 10.5 %second_norm_back.1 = (f32[128,2048]{1,0:T(8,128)}, bf16[128,2048]{1,0:T(8,128)(2,1)}, bf16[128,2048]{1,0:T(8,128)(2,1)}, f32[1,2048]{1,0:T(1,128)}, f32[1,2048]...) custom-call(s32[6]{0:T(128)} %pad_add_fusion.1.places_ref, bf16[128,4096]{1,0:T(8,128)(2,1)} %copy-done.26, ...), custom_call_target="tpu_custom_call" | custom-call | tf_op jit(solution)/shard_map/second_norm_back/pallas_call | solution.py:551
  444.3 4.6 all-to-all-start.4
  453.1 8.9 %all-to-all-done.4 = bf16[8,128,256]{2,1,0:T(8,128)(2,1)} async-done(((bf16[8,128,256]{2,1,0:T(8,128)(2,1)}), bf16[8,128,256]{2,1,0:T(8,128)(2,1)}, u32[]{:S(2)}, u32[]{:S(2)}) %all-to-all-start.4) | async-done | bytes 524320 | tf_op jit(solution)/shard_map/all_to_all | solution.py:676
  464.8 10.3 %collective-permute-done.52 = bf16[8,64,768]{2,1,0:T(8,128)(2,1)} collective-permute-done((bf16[8,64,768]{2,1,0:T(8,128)(2,1)}, bf16[8,64,768]{2,1,0:T(8,128)(2,1)}, u32[]{:S(2)}, u32[]{:S(2)}) %collective-permute-start.52) | collective-permute-done | bytes 786464 | tf_op jit(solution)/shard_map/ffn_grad/ppermute | solution.py:391
  478.0 4.9 all-to-all-start.5
  486.4 3.8 collective-permute-start.58
  490.2 13.3 %attend_backward.1 = (bf16[1024,256]{1,0:T(8,128)(2,1)}, bf16[1024,256]{1,0:T(8,128)(2,1)}, bf16[1024,256]{1,0:T(8,128)(2,1)}) custom-call(bf16[1024,768]{1,0:T(8,128)(2,1)} %get-tuple-element.474.q_ref.k_ref.v_ref, bf16[1024,768]{1,0:T(8,128)(2,1)} %get-tuple-element.474.q_ref.k_ref.v_ref, bf16[1024,768]{1,0:T(8,128)(2,1)} %get-tuple-element.474.q_ref.k_ref.v_ref, ...), custom_call_target="tpu_custom_call" | custom-call | tf_op jit(solution)/shard_map/attend_backward/pallas_call | solution.py:514
  503.5 11.5 %first_norm_back.1 = (bf16[1024,2048]{1,0:T(8,128)(2,1)}, f32[1,2048]{1,0:T(1,128)}, f32[1,2048]{1,0:T(1,128)}, f32[1,768]{1,0:T(1,128)}) custom-call(s32[4]{0:T(128)} %pad_add_fusion.places_ref, bf16[1024,256]{1,0:T(8,128)(2,1)} %get-tuple-element.512.refs_0_, bf16[1024,256]{1,0:T(8,128)(2,1)} %get-tuple-element.513.refs_1_, ...), custom_call_target="tpu_custom_call" | custom-call | tf_op jit(solution)/shard_map/first_norm_back/pallas_call | solution.py:551
  525.1 6.0 convolution_convert_fusion.1
  535.6 4.4 all-to-all-done.5
  540.0 8.8 %collective-permute-done.56 = bf16[64,2048]{1,0:T(8,128)(2,1)S(1)} collective-permute-done((bf16[64,2048]{1,0:T(8,128)(2,1)}, bf16[64,2048]{1,0:T(8,128)(2,1)S(1)}, u32[]{:S(2)}, u32[]{:S(2)}) %collective-permute-start.56) | collective-permute-done | bytes 262176 | tf_op jit(solution)/shard_map/grad_normed/ppermute | solution.py:184
  581.1 8.4 %collective-permute-done.67 = bf16[512,768]{1,0:T(8,128)(2,1)S(1)} collective-permute-done((bf16[512,768]{1,0:T(8,128)(2,1)S(1)}, bf16[512,768]{1,0:T(8,128)(2,1)S(1)}, u32[]{:S(2)}, u32[]{:S(2)}) %collective-permute-start.67) | collective-permute-done | bytes 786464 | tf_op jit(solution)/shard_map/ppermute | solution.py:303
  590.6 3.5 all-to-all-start.6
  604.9 8.5 %collective-permute-done.70 = bf16[4,2,64,512]{3,2,1,0:T(8,128)(2,1)S(1)} collective-permute-done((bf16[4,2,64,512]{3,2,1,0:T(8,128)(2,1)S(1)}, bf16[4,2,64,512]{3,2,1,0:T(8,128)(2,1)S(1)}, u32[]{:S(2)}, u32[]{:S(2)}) %collective-permute-start.70) | collective-permute-done | bytes 524320 | tf_op jit(solution)/shard_map/ppermute | solution.py:303
  615.2 7.9 %collective-permute-done.69.refs_1_ = bf16[128,2048]{1,0:T(8,128)(2,1)S(1)} collective-permute-done((bf16[128,2048]{1,0:T(8,128)(2,1)S(1)}, bf16[128,2048]{1,0:T(8,128)(2,1)S(1)}, u32[]{:S(2)}, u32[]{:S(2)}) %collective-permute-start.69) | collective-permute-done | bytes 524320 | tf_op jit(solution)/shard_map/grad_normed/ppermute | solution.py:184
  625.9 3.6 first_norm_tokens.1
  (480 shorter events, 287.8 us)
Async XLA Ops:
  7.1 44.3 %all-to-all-start = ((bf16[8,64,768]{2,1,0:T(8,128)(2,1)}), bf16[8,64,768]{2,1,0:T(8,128)(2,1)S(1)}, u32[]{:S(2)}, u32[]{:S(2)}) async-start(bf16[8,64,768]{2,1,0:T(8,128)(2,1)} %reshape.212), calls=%async_computation | async-start | bytes 1572864 | tf_op jit(solution)/shard_map/all_to_all | solution.py:676
  18.8 22.5 %collective-permute-start.2 = (bf16[128,2048]{1,0:T(8,128)(2,1)S(1)}, bf16[128,2048]{1,0:T(8,128)(2,1)}, u32[]{:S(2)}, u32[]{:S(2)}) collective-permute-start(bf16[128,2048]{1,0:T(8,128)(2,1)S(1)} %collective-permute-done), channel_id=1, source_target_pairs={{0,2},{2,4},{4,6},{6,7},{7,5},{5,3},{3,1},{1,0},{8,10},{10,12},{12... | collective-permute-start | bytes 1572872 | tf_op jit(solution)/shard_map/tokens/ppermute | solution.py:184
  20.4 20.9 %collective-permute-start.3 = (bf16[128,2048]{1,0:T(8,128)(2,1)S(1)}, bf16[128,2048]{1,0:T(8,128)(2,1)}, u32[]{:S(2)}, u32[]{:S(2)}) collective-permute-start(bf16[128,2048]{1,0:T(8,128)(2,1)S(1)} %collective-permute-done.1), channel_id=1, source_target_pairs={{2,0},{4,2},{6,4},{7,6},{5,7},{3,5},{1,3},{0,1},{10,8},{12,10},{14... | collective-permute-start | bytes 1572872 | tf_op jit(solution)/shard_map/tokens/ppermute | solution.py:184
  41.3 22.3 %collective-permute-start.4 = (bf16[128,2048]{1,0:T(8,128)(2,1)}, bf16[128,2048]{1,0:T(8,128)(2,1)}, u32[]{:S(2)}, u32[]{:S(2)}) collective-permute-start(bf16[128,2048]{1,0:T(8,128)(2,1)} %collective-permute-done.2), channel_id=1, source_target_pairs={{0,2},{2,4},{4,6},{6,7},{7,5},{5,3},{3,1},{1,0},{8,10},{10,12},{12... | collective-permute-start | bytes 1572872 | tf_op jit(solution)/shard_map/tokens/ppermute | solution.py:184
  51.4 30.2 %collective-permute-start.8 = (bf16[512,768]{1,0:T(8,128)(2,1)S(1)}, bf16[512,768]{1,0:T(8,128)(2,1)S(1)}, u32[]{:S(2)}, u32[]{:S(2)}) collective-permute-start(bf16[512,768]{1,0:T(8,128)(2,1)S(1)} %bitcast.326), channel_id=1, source_target_pairs={{0,16},{16,0},{1,17},{17,1},{2,18},{18,2},{3,19},{19,3},{4,20},{20... | collective-permute-start | bytes 2359304 | tf_op jit(solution)/shard_map/ppermute | solution.py:295
  54.0 30.0 %all-to-all-start.1 = ((bf16[4,64,2048]{2,1,0:T(8,128)(2,1)}), bf16[4,64,2048]{2,1,0:T(8,128)(2,1)S(1)}, u32[]{:S(2)}, u32[]{:S(2)}) async-start(bf16[4,64,2048]{2,1,0:T(8,128)(2,1)} %broadcast_in_dim.10), calls=%async_computation.1 | async-start | bytes 2097152 | tf_op jit(solution)/shard_map/all_to_all | solution.py:676
  84.0 65.4 %all-to-all-start.2 = ((bf16[8,64,1536]{2,1,0:T(8,128)(2,1)}), bf16[8,64,1536]{2,1,0:T(8,128)(2,1)}, u32[]{:S(2)}, u32[]{:S(2)}) async-start(bf16[8,64,1536]{2,1,0:T(8,128)(2,1)} %pad_maximum_fusion.7), calls=%async_computation.2 | async-start | bytes 3145728 | tf_op jit(solution)/shard_map/all_to_all | solution.py:676
  92.6 45.1 %collective-permute-start.15 = (bf16[4,64,2048]{2,1,0:T(8,128)(2,1)S(1)}, bf16[4,64,2048]{2,1,0:T(8,128)(2,1)}, u32[]{:S(2)}, u32[]{:S(2)}) collective-permute-start(bf16[4,64,2048]{2,1,0:T(8,128)(2,1)S(1)} %all-to-all-done.1), channel_id=1, source_target_pairs={{0,1},{1,0},{2,3},{3,2},{4,5},{5,4},{6,7},{7,6},{8,9},{9,8},{10,11... | collective-permute-start | bytes 3145736 | tf_op jit(solution)/shard_map/w_out/ppermute | solution.py:295
  94.2 43.4 %collective-permute-start.14 = (bf16[4,64,2048]{2,1,0:T(8,128)(2,1)S(1)}, bf16[4,64,2048]{2,1,0:T(8,128)(2,1)}, u32[]{:S(2)}, u32[]{:S(2)}) collective-permute-start(bf16[4,64,2048]{2,1,0:T(8,128)(2,1)S(1)} %all-to-all-done.1), channel_id=1, source_target_pairs={{0,16},{16,0},{1,17},{17,1},{2,18},{18,2},{3,19},{19,3},{4,20},{20... | collective-permute-start | bytes 3145736 | tf_op jit(solution)/shard_map/w_out/ppermute | solution.py:295
  158.7 26.4 %collective-permute-start.23 = (bf16[512,2048]{1,0:T(8,128)(2,1)S(1)}, bf16[512,2048]{1,0:T(8,128)(2,1)}, u32[]{:S(2)}, u32[]{:S(2)}) collective-permute-start(bf16[512,2048]{1,0:T(8,128)(2,1)S(1)} %bitcast.317), channel_id=1, source_target_pairs={{0,8},{8,0},{1,9},{9,1},{2,10},{10,2},{3,11},{11,3},{4,12},{12,4},... | collective-permute-start | bytes 6291464 | tf_op jit(solution)/shard_map/ppermute | solution.py:679
  158.7 34.7 %collective-permute-start.22 = (bf16[512,2048]{1,0:T(8,128)(2,1)}, bf16[512,2048]{1,0:T(8,128)(2,1)}, u32[]{:S(2)}, u32[]{:S(2)}) collective-permute-start(bf16[512,2048]{1,0:T(8,128)(2,1)} %bitcast.47.refs_6_.refs_7_), channel_id=1, source_target_pairs={{0,8},{8,0},{1,9},{9,1},{2,10},{10,2},{3,11},{11,3},{4,12},{12,4},... | collective-permute-start | bytes 6291464 | tf_op jit(solution)/shard_map/ppermute | solution.py:679
  175.2 36.8 %collective-permute-start.20 = (bf16[512,512]{1,0:T(8,128)(2,1)}, bf16[512,512]{1,0:T(8,128)(2,1)S(1)}, u32[]{:S(2)}, u32[]{:S(2)}) collective-permute-start(bf16[512,512]{1,0:T(8,128)(2,1)} %collective-permute-done.16), channel_id=1, source_target_pairs={{4,6},{5,7},{12,14},{13,15},{20,22},{21,23},{28,30},{29,31}} | collective-permute-start | bytes 1572872 | tf_op jit(solution)/shard_map/attended/ppermute | solution.py:240
  175.9 62.7 %collective-permute-start.29 = (bf16[8,64,1536]{2,1,0:T(8,128)(2,1)}, bf16[8,64,1536]{2,1,0:T(8,128)(2,1)}, u32[]{:S(2)}, u32[]{:S(2)}) collective-permute-start(bf16[8,64,1536]{2,1,0:T(8,128)(2,1)} %all-to-all-done.2), channel_id=1, source_target_pairs={{0,1},{1,0},{2,3},{3,2},{4,5},{5,4},{6,7},{7,6},{8,9},{9,8},{10,11... | collective-permute-start | bytes 4718600 | tf_op jit(solution)/shard_map/gate_up/ppermute | solution.py:295
  177.2 61.4 %collective-permute-start.28 = (bf16[8,64,1536]{2,1,0:T(8,128)(2,1)}, bf16[8,64,1536]{2,1,0:T(8,128)(2,1)}, u32[]{:S(2)}, u32[]{:S(2)}) collective-permute-start(bf16[8,64,1536]{2,1,0:T(8,128)(2,1)} %all-to-all-done.2), channel_id=1, source_target_pairs={{0,16},{16,0},{1,17},{17,1},{2,18},{18,2},{3,19},{19,3},{4,20},{20... | collective-permute-start | bytes 4718600 | tf_op jit(solution)/shard_map/gate_up/ppermute | solution.py:295
  177.8 74.5 %all-to-all-start.3 = ((bf16[8,64,768]{2,1,0:T(8,128)(2,1)}), bf16[8,64,768]{2,1,0:T(8,128)(2,1)}, u32[]{:S(2)}, u32[]{:S(2)}) async-start(bf16[8,64,768]{2,1,0:T(8,128)(2,1)} %copy-done.39), calls=%async_computation.3 | async-start | bytes 1572864 | tf_op jit(solution)/shard_map/all_to_all | solution.py:676
  185.1 26.9 %collective-permute-start.21 = (bf16[512,512]{1,0:T(8,128)(2,1)}, bf16[512,512]{1,0:T(8,128)(2,1)S(1)}, u32[]{:S(2)}, u32[]{:S(2)}) collective-permute-start(bf16[512,512]{1,0:T(8,128)(2,1)} %collective-permute-done.17), channel_id=1, source_target_pairs={{2,0},{3,1},{10,8},{11,9},{18,16},{19,17},{26,24},{27,25}} | collective-permute-start | bytes 1572872 | tf_op jit(solution)/shard_map/attended/ppermute | solution.py:243
  213.7 23.4 %collective-permute-start.25 = (bf16[128,2048]{1,0:T(8,128)(2,1)S(1)}, bf16[128,2048]{1,0:T(8,128)(2,1)}, u32[]{:S(2)}, u32[]{:S(2)}) collective-permute-start(bf16[128,2048]{1,0:T(8,128)(2,1)S(1)} %pad_maximum_fusion.10), channel_id=1, source_target_pairs={{2,0},{4,2},{6,4},{3,1},{5,3},{7,5},{10,8},{12,10},{14,12},{11,9},... | collective-permute-start | bytes 1572872 | tf_op jit(solution)/shard_map/out_grad/ppermute | solution.py:243
  215.0 22.2 %collective-permute-start.24 = (bf16[128,2048]{1,0:T(8,128)(2,1)S(1)}, bf16[128,2048]{1,0:T(8,128)(2,1)}, u32[]{:S(2)}, u32[]{:S(2)}) collective-permute-start(bf16[128,2048]{1,0:T(8,128)(2,1)S(1)} %pad_maximum_fusion.10), channel_id=1, source_target_pairs={{0,2},{2,4},{4,6},{1,3},{3,5},{5,7},{8,10},{10,12},{12,14},{9,11},... | collective-permute-start | bytes 1572872 | tf_op jit(solution)/shard_map/out_grad/ppermute | solution.py:240
  232.9 40.0 %collective-permute-start.32 = (bf16[512,2048]{1,0:T(8,128)(2,1)}, bf16[512,2048]{1,0:T(8,128)(2,1)}, u32[]{:S(2)}, u32[]{:S(2)}) collective-permute-start(bf16[512,2048]{1,0:T(8,128)(2,1)} %get-tuple-element.366), channel_id=1, source_target_pairs={{0,8},{8,0},{1,9},{9,1},{2,10},{10,2},{3,11},{11,3},{4,12},{12,4},... | collective-permute-start | bytes 6291464 | tf_op jit(solution)/shard_map/ppermute | solution.py:679
  237.1 18.0 %collective-permute-start.26 = (bf16[128,2048]{1,0:T(8,128)(2,1)}, bf16[128,2048]{1,0:T(8,128)(2,1)}, u32[]{:S(2)}, u32[]{:S(2)}) collective-permute-start(bf16[128,2048]{1,0:T(8,128)(2,1)} %collective-permute-done.24), channel_id=1, source_target_pairs={{2,4},{4,6},{3,5},{5,7},{10,12},{12,14},{11,13},{13,15},{18,20},{2... | collective-permute-start | bytes 1572872 | tf_op jit(solution)/shard_map/out_grad/ppermute | solution.py:240
  244.0 20.3 %collective-permute-start.33 = (bf16[8,64,768]{2,1,0:T(8,128)(2,1)}, bf16[8,64,768]{2,1,0:T(8,128)(2,1)}, u32[]{:S(2)}, u32[]{:S(2)}) collective-permute-start(bf16[8,64,768]{2,1,0:T(8,128)(2,1)} %slice.346), channel_id=1, source_target_pairs={{0,1},{1,0},{2,3},{3,2},{4,5},{5,4},{6,7},{7,6},{8,9},{9,8},{10,11... | collective-permute-start | bytes 2359304 | tf_op jit(solution)/shard_map/gate_up/ppermute | solution.py:295
  245.4 20.0 %collective-permute-start.34 = (bf16[8,64,768]{2,1,0:T(8,128)(2,1)}, bf16[8,64,768]{2,1,0:T(8,128)(2,1)}, u32[]{:S(2)}, u32[]{:S(2)}) collective-permute-start(bf16[8,64,768]{2,1,0:T(8,128)(2,1)} %slice.347), channel_id=1, source_target_pairs={{0,16},{16,0},{1,17},{17,1},{2,18},{18,2},{3,19},{19,3},{4,20},{20... | collective-permute-start | bytes 2359304 | tf_op jit(solution)/shard_map/gate_up/ppermute | solution.py:295
  255.1 17.8 %collective-permute-start.31 = (bf16[128,2048]{1,0:T(8,128)(2,1)}, bf16[128,2048]{1,0:T(8,128)(2,1)}, u32[]{:S(2)}, u32[]{:S(2)}) collective-permute-start(bf16[128,2048]{1,0:T(8,128)(2,1)} %collective-permute-done.27), channel_id=1, source_target_pairs={{2,0},{3,1},{10,8},{11,9},{18,16},{19,17},{26,24},{27,25}} | collective-permute-start | bytes 1572872 | tf_op jit(solution)/shard_map/out_grad/ppermute | solution.py:243
  270.6 19.1 %collective-permute-start.37 = (bf16[8,64,768]{2,1,0:T(8,128)(2,1)}, bf16[8,64,768]{2,1,0:T(8,128)(2,1)S(1)}, u32[]{:S(2)}, u32[]{:S(2)}) collective-permute-start(bf16[8,64,768]{2,1,0:T(8,128)(2,1)} %all-to-all-done.3), channel_id=1, source_target_pairs={{0,1},{1,0},{2,3},{3,2},{4,5},{5,4},{6,7},{7,6},{8,9},{9,8},{10,11... | collective-permute-start | bytes 2359304 | tf_op jit(solution)/shard_map/down/ppermute | solution.py:295
  271.4 18.8 %collective-permute-start.36 = (bf16[8,64,768]{2,1,0:T(8,128)(2,1)}, bf16[8,64,768]{2,1,0:T(8,128)(2,1)S(1)}, u32[]{:S(2)}, u32[]{:S(2)}) collective-permute-start(bf16[8,64,768]{2,1,0:T(8,128)(2,1)} %all-to-all-done.3), channel_id=1, source_target_pairs={{0,16},{16,0},{1,17},{17,1},{2,18},{18,2},{3,19},{19,3},{4,20},{20... | collective-permute-start | bytes 2359304 | tf_op jit(solution)/shard_map/down/ppermute | solution.py:295
  334.1 27.6 %collective-permute-start.41 = (bf16[128,4096]{1,0:T(8,128)(2,1)S(1)}, bf16[128,4096]{1,0:T(8,128)(2,1)S(1)}, u32[]{:S(2)}, u32[]{:S(2)}) collective-permute-start(bf16[128,4096]{1,0:T(8,128)(2,1)S(1)} %get-tuple-element.414), channel_id=1, source_target_pairs={{0,2},{1,3},{8,10},{9,11},{16,18},{17,19},{24,26},{25,27}} | collective-permute-start | bytes 3145736 | tf_op jit(solution)/shard_map/second_half/ppermute | solution.py:240
  338.7 19.7 %collective-permute-start.42 = (bf16[128,4096]{1,0:T(8,128)(2,1)S(1)}, bf16[128,4096]{1,0:T(8,128)(2,1)S(1)}, u32[]{:S(2)}, u32[]{:S(2)}) collective-permute-start(bf16[128,4096]{1,0:T(8,128)(2,1)S(1)} %get-tuple-element.415), channel_id=1, source_target_pairs={{6,4},{7,5},{14,12},{15,13},{22,20},{23,21},{30,28},{31,29}} | collective-permute-start | bytes 3145736 | tf_op jit(solution)/shard_map/second_half/ppermute | solution.py:243
  357.5 53.7 %collective-permute-start.47 = (bf16[8,2,64,1152]{3,2,0,1:T(8,128)(2,1)}, bf16[8,2,64,1152]{3,2,0,1:T(8,128)(2,1)}, u32[]{:S(2)}, u32[]{:S(2)}) collective-permute-start(bf16[8,2,64,1152]{3,2,0,1:T(8,128)(2,1)} %copy.109), channel_id=1, source_target_pairs={{0,16},{16,0},{1,17},{17,1},{2,18},{18,2},{3,19},{19,3},{4,20},{20... | collective-permute-start | bytes 7077896 | tf_op jit(solution)/shard_map/ffn_grad/ppermute | solution.py:391
  365.5 26.8 %collective-permute-start.43 = (bf16[128,4096]{1,0:T(8,128)(2,1)}, bf16[128,4096]{1,0:T(8,128)(2,1)}, u32[]{:S(2)}, u32[]{:S(2)}) collective-permute-start(bf16[128,4096]{1,0:T(8,128)(2,1)} %get-tuple-element.426), channel_id=1, source_target_pairs={{0,2},{2,4},{1,3},{3,5},{8,10},{10,12},{9,11},{11,13},{16,18},{18,... | collective-permute-start | bytes 3145736 | tf_op jit(solution)/shard_map/second_half/ppermute | solution.py:240
  371.8 39.4 %collective-permute-start.48 = (bf16[2,8,64,384]{3,2,1,0:T(8,128)(2,1)S(1)}, bf16[2,8,64,384]{3,2,1,0:T(8,128)(2,1)S(1)}, u32[]{:S(2)}, u32[]{:S(2)}) collective-permute-start(bf16[2,8,64,384]{3,2,1,0:T(8,128)(2,1)S(1)} %dynamic-slice_bitcast_fusion.5), channel_id=1, source_target_pairs={{0,1},{1,0},{2,3},{3,2},{4,5},{5,4},{6,7},{7,6},{8,9},{9,8},{10,11... | collective-permute-start | bytes 2359304 | tf_op jit(solution)/shard_map/ffn_grad/ppermute | solution.py:303
  374.2 50.3 %collective-permute-start.49 = (bf16[2,8,64,768]{3,2,1,0:T(8,128)(2,1)S(1)}, bf16[2,8,64,768]{3,2,1,0:T(8,128)(2,1)S(1)}, u32[]{:S(2)}, u32[]{:S(2)}) collective-permute-start(bf16[2,8,64,768]{3,2,1,0:T(8,128)(2,1)S(1)} %dynamic-slice_bitcast_fusion.1), channel_id=1, source_target_pairs={{0,1},{1,0},{2,3},{3,2},{4,5},{5,4},{6,7},{7,6},{8,9},{9,8},{10,11... | collective-permute-start | bytes 4718600 | tf_op jit(solution)/shard_map/ffn_grad/ppermute | solution.py:303
  394.5 36.0 %collective-permute-start.46 = (bf16[128,4096]{1,0:T(8,128)(2,1)S(1)}, bf16[128,4096]{1,0:T(8,128)(2,1)S(1)}, u32[]{:S(2)}, u32[]{:S(2)}) collective-permute-start(bf16[128,4096]{1,0:T(8,128)(2,1)S(1)} %get-tuple-element.433), channel_id=1, source_target_pairs={{2,0},{4,2},{6,4},{3,1},{5,3},{7,5},{10,8},{12,10},{14,12},{11,9},... | collective-permute-start | bytes 3145736 | tf_op jit(solution)/shard_map/second_half/ppermute | solution.py:243
  395.8 34.8 %collective-permute-start.45 = (bf16[128,4096]{1,0:T(8,128)(2,1)S(1)}, bf16[128,4096]{1,0:T(8,128)(2,1)S(1)}, u32[]{:S(2)}, u32[]{:S(2)}) collective-permute-start(bf16[128,4096]{1,0:T(8,128)(2,1)S(1)} %get-tuple-element.432), channel_id=1, source_target_pairs={{0,2},{2,4},{4,6},{1,3},{3,5},{5,7},{8,10},{10,12},{12,14},{9,11},... | collective-permute-start | bytes 3145736 | tf_op jit(solution)/shard_map/second_half/ppermute | solution.py:240
  427.5 34.5 %collective-permute-start.50 = (bf16[8,64,1152]{2,1,0:T(8,128)(2,1)}, bf16[8,64,1152]{2,1,0:T(8,128)(2,1)}, u32[]{:S(2)}, u32[]{:S(2)}) collective-permute-start(bf16[8,64,1152]{2,1,0:T(8,128)(2,1)} %dynamic-slice_bitcast_fusion.2), channel_id=1, source_target_pairs={{0,1},{1,0},{2,3},{3,2},{4,5},{5,4},{6,7},{7,6},{8,9},{9,8},{10,11... | collective-permute-start | bytes 3538952 | tf_op jit(solution)/shard_map/ffn_grad/ppermute | solution.py:303
  444.3 17.7 %all-to-all-start.4 = ((bf16[8,128,256]{2,1,0:T(8,128)(2,1)}), bf16[8,128,256]{2,1,0:T(8,128)(2,1)}, u32[]{:S(2)}, u32[]{:S(2)}) async-start(bf16[8,128,256]{2,1,0:T(8,128)(2,1)} %bitcast.347), calls=%async_computation.4 | async-start | bytes 1048576 | tf_op jit(solution)/shard_map/all_to_all | solution.py:676
  451.8 23.3 %collective-permute-start.52 = (bf16[8,64,768]{2,1,0:T(8,128)(2,1)}, bf16[8,64,768]{2,1,0:T(8,128)(2,1)}, u32[]{:S(2)}, u32[]{:S(2)}) collective-permute-start(bf16[8,64,768]{2,1,0:T(8,128)(2,1)} %slice_bitcast_fusion), channel_id=1, source_target_pairs={{0,16},{16,0},{1,17},{17,1},{2,18},{18,2},{3,19},{19,3},{4,20},{20... | collective-permute-start | bytes 2359304 | tf_op jit(solution)/shard_map/ffn_grad/ppermute | solution.py:391
  478.0 62.1 %all-to-all-start.5 = ((bf16[8,64,2304]{2,1,0:T(8,128)(2,1)}), bf16[8,64,2304]{2,1,0:T(8,128)(2,1)S(1)}, u32[]{:S(2)}, u32[]{:S(2)}) async-start(bf16[8,64,2304]{2,1,0:T(8,128)(2,1)} %pad_maximum_fusion.6), calls=%async_computation.5 | async-start | bytes 4718592 | tf_op jit(solution)/shard_map/all_to_all | solution.py:676
  486.4 86.4 %collective-permute-start.58 = (bf16[128,512]{1,0:T(8,128)(2,1)}, bf16[128,512]{1,0:T(8,128)(2,1)S(1)}, u32[]{:S(2)}, u32[]{:S(2)}) collective-permute-start(bf16[128,512]{1,0:T(8,128)(2,1)} %bitcast.316), channel_id=1, source_target_pairs={{0,6},{2,0},{4,2},{6,4},{1,7},{3,1},{5,3},{7,5},{8,14},{10,8},{12,... | collective-permute-start | bytes 393224 | tf_op jit(solution)/shard_map/grad_attn/ppermute | solution.py:303
  490.2 82.6 %collective-permute-start.59 = (bf16[128,512]{1,0:T(8,128)(2,1)}, bf16[128,512]{1,0:T(8,128)(2,1)S(1)}, u32[]{:S(2)}, u32[]{:S(2)}) collective-permute-start(bf16[128,512]{1,0:T(8,128)(2,1)} %bitcast.315), channel_id=1, source_target_pairs={{0,4},{2,6},{4,0},{6,2},{1,5},{3,7},{5,1},{7,3},{8,12},{10,14},{12... | collective-permute-start | bytes 393224 | tf_op jit(solution)/shard_map/grad_attn/ppermute | solution.py:303
  516.9 32.6 %collective-permute-start.55 = (bf16[64,2048]{1,0:T(8,128)(2,1)}, bf16[64,2048]{1,0:T(8,128)(2,1)}, u32[]{:S(2)}, u32[]{:S(2)}) collective-permute-start(bf16[64,2048]{1,0:T(8,128)(2,1)} %get-tuple-element.500), channel_id=1, source_target_pairs={{0,2},{2,4},{4,6},{6,7},{7,5},{5,3},{3,1},{1,0},{8,10},{10,12},{12... | collective-permute-start | bytes 786440 | tf_op jit(solution)/shard_map/grad_normed/ppermute | solution.py:184
  531.1 17.7 %collective-permute-start.56 = (bf16[64,2048]{1,0:T(8,128)(2,1)}, bf16[64,2048]{1,0:T(8,128)(2,1)S(1)}, u32[]{:S(2)}, u32[]{:S(2)}) collective-permute-start(bf16[64,2048]{1,0:T(8,128)(2,1)} %get-tuple-element.516), channel_id=1, source_target_pairs={{2,0},{4,2},{6,4},{7,6},{5,7},{3,5},{1,3},{0,1},{10,8},{12,10},{14... | collective-permute-start | bytes 786440 | tf_op jit(solution)/shard_map/grad_normed/ppermute | solution.py:184
  535.6 27.5 %collective-permute-start.54 = (bf16[2,512,768]{2,1,0:T(8,128)(2,1)}, bf16[2,512,768]{2,1,0:T(8,128)(2,1)}, u32[]{:S(2)}, u32[]{:S(2)}) collective-permute-start(bf16[2,512,768]{2,1,0:T(8,128)(2,1)} %dynamic-slice_bitcast_fusion), channel_id=1, source_target_pairs={{0,8},{8,0},{1,9},{9,1},{2,10},{10,2},{3,11},{11,3},{4,12},{12,4},... | collective-permute-start | bytes 4718600 | tf_op jit(solution)/shard_map/ppermute | solution.py:303
  568.0 21.5 %collective-permute-start.67 = (bf16[512,768]{1,0:T(8,128)(2,1)S(1)}, bf16[512,768]{1,0:T(8,128)(2,1)S(1)}, u32[]{:S(2)}, u32[]{:S(2)}) collective-permute-start(bf16[512,768]{1,0:T(8,128)(2,1)S(1)} %dynamic-slice_bitcast_fusion.4), channel_id=1, source_target_pairs={{0,16},{16,0},{1,17},{17,1},{2,18},{18,2},{3,19},{19,3},{4,20},{20... | collective-permute-start | bytes 2359304 | tf_op jit(solution)/shard_map/ppermute | solution.py:303
  578.2 17.6 %collective-permute-start.64 = (bf16[128,2048]{1,0:T(8,128)(2,1)}, bf16[128,2048]{1,0:T(8,128)(2,1)S(1)}, u32[]{:S(2)}, u32[]{:S(2)}) collective-permute-start(bf16[128,2048]{1,0:T(8,128)(2,1)} %get-tuple-element.528), channel_id=1, source_target_pairs={{0,2},{2,4},{4,6},{6,7},{7,5},{5,3},{3,1},{1,0},{8,10},{10,12},{12... | collective-permute-start | bytes 1572872 | tf_op jit(solution)/shard_map/grad_normed/ppermute | solution.py:184
  590.6 48.3 %all-to-all-start.6 = ((bf16[8,64,768]{2,1,0:T(8,128)(2,1)}), bf16[8,64,768]{2,1,0:T(8,128)(2,1)S(1)}, u32[]{:S(2)}, u32[]{:S(2)}) async-start(bf16[8,64,768]{2,1,0:T(8,128)(2,1)} %bitcast.113), calls=%async_computation.6 | async-start | bytes 1572864 | tf_op jit(solution)/shard_map/all_to_all | solution.py:676
  598.7 24.4 %collective-permute-start.68 = (bf16[128,2048]{1,0:T(8,128)(2,1)S(1)}, bf16[128,2048]{1,0:T(8,128)(2,1)S(1)}, u32[]{:S(2)}, u32[]{:S(2)}) collective-permute-start(bf16[128,2048]{1,0:T(8,128)(2,1)S(1)} %get-tuple-element.544), channel_id=1, source_target_pairs={{0,2},{2,4},{4,6},{6,7},{7,5},{5,3},{3,1},{1,0},{8,10},{10,12},{12... | collective-permute-start | bytes 1572872 | tf_op jit(solution)/shard_map/grad_normed/ppermute | solution.py:184
  602.7 20.4 %collective-permute-start.72 = (f32[29696]{0:T(1024)S(1)}, f32[29696]{0:T(1024)S(1)}, u32[]{:S(2)}, u32[]{:S(2)}) collective-permute-start(f32[29696]{0:T(1024)S(1)} %add.600), channel_id=1, source_target_pairs={{0,2},{2,0},{4,6},{6,4},{1,3},{3,1},{5,7},{7,5},{8,10},{10,8},{12,... | collective-permute-start | bytes 356360 | tf_op jit(solution)/shard_map/small/ppermute | solution.py:418
  604.2 18.9 %collective-permute-start.69 = (bf16[128,2048]{1,0:T(8,128)(2,1)S(1)}, bf16[128,2048]{1,0:T(8,128)(2,1)S(1)}, u32[]{:S(2)}, u32[]{:S(2)}) collective-permute-start(bf16[128,2048]{1,0:T(8,128)(2,1)S(1)} %get-tuple-element.551), channel_id=1, source_target_pairs={{2,0},{4,2},{6,4},{7,6},{5,7},{3,5},{1,3},{0,1},{10,8},{12,10},{14... | collective-permute-start | bytes 1572872 | tf_op jit(solution)/shard_map/grad_normed/ppermute | solution.py:184
  (96 other events, 1053.8 us)

commit v3 on v2

--- a/solution.py
+++ b/solution.py
@@ -11,6 +11,7 @@
 HEADS = 16
 HEAD = 128
 LANES = 128
+PIECES = 4
 
 epsilon = 1e-05
 masked_value = -1000000000.0
@@ -133,24 +134,31 @@
         return out if len(values) > 1 else out[0]
 
 
-class Task:
-    def __init__(self, name, steps):
-        self.name, self.steps = name, steps
-        self.result = None
-        self.step()
-
-    def step(self):
-        with jax.named_scope(self.name):
-            try:
-                next(self.steps)
-            except StopIteration as end:
-                self.steps, self.result = None, end.value
-        return self
-
-    def finish(self):
-        while self.steps is not None:
-            self.step()
-        return self.result
+class Plan:
+    def __init__(self):
+        self.steps, self.transfers, self.running = {}, {}, {}
+
+    def step(self, function):
+        self.steps[function.__name__] = function
+        return function
+
+    def transfer(self, function):
+        self.transfers[function.__name__] = function
+        return function
+
+    def run(self, order):
+        for i, name in enumerate(order):
+            with jax.named_scope(name):
+                if name in self.steps:
+                    self.steps[name]()
+                    continue
+                if name not in self.running:
+                    self.running[name] = self.transfers[name]()
+                if name in order[i + 1 :]:
+                    next(self.running[name], None)
+                    continue
+                for _ in self.running[name]:
+                    pass
 
 
 class Ring:
@@ -235,54 +243,49 @@
         self.count = count
         self.clock = clock
         self.me = lax.axis_index("z")
-
-    def up(self, values, low, high):
-        return lax.ppermute(values, "z", [(i, i + 1) for i in range(low, high)])
-
-    def down(self, values, low, high):
-        return lax.ppermute(values, "z", [(i + 1, i) for i in range(low, high)])
+        order = list(range(0, count, 2)) + list(range(1, count, 2))[::-1]
+        self.cycle = [(order[i], order[(i + 1) % count]) for i in range(count)]
+        evens = (count + 1) // 2
+        place = jnp.where(self.me % 2 == 0, self.me // 2, count - 1 - self.me // 2)
+        self.at = []
+        for k in range(count):
+            spot = lax.rem(place + k, count)
+            self.at.append(jnp.where(spot < evens, 2 * spot, 2 * (count - 1 - spot) + 1))
+
+    def ahead(self, k):
+        return self.at[k % self.count]
 
     def gather(self, block, axis):
-        last = self.count - 1
         size = block.shape[axis]
         shape = list(block.shape)
-        shape[axis] = size * (self.count + 1)
-        block = self.clock.hold(block)
-        total = jnp.zeros(shape, block.dtype)
-
-        def put_at(total, piece, owner):
-            owner = jnp.where((owner < 0) | (owner > last), self.count, owner)
-            return put(total, piece, [owner * size if d == axis else 0 for d in range(2)])
-
-        total = put_at(total, block, self.me)
-        below = above = block
-        for k in range(last):
-            below, above = self.up(below, k, last), self.down(above, 0, last - k)
+        shape[axis] = size * self.count
+        moved = self.clock.hold(block)
+        pieces = [moved]
+        for _ in range(1, self.count):
+            moved = lax.ppermute(moved, "z", self.cycle)
             yield
-            below, above = self.clock(below, above)
-            total = put_at(total, below, self.me - k - 1)
-            total = put_at(total, above, self.me + k + 1)
-        return total
-
-    def scatter(self, parts, before=None):
-        last = self.count - 1
-        rows, width = parts.shape[0] // self.count, parts.shape[1]
-        parts = self.clock.hold(parts)
-
-        def piece(owner):
-            return cut(parts, (owner * rows, 0), (rows, width)).astype(f32)
-
-        below = above = None
-        for k in range(last, 0, -1):
-            upward, downward = piece(self.me + k), piece(self.me - k)
-            if below is not None:
-                upward, downward = upward + below.astype(f32), downward + above.astype(f32)
-            upward, downward = self.clock(upward.astype(bf16), downward.astype(bf16))
-            below = self.up(upward, 0, last - k + 1)
-            above = self.down(downward, k - 1, last)
+            moved = self.clock(moved)
+            pieces.append(moved)
+        where = [
+            [(i, size) if d == axis else None for d in range(2)] for i in range(len(pieces))
+        ]
+        return assemble(pieces, shape, where, [self.ahead(-k) for k in range(self.count)])
+
+    def scatter(self, *parts):
+        rows, width = parts[0].shape[0] // self.count, parts[0].shape[1]
+        parts = self.clock.hold(*parts)
+
+        def pieces(owner):
+            return [cut(part, (owner * rows, 0), (rows, width)) for part in parts]
+
+        moved = self.clock(add_up(*pieces(self.ahead(-1))))
+        for k in range(self.count - 1, 0, -1):
+            moved = lax.ppermute(moved, "z", self.cycle)
             yield
-            below, above = self.clock(below, above)
-        return below, above, piece(self.me)
+            moved = self.clock(moved)
+            if k > 1:
+                moved = self.clock(add_up(moved, *pieces(self.ahead(k - 1))))
+        return moved, *pieces(self.me)
 
 
 def shifts(count):
@@ -333,7 +336,7 @@
     return lax.dynamic_index_in_dim(values, lax.axis_index(axis), dim, False)
 
 
-def add_up(own, others):
+def add_up(own, *others):
     total = own.astype(f32)
     for other in others:
         total = total + other.astype(f32)
@@ -345,25 +348,47 @@
         self.nx, self.ny, self.clock = nx, ny, clock
         self.x, self.y = lax.axis_index("x"), lax.axis_index("y")
 
-    def gather(self, block):
-        half = block.shape[2] // 2 // LANES * LANES
+    def gather(self, block, apart):
+        rows, deep, width = block.shape
+        half = rows // 2
         block = self.clock.hold(block)
         along_x, along_y = from_axis(block, "x", self.nx), from_axis(block, "y", self.ny)
         yield
         values = self.clock(*[v for v, _ in along_x + along_y])
         along_x, along_y = values[: self.nx - 1], values[self.nx - 1 :]
-        left = [[w for w, _ in from_axis(v[..., :half], "y", self.ny)] for v in along_x]
-        right = [[w for w, _ in from_axis(v[..., half:], "x", self.nx)] for v in along_y]
-        own = in_order([block, *along_y], "y", self.ny, 1)
-        yield
-        found = [own]
+        left = [[w for w, _ in from_axis(v[:half], "y", self.ny)] for v in along_x]
+        right = [[w for w, _ in from_axis(v[half:], "x", self.nx)] for v in along_y]
+        yield
+        owners = [lax.rem(self.y - k + self.ny, self.ny) for k in range(self.ny)]
+        everything = slice(None)
+        found = [([block, *along_y], [(everything, k) for k in range(self.ny)])]
         for i, value in enumerate(along_x):
-            corners = [
-                jnp.concatenate(self.clock(left[i][j], right[j][i]), axis=2)
-                for j in range(self.ny - 1)
+            pieces, where = [value], [(everything, 0)]
+            for j in range(self.ny - 1):
+                pieces += self.clock(left[i][j], right[j][i])
+                where += [(slice(0, half), j + 1), (slice(half, rows), j + 1)]
+            found.append((pieces, where))
+        size = rows * self.ny * deep
+        if apart:
+            return [
+                assemble(
+                    pieces,
+                    (rows, self.ny, deep, width),
+                    [[span, (k, None), None, None] for span, k in where],
+                    owners,
+                ).reshape(size, width)
+                for pieces, where in found
             ]
-            found.append(in_order([value, *corners], "y", self.ny, 1))
-        return [value.reshape(-1, value.shape[-1]) for value in found]
+        return assemble(
+            [piece for pieces, _ in found for piece in pieces],
+            (self.nx, rows, self.ny, deep, width),
+            [
+                [i, span, (k, None), None, None]
+                for i, (_, where) in enumerate(found)
+                for span, k in where
+            ],
+            owners,
+        ).reshape(self.nx * size, width)
 
     def place(self, k):
         return lax.rem(self.x - k + self.nx, self.nx)
@@ -395,15 +420,15 @@
         sent = [send_x(v) for v in one] + [to_axis(v, "y", ny, 2) for v in two]
         yield
         sent = [[self.clock(v) for v in group] for group in sent]
-        one = [add_up(v[0], group) for v, group in zip(one, sent)]
-        two = [add_up(own_part(v, "y", 2), group) for v, group in zip(two, sent[count:])]
+        one = [add_up(v[0], *group) for v, group in zip(one, sent)]
+        two = [add_up(own_part(v, "y", 2), *group) for v, group in zip(two, sent[count:])]
         values = self.clock(*one, *two)
         one, two = values[:count], values[count:]
         sent = [to_axis(v, "y", ny, 1) for v in one] + [send_x(v) for v in two]
         yield
         sent = [[self.clock(v) for v in group] for group in sent]
-        one = [add_up(own_part(v, "y", 1), group) for v, group in zip(one, sent)]
-        two = [add_up(v[0], group) for v, group in zip(two, sent[count:])]
+        one = [add_up(own_part(v, "y", 1), *group) for v, group in zip(one, sent)]
+        two = [add_up(v[0], *group) for v, group in zip(two, sent[count:])]
         return jnp.concatenate([*one, *two], axis=2)
 
 
@@ -473,6 +498,76 @@
 cost = pl.CostEstimate(flops=0, bytes_accessed=0, transcendentals=0)
 
 
+def assemble(pieces, shape, where, places):
+    def kernel(places_ref, *refs):
+        out, arrived = refs[len(pieces)], refs[-1]
+
+        def index(part):
+            if not isinstance(part, tuple):
+                return slice(None) if part is None else part
+            k, size = part
+            if size is None:
+                return places_ref[k]
+            return pl.ds(pl.multiple_of(places_ref[k] * size, size), size)
+
+        copies = [
+            pltpu.make_async_copy(refs[i], out.at[tuple(map(index, parts))], arrived.at[i])
+            for i, parts in enumerate(where)
+        ]
+        for copy in copies:
+            copy.start()
+        for copy in copies:
+            copy.wait()
+
+    return pl.pallas_call(
+        kernel,
+        grid_spec=pltpu.PrefetchScalarGridSpec(
+            num_scalar_prefetch=1,
+            grid=(1,),
+            in_specs=[pl.BlockSpec(memory_space=pl.ANY)] * len(pieces),
+            out_specs=pl.BlockSpec(tuple(shape), lambda i, places: (0,) * len(shape)),
+            scratch_shapes=[pltpu.SemaphoreType.DMA((len(pieces),))],
+        ),
+        out_shape=jax.ShapeDtypeStruct(tuple(shape), pieces[0].dtype),
+        compiler_params=params,
+        cost_estimate=cost,
+        name="assemble",
+    )(jnp.stack(places).astype(jnp.int32), *pieces)
+
+
+def lay_out(name, pieces, shape, kind, where, places=None):
+    places = jnp.zeros((1,), jnp.int32) if places is None else places
+
+    def kernel(places_ref, *refs):
+        out = refs[-1]
+        out[...] = jnp.zeros_like(out)
+        for i, part, columns in where:
+            value = refs[i][part].astype(kind)
+            if isinstance(columns, list):
+                place, start = columns
+                size = value.shape[-1]
+                begin = pl.multiple_of(places_ref[place] + start, LANES)
+                out[:, pl.ds(begin, size)] = value
+            else:
+                out[:, columns : columns + value.shape[-1]] = value
+
+    return pl.pallas_call(
+        kernel,
+        grid_spec=pltpu.PrefetchScalarGridSpec(
+            num_scalar_prefetch=1,
+            grid=(1,),
+            in_specs=[
+                pl.BlockSpec(a.shape, lambda i, places, n=a.ndim: (0,) * n) for a in pieces
+            ],
+            out_specs=pl.BlockSpec(shape, lambda i, places: (0, 0)),
+        ),
+        out_shape=jax.ShapeDtypeStruct(shape, kind),
+        compiler_params=params,
+        cost_estimate=cost,
+        name=name,
+    )(places, *pieces)
+
+
 def attention_specs(count, heads, block):
     def one(column):
         return pl.BlockSpec((block, HEAD), lambda h, i: (i, column + h))
@@ -487,7 +582,7 @@
 
 def attend_forward(packed, low, high):
     count, heads = packed.shape[0], packed.shape[1] // (3 * HEAD)
-    block = min(256, count)
+    block = min(512, count)
     one, whole, edge, lse = attention_specs(count, heads, block)
     return pl.pallas_call(
         forward_kernel,
@@ -506,7 +601,7 @@
 
 def attend_backward(packed, grads, low, high, log_sums, cosine, sine):
     count, heads = packed.shape[0], packed.shape[1] // (3 * HEAD)
-    block = min(256, count)
+    block = min(512, count)
     one, whole, edge, lse = attention_specs(count, heads, block)
     shape = jax.ShapeDtypeStruct((count, heads * HEAD), bf16)
     turn = pl.BlockSpec((block, HEAD), lambda h, i: (i, 0))
@@ -525,8 +620,10 @@
     )(packed, packed, packed, grads, low, high, log_sums, cosine, sine, cosine, sine)
 
 
-def over_rows(name, body, block, rows, whole, outs, sums=(), places=None, scratch=()):
-    count = rows[-1].shape[0]
+def over_rows(
+    name, body, block, rows, whole, outs, sums=(), places=None, scratch=(), first_map=None, count=None
+):
+    count = count or rows[-1].shape[0]
     places = jnp.zeros((1,), jnp.int32) if places is None else places
 
     def kernel(places_ref, *refs):
@@ -554,7 +651,8 @@
             num_scalar_prefetch=1,
             grid=(count // block,),
             in_specs=[
-                pl.BlockSpec((block, a.shape[1]), by_row) for a in rows
+                pl.BlockSpec((block, a.shape[1]), first_map if first_map and not i else by_row)
+                for i, a in enumerate(rows)
             ]
             + [pl.BlockSpec(a.shape, fixed) for a in whole],
             out_specs=[pl.BlockSpec((block, width), by_row) for width, _ in outs]
@@ -633,6 +731,26 @@
     sizes = [least + (1 if i < extra else 0) for i in range(count)]
     starts = [sum(sizes[:i]) for i in range(count)]
     return (starts, sizes, max(sizes))
+
+
+class Values:
+    pass
+
+
+ORDER = (
+    "tokens_in", "qkv_in", "tokens_in", "gate_up_pack", "tokens_in", "down_pack", "qkv_in", "out_in",
+    "tokens_in", "tables", "turn", "qkv_in", "tokens_in", "out_in", "gate_up_in", "qkv_in", "project",
+    "out_grad_in", "attend", "to_y", "out_grad_in", "to_y", "attended_in", "out_in", "attended_in",
+    "gate_up_in", "out_grad_in", "out_in", "attended_in", "out_in", "down_in", "attended_in", "out_grad_in",
+    "gate_up_in", "second_norm", "normed_core", "gate_up_in", "down_in", "down_in", "normed_core",
+    "out_grad_core", "gate_up", "down_in", "out_grad_core", "down_in", "act", "other_parts", "own_parts",
+    "other_parts", "parts_out", "first_share", "second_share", "ffn_grad", "parts_out", "parts_out",
+    "ffn_grad", "parts_out", "second_back", "heads_in", "ffn_grad", "heads_in", "ffn_back", "attend_back",
+    "first_back", "normed_out", "small", "qkv_back", "ffn_back", "normed_out", "grad_attn_in", "qkv_back",
+    "ffn_rows", "small", "normed_out", "grad_attn_in", "out_back", "small", "qkv_back", "out_back",
+    "normed_out", "small", "output", "out_back", "normed_out", "small", "out_back", "first_norm_tokens",
+    "qkv_back", "small", "out_back", "out_rows", "qkv_rows",
+)
 
 
 def per_device(
@@ -678,18 +796,18 @@
     def other_core(values):
         return lax.ppermute(values, "core", [(0, 1), (1, 0)])
 
-    token_task = Task("tokens", ring.gather(tokens))
-    qkv_blocks = (
-        w_qkv.reshape(weight_rows, 3, seq_count, own_width)
-        .transpose(2, 0, 1, 3)
-        .reshape(seq_count, weight_rows, 3 * own_width)
-    )
-    qkv_moved = all_to_all(qkv_blocks, GROUP)
-
     starts, sizes, most = tile_split(ffn_width, team_count)
     own_ffn = most * LANES
     padded = (starts[-1] + most) * LANES
     first_tile = jnp.asarray(starts, jnp.int32)[core * nz + z] * LANES
+    split = 3 * own_ffn // 2 // LANES * LANES
+    half_places = jnp.stack([lax.rem(x - k + nx, nx) for k in range(nx)])
+    places = jnp.concatenate([half_places * 2 + core, half_places * 2 + 1 - core])
+    cotangent = out_grad.astype(f32)
+    pieces_of = PIECES if PIECES % nx == 0 else nx
+    piece_width = width // pieces_of
+    plan = Plan()
+    v = Values()
 
     def ffn_blocks(weight, mask):
         whole = jnp.pad(weight, ((0, 0), (0, padded - ffn_width)))
@@ -704,40 +822,84 @@
     def ffn_bias(bias):
         return cut(jnp.pad(bias, (0, padded - ffn_width)), (first_tile,), (own_ffn,))
 
-    half_places = jnp.stack([lax.rem(x - k + nx, nx) for k in range(nx)])
-    places = jnp.concatenate([half_places * 2 + core, half_places * 2 + 1 - core])
-
-    row = lambda values: values.reshape(1, -1)
-    token_task.step()
-    gate_up_blocks = clock.run(
-        lambda gate, up: jnp.concatenate([ffn_blocks(gate, False), ffn_blocks(up, False)], axis=2),
-        w_gate,
-        w_up,
-    )
-    token_task.step()
-    down_blocks = clock.run(lambda down: ffn_blocks(down, True), w_down)
-    qkv_rows = clock(qkv_moved).reshape(seq_count * weight_rows, 3 * own_width)
-    from_x = from_axis(qkv_rows, "x", nx)
-    out_moved = all_to_all(
-        clock.hold(jnp.broadcast_to(w_out[None], (nz, weight_rows, width))), "z"
-    )
-    token_task.step()
-
-    def tables(lengths, prefixes):
-        position, low, high = group_layout(lengths[0], prefixes[0], count)
-        return (*rotary_tables(position), low[:, None], high[:, None])
-
-    cosine, sine, low, high = clock.run(tables, protein_lengths, prefix_lengths)
-    arrived = [clock(value) for value, _ in from_x]
-    qkv_pieces = [qkv_rows, *arrived]
-    from_core = [other_core(value) for value in qkv_pieces]
-    tokens_all = clock(token_task.finish())
-    out_task = Task("w_out", grid.gather(clock(out_moved)))
-    gate_up_moved = all_to_all(clock.hold(gate_up_blocks), TEAM)
-    qkv_pieces += [clock(value) for value in from_core]
-    qkv_bias = cut(b_qkv.reshape(3, width), (0, me * own_width), (3, own_width))
-
-    def first_kernel(rows, whole, places_ref, outs, sums):
+    def row(values):
+        return values.reshape(1, -1)
+
+    def low_nt(left, right):
+        return dot_nt(left, right).astype(bf16)
+
+    def low_tn(left, right):
+        return dot_tn(left, right).astype(bf16)
+
+    @plan.transfer
+    def tokens_in():
+        v.tokens_all = clock((yield from ring.gather(tokens)))
+
+    @plan.transfer
+    def qkv_in():
+        blocks = (
+            w_qkv.reshape(weight_rows, 3, seq_count, own_width)
+            .transpose(2, 0, 1, 3)
+            .reshape(seq_count, weight_rows, 3 * own_width)
+        )
+        moved = all_to_all(clock.hold(blocks), GROUP)
+        yield
+        rows = clock(moved).reshape(seq_count * weight_rows, 3 * own_width)
+        from_x = from_axis(rows, "x", nx)
+        yield
+        pieces = [rows] + [clock(value) for value, _ in from_x]
+        from_core = [other_core(value) for value in pieces]
+        yield
+        v.qkv_pieces = pieces + [clock(value) for value in from_core]
+
+    @plan.transfer
+    def out_in():
+        block = jnp.broadcast_to(w_out[None], (nz, weight_rows, width))
+        moved = all_to_all(clock.hold(block), "z")
+        yield
+        pieces = yield from grid.gather(clock(moved), True)
+        pieces = list(clock(*pieces))
+        from_core = [other_core(piece) for piece in pieces]
+        yield
+        v.out_pieces = pieces + [clock(value) for value in from_core]
+
+    @plan.step
+    def gate_up_pack():
+        v.gate_up_blocks = clock.run(
+            lambda gate, up: jnp.concatenate(
+                [ffn_blocks(gate, False), ffn_blocks(up, False)], axis=2
+            ),
+            w_gate,
+            w_up,
+        )
+
+    @plan.step
+    def down_pack():
+        v.down_blocks = clock.run(lambda down: ffn_blocks(down, True), w_down)
+
+    @plan.transfer
+    def gate_up_in():
+        moved = all_to_all(clock.hold(v.gate_up_blocks), TEAM)
+        yield
+        v.gate_up_own = clock((yield from grid.gather(clock(moved), False)))
+
+    @plan.transfer
+    def down_in():
+        moved = all_to_all(clock.hold(v.down_blocks), TEAM)
+        yield
+        v.down_moved = clock(moved)
+        yield
+        v.down_own = clock((yield from grid.gather(v.down_moved, False)))
+
+    @plan.step
+    def tables():
+        def make(lengths, prefixes):
+            position, low, high = group_layout(lengths[0], prefixes[0], count)
+            return (*rotary_tables(position), low[:, None], high[:, None])
+
+        v.cosine, v.sine, v.low, v.high = clock.run(make, protein_lengths, prefix_lengths)
+
+    def project_kernel(rows, whole, places_ref, outs, sums):
         tokens_ref, cos_ref, sin_ref = rows
         gain, bias, qkv_bias, *pieces = whole
         normed_ref, packed_ref = outs
@@ -750,151 +912,179 @@
                 piece = rotate(piece, cos_ref[...], sin_ref[...])
             packed_ref[:, i * HEAD : (i + 1) * HEAD] = piece.astype(bf16)
 
-    normed, packed = clock.run(
-        lambda tokens_all, *pieces: over_rows(
-            "project",
-            first_kernel,
-            256,
-            [tokens_all, cosine, sine],
-            [row(ln1_gain), row(ln1_bias), row(qkv_bias), *pieces],
-            [(width, bf16), (3 * own_width, bf16)],
-            places=places,
-        ),
-        tokens_all,
-        *qkv_pieces,
-    )
-    head_result, log_sums = clock.run(lambda values: attend_forward(values, low, high), packed)
-
-    head_result = head_result.reshape(nz, ny, own_rows, own_width)
-    moved_task = Task("to_y", exchange(head_result, "y", ny, 1, clock))
-    moved = moved_task.finish().transpose(0, 2, 1, 3).reshape(line_rows, ny * own_width)
-    attended_task = Task("attended", line.gather(clock(moved), 1))
-    out_task.step()
-    attended_task.step()
-    gate_up_moved = clock(gate_up_moved)
-    out_pieces = list(clock(*out_task.finish()))
-    from_core = [other_core(piece) for piece in out_pieces]
-    attended_task.step()
-    gate_up_task = Task("gate_up", grid.gather(gate_up_moved))
-    down_moved = all_to_all(clock.hold(down_blocks), TEAM)
-    inputs_line, out_grad_turned = clock.run(
-        lambda values, grads: (
-            lax.dynamic_index_in_dim(
-                values.reshape(nz, ny, own_rows, width), y, 1, False
-            ).reshape(line_rows, width),
-            grid.turn(grads),
-        ),
-        tokens_all,
-        out_grad,
-    )
-    out_pieces = out_pieces + [clock(value) for value in from_core]
-    attended = clock(attended_task.finish())
-    grad_out_task = Task("out_grad", line.gather(out_grad_turned, 0))
+    @plan.step
+    def project():
+        qkv_bias = cut(b_qkv.reshape(3, width), (0, me * own_width), (3, own_width))
+        v.normed, v.packed = clock.run(
+            lambda tokens_all, *pieces: over_rows(
+                "project",
+                project_kernel,
+                256,
+                [tokens_all, v.cosine, v.sine],
+                [row(ln1_gain), row(ln1_bias), row(qkv_bias), *pieces],
+                [(width, bf16), (3 * own_width, bf16)],
+                places=places,
+            ),
+            v.tokens_all,
+            *v.qkv_pieces,
+        )
+
+    @plan.step
+    def attend():
+        v.head_result, v.log_sums = clock.run(
+            lambda values: attend_forward(values, v.low, v.high), v.packed
+        )
+
+    @plan.transfer
+    def to_y():
+        result = v.head_result.reshape(nz, ny, own_rows, own_width)
+        moved = yield from exchange(result, "y", ny, 1, clock)
+        moved = moved.transpose(0, 2, 1, 3).reshape(line_rows, ny * own_width)
+        v.head_columns = clock(moved)
+
+    @plan.transfer
+    def attended_in():
+        v.attended = clock((yield from line.gather(v.head_columns, 1)))
+
+    @plan.step
+    def turn():
+        v.out_grad_turned = clock.run(grid.turn, out_grad)
+
+    @plan.transfer
+    def out_grad_in():
+        found = yield from line.gather(v.out_grad_turned, 0)
+        v.grad_out_line = clock(found)
+
+    @plan.transfer
+    def out_grad_core():
+        moved = other_core(v.grad_out_line)
+        yield
+        both = [v.grad_out_line, clock(moved)]
+        v.grad_out_all = clock(jnp.concatenate(both, axis=0))
 
     def second_kernel(rows, whole, places_ref, outs, more):
         tokens_ref, attended_ref = rows
         gain, bias, out_bias, *pieces = whole
         attn = project_pieces(attended_ref, pieces, places_ref) + out_bias[...]
         hidden = tokens_ref[...].astype(f32) + attn
-        outs[1][...] = hidden
+        outs[0][...] = hidden
         (normed_ref,) = more
         normed_ref[...] = layer_norm(hidden, gain[...], bias[...]).astype(bf16)
+        for k in range(nx):
+            place = places_ref[2 * nx + k]
+            whole = columns_of(normed_ref, place, width // nx)
+            for j in range(pieces_of // nx):
+                out = outs[1 + k * (pieces_of // nx) + j]
+                out[...] = whole[:, j * piece_width : (j + 1) * piece_width]
+
+    @plan.step
+    def second_norm():
+        hidden_in, *v.normed_line = clock.run(
+            lambda tokens, attended, *pieces: over_rows(
+                "second_norm",
+                second_kernel,
+                own_rows,
+                [tokens, attended],
+                [row(ln2_gain), row(ln2_bias), row(b_out), *pieces],
+                [(width, f32)] + [(piece_width, bf16)] * pieces_of,
+                places=jnp.concatenate([places, half_places, row(y)[0]]),
+                scratch=[(width, bf16)],
+                first_map=lambda i, places: (i * ny + places[3 * nx], 0),
+                count=line_rows,
+            ),
+            v.tokens_all,
+            v.attended,
+            *v.out_pieces,
+        )
+        v.hidden_own = cut(hidden_in, (z * own_rows, 0), (own_rows, width))
+
+    @plan.transfer
+    def normed_core():
+        moved = [other_core(piece) for piece in v.normed_line]
+        yield
+        moved = clock(*moved)
+        where = [
+            [slice(j * line_rows, (j + 1) * line_rows), slice(i * piece_width, (i + 1) * piece_width)]
+            for j in range(2)
+            for i in range(pieces_of)
+        ]
+        v.normed_two = clock(
+            assemble([*v.normed_line, *moved], (2 * line_rows, width), where, [me])
+        )
+
+    @plan.step
+    def gate_up():
+        bias = jnp.concatenate([ffn_bias(b_gate), ffn_bias(b_up)])
+        v.gate_up = clock.run(lambda a, b: dot_nn(a, b) + bias, v.normed_two, v.gate_up_own)
+
+    @plan.step
+    def act():
+        def make(grads, weight, gate_up):
+            grad_act = dot_nn(grads, weight)
+            values, pull = jax.vjp(geglu, gate_up[:, :own_ffn], gate_up[:, own_ffn:])
+            grads = [g.astype(bf16) for g in pull(grad_act)]
+            return jnp.concatenate(grads, axis=1), values.astype(bf16)
+
+        v.grad_gate_up, v.act = clock.run(make, v.grad_out_all, v.down_own, v.gate_up)
+
+    def both_parts(grads, gate_up, act, down):
+        return jnp.concatenate([low_nt(grads, gate_up), low_nt(act, down)], axis=1)
+
+    @plan.transfer
+    def other_parts():
+        found = clock.run(
+            both_parts, v.grad_gate_up[line_rows:], v.gate_up_own, v.act[line_rows:], v.down_own
+        )
+        moved = other_core(found)
+        yield
+        v.other_parts = clock(moved)
+
+    @plan.step
+    def own_parts():
+        v.own_parts = clock.run(
+            both_parts, v.grad_gate_up[:line_rows], v.gate_up_own, v.act[:line_rows], v.down_own
+        )
+
+    @plan.transfer
+    def parts_out():
+        v.two_parts = yield from line.scatter(v.own_parts, v.other_parts)
+
+    @plan.step
+    def first_share():
+        v.first_share = clock.run(low_tn, v.normed_two, v.grad_gate_up[:, :split])
+
+    @plan.step
+    def second_share():
+        v.second_share, v.third_share = clock.run(
+            lambda a, b, c, d: (low_tn(a, b[:, split:]), low_tn(c, d)),
+            v.normed_two,
+            v.grad_gate_up,
+            v.grad_out_all,
+            v.act,
+        )
+
+    @plan.transfer
+    def ffn_grad():
+        found = yield from grid.scatter(
+            [v.first_share], [v.second_share, v.third_share], team_count
+        )
+        v.ffn_share = clock(found)
+
+    @plan.transfer
+    def ffn_back():
+        moved = all_to_all(clock.hold(v.ffn_share), TEAM)
+        yield
+        v.ffn_back = clock(moved)
+
+    def second_back_kernel(rows, whole, places_ref, outs, more):
+        *sums, grads_ref = more
+        *terms, hidden, out_grad_ref = rows
+        gain, *pieces = whole
+        turned = sum(term[:, :width].astype(f32) for term in terms)
         part = width // nx
         for k in range(nx):
             place = places_ref[2 * nx + k]
-            outs[0][:, k * part : (k + 1) * part] = columns_of(normed_ref, place, part)[...]
-
-    normed_two, hidden_in = clock.run(
-        lambda tokens, attended, *pieces: over_rows(
-            "second_norm",
-            second_kernel,
-            min(256, line_rows),
-            [tokens, attended],
-            [row(ln2_gain), row(ln2_bias), row(b_out), *pieces],
-            [(width, bf16), (width, f32)],
-            places=jnp.concatenate([places, half_places]),
-            scratch=[(width, bf16)],
-        ),
-        inputs_line,
-        attended,
-        *out_pieces,
-    )
-    hidden_own = cut(hidden_in, (z * own_rows, 0), (own_rows, width))
-    grad_out_task.step()
-    normed_other = other_core(normed_two)
-    gate_up_task.step()
-    down_moved = clock(down_moved)
-    grad_out_task.step()
-    gate_up_own = clock(jnp.concatenate(gate_up_task.finish(), axis=0))
-    down_task = Task("down", grid.gather(down_moved))
-    normed_two = jnp.concatenate([normed_two, clock(normed_other)], axis=0)
-    grad_out_line = clock(grad_out_task.finish())[:line_rows]
-    grad_out_other = other_core(grad_out_line)
-
-    def first_half(values, weight):
-        gate_up = dot_nn(values, weight)
-        gate = gate_up[:, :own_ffn] + ffn_bias(b_gate)
-        upper = gate_up[:, own_ffn:] + ffn_bias(b_up)
-        return gate, upper
-
-    gate, upper = clock.run(first_half, normed_two, gate_up_own)
-    down_task.step()
-    grad_out_all = clock(jnp.concatenate([grad_out_line, clock(grad_out_other)], axis=0))
-    down_own = clock(jnp.concatenate(down_task.finish(), axis=0))
-
-    def first_half_back(grads, weight, gate, upper):
-        grad_act = dot_nn(grads, weight)
-        act, pull = jax.vjp(geglu, gate, upper)
-        return jnp.concatenate([g.astype(bf16) for g in pull(grad_act)], axis=1), act.astype(bf16)
-
-    grad_gate_up, act = clock.run(first_half_back, grad_out_all, down_own, gate, upper)
-
-    def low_nt(left, right):
-        return dot_nt(left, right).astype(bf16)
-
-    def low_tn(left, right):
-        return dot_tn(left, right).astype(bf16)
-
-    def both_parts(grads, gate_up, act, down):
-        return jnp.concatenate([low_nt(grads, gate_up), low_nt(act, down)], axis=1)
-
-    other_parts = other_core(
-        clock.run(both_parts, grad_gate_up[line_rows:], gate_up_own, act[line_rows:], down_own)
-    )
-    own_parts = clock.run(
-        both_parts, grad_gate_up[:line_rows], gate_up_own, act[:line_rows], down_own
-    )
-    parts_task = Task("second_half", line.scatter(clock(add_up(own_parts, [clock(other_parts)]))))
-    split = 3 * own_ffn // 2 // LANES * LANES
-    first_share = clock.run(low_tn, normed_two, grad_gate_up[:, :split])
-    second_share, third_share = clock.run(
-        lambda a, b, c, d: (low_tn(a, b[:, split:]), low_tn(c, d)),
-        normed_two,
-        grad_gate_up,
-        grad_out_all,
-        act,
-    )
-    ffn_grad_task = Task(
-        "ffn_grad", grid.scatter([first_share], [second_share, third_share], team_count)
-    )
-    parts_task.step()
-    bias_gate_up = clock.run(
-        lambda grads: jnp.sum(grads.astype(f32), axis=0), grad_gate_up
-    )
-    parts_task.step()
-    ffn_grad_task.step()
-    two_parts = parts_task.finish()
-
-    def second_back_kernel(rows, whole, places_ref, outs, more):
-        *sums, _ = more
-        more = more[-1:]
-        below, above, own, hidden, out_grad_ref = rows
-        gain, *pieces = whole
-        turned = below[:, :width].astype(f32) + above[:, :width].astype(f32) + own[:, :width]
-        (grads_ref,) = more
-        part = width // nx
-        for k in range(nx):
-            columns_of(grads_ref, places_ref[2 * nx + k], part)[...] = turned[:, k * part : (k + 1) * part]
+            columns_of(grads_ref, place, part)[...] = turned[:, k * part : (k + 1) * part]
         grads = grads_ref[...]
         unit, inverse = norm_parts(hidden[...])
         cotangent = out_grad_ref[...].astype(f32)
@@ -908,35 +1098,40 @@
         for ref, values in zip(sums, (grads * unit, grads, low.astype(f32), cotangent)):
             ref[...] += jnp.sum(values, axis=0, keepdims=True)
 
-    grad_hidden, grad_attn, grad_attended, *second_sums = clock.run(
-        lambda *values: over_rows(
-            "second_norm_back",
-            second_back_kernel,
-            own_rows,
-            values[:5],
-            [row(ln2_gain), *values[5:]],
-            [(width, f32), (width, bf16), (width, bf16)],
-            [width] * 4,
-            places=jnp.concatenate([places, half_places]),
-            scratch=[(width, f32)],
-        ),
-        *two_parts,
-        hidden_own,
-        out_grad,
-        *out_pieces,
-    )
-
-    grad_heads = all_to_all(
-        grad_attended.reshape(own_rows, seq_count, own_width).transpose(1, 0, 2), GROUP
-    )
-    grad_heads = clock(grad_heads).reshape(count, own_width)
-    ffn_share = clock(ffn_grad_task.finish())
-    ffn_back = all_to_all(ffn_share, TEAM)
-    grad_parts = clock.run(
-        lambda *values: attend_backward(*values, low, high, log_sums, cosine, sine),
-        packed,
-        grad_heads,
-    )
+    @plan.step
+    def second_back():
+        v.grad_hidden, v.grad_attn, v.grad_attended, *v.second_sums = clock.run(
+            lambda *values: over_rows(
+                "second_norm_back",
+                second_back_kernel,
+                own_rows,
+                values[:5],
+                [row(ln2_gain), *values[5:]],
+                [(width, f32), (width, bf16), (width, bf16)],
+                [width] * 4,
+                places=jnp.concatenate([places, half_places]),
+                scratch=[(width, f32)],
+            ),
+            *v.two_parts,
+            v.hidden_own,
+            out_grad,
+            *v.out_pieces,
+        )
+
+    @plan.transfer
+    def heads_in():
+        blocks = v.grad_attended.reshape(own_rows, seq_count, own_width).transpose(1, 0, 2)
+        moved = all_to_all(clock.hold(blocks), GROUP)
+        yield
+        v.grad_heads = clock(moved).reshape(count, own_width)
+
+    @plan.step
+    def attend_back():
+        v.grad_parts = clock.run(
+            lambda *values: attend_backward(*values, v.low, v.high, v.log_sums, v.cosine, v.sine),
+            v.packed,
+            v.grad_heads,
+        )
 
     def first_back_kernel(rows, whole, places_ref, outs, more):
         *sums, part_ref = more
@@ -957,85 +1152,98 @@
             total = jnp.sum(grad[...].astype(f32), axis=0, keepdims=True)
             sums[2][:, j * own_width : (j + 1) * own_width] += total
 
-    normed_part, *first_sums = clock.run(
-        lambda *values: over_rows(
-            "first_norm_back",
-            first_back_kernel,
-            256,
-            values[:4],
-            values[4:],
-            [(width, bf16)],
-            [width, width, 3 * own_width],
-            places=places,
-            scratch=[(width, f32)],
-        ),
-        *grad_parts,
-        tokens_all,
-        *qkv_pieces,
-    )
-    one_task = Task("grad_normed", ring.scatter(normed_part))
-
-    def spread(values, start, size):
-        return put(jnp.zeros((size,), f32), values, (start,))
-
-    def gather_small(bias_gate_up, *sums):
-        bias_qkv = sums[-1][0]
-        small = [value[0] for value in sums[:-1]]
-        small += [
-            spread(bias_qkv[i * own_width : (i + 1) * own_width], me * own_width, width)
-            for i in range(3)
-        ]
-        small += [
-            spread(bias_gate_up[:own_ffn], first_tile, padded),
-            spread(bias_gate_up[own_ffn:], first_tile, padded),
-        ]
-        return jnp.concatenate(small)
-
-    small = clock.run(gather_small, bias_gate_up, *second_sums, *first_sums)
-    small_task = Task("small", sum_everywhere(small, sizes_of, clock))
-    qkv_share = clock.run(
-        lambda a, b, c, d: low_tn(a, jnp.concatenate([b, c, d], axis=1)), normed, *grad_parts
-    )
-    qkv_share = qkv_share.reshape(nx, 2, seq_count * weight_rows, 3 * own_width)
-    qkv_core = to_axis(qkv_share, "core", 2, 1)
-    ffn_back = clock(ffn_back)
-    one_task.step()
-    grad_attn_task = Task(
-        "grad_attn",
-        exchange(grad_attn.reshape(own_rows, nz, width // nz).transpose(1, 0, 2), "z", nz, 0, clock),
-    )
-    qkv_share = clock(add_up(own_part(qkv_share, "core", 1), [clock(v) for v in qkv_core]))
-    qkv_x = to_axis(qkv_share, "x", nx, 0)
-    small_task.step()
-    one_task.step()
-    grad_attn_block = clock(grad_attn_task.finish()).reshape(line_rows, width // nz)
-    out_share = clock.run(lambda a, b: low_tn(a[:, :width], b), attended, grad_attn_block)
-    out_share = out_share.reshape(nx, 2, nz, ny, weight_rows, width // nz)
-    out_core = to_axis(out_share, "core", 2, 1)
-    small_task.step()
-    qkv_share = clock(add_up(own_part(qkv_share, "x", 0), [clock(v) for v in qkv_x]))
-    qkv_back = all_to_all(qkv_share.reshape(seq_count, weight_rows, 3 * own_width), GROUP)
-    out_share = clock(add_up(own_part(out_share, "core", 1), [clock(v) for v in out_core]))
-    out_x = to_axis(out_share, "x", nx, 0)
-    one_task.step()
-    small_task.step()
-    output = clock.run(
-        lambda below, above, own, hidden: (
-            grid.turn_back(
-                below[:, width:].astype(f32) + above[:, width:].astype(f32) + own[:, width:]
-            )
-            + hidden
-            + b_down
-        ).astype(bf16),
-        *two_parts,
-        hidden_own,
-    )
-    out_share = clock(add_up(own_part(out_share, "x", 0), [clock(v) for v in out_x]))
-    out_y = to_axis(out_share, "y", ny, 1)
-    one_parts = one_task.finish()
-    small_task.step()
-    out_share = clock(add_up(own_part(out_share, "y", 1), [clock(v) for v in out_y]))
-    out_back = Task("out_grad", exchange(out_share, "z", nz, 0, clock))
+    @plan.step
+    def first_back():
+        v.normed_part, *v.first_sums = clock.run(
+            lambda *values: over_rows(
+                "first_norm_back",
+                first_back_kernel,
+                256,
+                values[:4],
+                values[4:],
+                [(width, bf16)],
+                [width, width, 3 * own_width],
+                places=places,
+                scratch=[(width, f32)],
+            ),
+            *v.grad_parts,
+            v.tokens_all,
+            *v.qkv_pieces,
+        )
+
+    @plan.transfer
+    def normed_out():
+        v.one_parts = yield from ring.scatter(v.normed_part)
+
+    @plan.transfer
+    def small():
+        sums = [*v.second_sums, *v.first_sums[:2]]
+        bias_gate_up = jnp.sum(v.grad_gate_up.astype(f32), axis=0, keepdims=True)
+        where = [(i, (slice(None), slice(None)), i * width) for i in range(len(sums))]
+        start = len(sums) * width
+        for i in range(3):
+            part = (slice(None), slice(i * own_width, (i + 1) * own_width))
+            where.append((len(sums), part, [0, start + i * width]))
+        start += 3 * width
+        for i in range(2):
+            part = (slice(None), slice(i * own_ffn, (i + 1) * own_ffn))
+            where.append((len(sums) + 1, part, [1, start + i * padded]))
+        values = clock.run(
+            lambda *values: lay_out(
+                "small",
+                values,
+                (1, start + 2 * padded),
+                f32,
+                where,
+                jnp.stack([me * own_width, first_tile]).astype(jnp.int32),
+            ),
+            *sums,
+            v.first_sums[2],
+            bias_gate_up,
+        )
+        v.small = (yield from sum_everywhere(values, sizes_of, clock))[0]
+
+    @plan.transfer
+    def qkv_back():
+        share = clock.run(
+            lambda a, *b: low_tn(a, jnp.concatenate(b, axis=1)), v.normed, *v.grad_parts
+        )
+        share = share.reshape(nx, 2, seq_count * weight_rows, 3 * own_width)
+        for axis, size, dim in (("core", 2, 1), ("x", nx, 0)):
+            arrived = to_axis(share, axis, size, dim)
+            yield
+            share = clock(add_up(own_part(share, axis, dim), *[clock(a) for a in arrived]))
+        moved = all_to_all(share.reshape(seq_count, weight_rows, 3 * own_width), GROUP)
+        yield
+        v.qkv_back = clock(moved)
+
+    @plan.transfer
+    def grad_attn_in():
+        blocks = clock.hold(v.grad_attn).reshape(own_rows, nz, width // nz).transpose(1, 0, 2)
+        found = yield from exchange(blocks, "z", nz, 0, clock)
+        v.grad_attn_block = clock(found).reshape(line_rows, width // nz)
+
+    @plan.transfer
+    def out_back():
+        share = clock.run(low_tn, v.attended, v.grad_attn_block)
+        share = share.reshape(nx, 2, nz, ny, weight_rows, width // nz)
+        for axis, size, dim in (("core", 2, 1), ("x", nx, 0), ("y", ny, 1)):
+            arrived = to_axis(share, axis, size, dim)
+            yield
+            share = clock(add_up(own_part(share, axis, dim), *[clock(a) for a in arrived]))
+        v.out_back = yield from exchange(share, "z", nz, 0, clock)
+
+    @plan.step
+    def output():
+        v.output = clock.run(
+            lambda hidden, *terms: (
+                grid.turn_back(sum(term[:, width:].astype(f32) for term in terms))
+                + hidden
+                + b_down
+            ).astype(bf16),
+            v.hidden_own,
+            *v.two_parts,
+        )
 
     def last_kernel(rows, whole, places_ref, outs, sums):
         below, above, own, tokens_ref, hidden_grad = rows
@@ -1044,58 +1252,82 @@
         total = hidden_grad[...] + layer_norm_back(unit, inverse, whole[0][...], grads)
         outs[0][...] = total.astype(bf16)
 
-    tokens_grad = clock.run(
-        lambda *values: over_rows(
-            "first_norm_tokens",
-            last_kernel,
-            own_rows,
-            values,
-            [row(ln1_gain)],
-            [(width, bf16)],
-        )[0],
-        *one_parts,
-        tokens,
-        grad_hidden,
+    @plan.step
+    def first_norm_tokens():
+        v.tokens_grad = clock.run(
+            lambda *values: over_rows(
+                "first_norm_tokens",
+                last_kernel,
+                own_rows,
+                values,
+                [row(ln1_gain)],
+                [(width, bf16)],
+            )[0],
+            *v.one_parts,
+            tokens,
+            v.grad_hidden,
+        )
+
+    @plan.step
+    def ffn_rows():
+        def rows_of(moved, which):
+            everything = slice(None)
+            where = []
+            for i in range(team_count):
+                size = min(sizes[i] * LANES, ffn_width - starts[i] * LANES)
+                span = slice(which * own_ffn, which * own_ffn + size)
+                where.append((0, (i, everything, span), starts[i] * LANES))
+            return lay_out("ffn_rows", [moved], (weight_rows, ffn_width), f32, where)
+
+        v.ffn_rows = clock.run(lambda moved: [rows_of(moved, i) for i in range(3)], v.ffn_back)
+
+    @plan.step
+    def qkv_rows():
+        everything = slice(None)
+        where = [
+            (0, (i, everything, slice(j * own_width, (j + 1) * own_width)), j * width + i * own_width)
+            for i in range(seq_count)
+            for j in range(3)
+        ]
+        v.qkv_rows = clock.run(
+            lambda moved: lay_out("qkv_rows", [moved], (weight_rows, 3 * width), f32, where),
+            v.qkv_back,
+        )
+
+    @plan.step
+    def out_rows():
+        everything = slice(None)
+        where = [(0, (i, everything, everything), i * (width // nz)) for i in range(nz)]
+        v.out_rows = clock.run(
+            lambda moved: lay_out("out_rows", [moved], (weight_rows, width), f32, where),
+            v.out_back,
+        )
+
+    plan.run(ORDER)
+
+
+    gain_two, bias_two, b_out_grad, b_down_grad, gain_one, bias_one = (
+        v.small[i * width : (i + 1) * width] for i in range(6)
     )
-    small = small_task.finish()
-    out_back = out_back.finish()
-
-    def ffn_rows(moved, begin):
-        pieces = [moved[i, :, begin : begin + sizes[i] * LANES] for i in range(team_count)]
-        return jnp.concatenate(pieces, axis=1)[:, :ffn_width].astype(f32)
-
-    out_weight_grad = (
-        out_back.transpose(1, 0, 2).reshape(weight_rows, width).astype(f32)
-    )
-    qkv_weight_grad = (
-        clock(qkv_back)
-        .reshape(seq_count, weight_rows, 3, own_width)
-        .transpose(1, 2, 0, 3)
-        .reshape(weight_rows, 3 * width)
-        .astype(f32)
-    )
-    gain_two, bias_two, b_out_grad, b_down_grad, gain_one, bias_one = (
-        small[i * width : (i + 1) * width] for i in range(6)
-    )
-    b_qkv_grad = small[6 * width : 9 * width]
-    b_gate_grad = small[9 * width : 9 * width + ffn_width]
-    b_up_grad = small[9 * width + padded : 9 * width + padded + ffn_width]
+    b_qkv_grad = v.small[6 * width : 9 * width]
+    b_gate_grad = v.small[9 * width : 9 * width + ffn_width]
+    b_up_grad = v.small[9 * width + padded : 9 * width + padded + ffn_width]
     return (
-        output,
-        tokens_grad,
+        v.output,
+        v.tokens_grad,
         gain_one,
         bias_one,
-        qkv_weight_grad,
+        v.qkv_rows,
         b_qkv_grad,
-        out_weight_grad,
+        v.out_rows,
         b_out_grad,
         gain_two,
         bias_two,
-        ffn_rows(ffn_back, 0),
+        v.ffn_rows[0],
         b_gate_grad,
-        ffn_rows(ffn_back, own_ffn),
+        v.ffn_rows[1],
         b_up_grad,
-        ffn_rows(ffn_back, 2 * own_ffn),
+        v.ffn_rows[2],
         b_down_grad,
     )
 

time: 654 us -> 626 us (0.957)
  local copies, waits for them, and re-layouts: 118 us -> 72.9 us
  Pallas kernels: 72.6 us -> 115 us
  starting transfers between devices: 146 us -> 123 us
  other arithmetic: 74.5 us -> 54.5 us
  waiting for transfers between devices: 179 us -> 193 us
    pallas_call x0 -> x13, Pallas kernels: none -> 43.8 us  [the longest x7 28.9 us: assemble(): pl.pallas_call(kernel, grid_spec=pltpu.PrefetchScalarGridSpec(num_scalar_...]
    ppermute x18 -> x9, starting transfers between devices: 43 us -> 18.3 us  [the longest x3 9.52 us: scatter(): moved = lax.ppermute(moved, 'z', self.cycle)]
    dynamic_update_slice x28 -> x9, local copies, waits for them, and re-layouts: 35.2 us -> 11.9 us  [put(): return lax.dynamic_update_slice(total, piece, [jnp.int32(i) for i in where])]
    another operation x10 -> x4, other arithmetic: 18.4 us -> 2.03 us  [the longest x2 1.18 us: assemble(): jnp.stack(places).astype(jnp.int32)]
    all_to_all x7, waiting for transfers between devices: 13.4 us -> 28.9 us  [all_to_all(): return lax.all_to_all(values, axes, split_axis=0, concat_axis=0, tiled=True)]
    unnamed x179 -> x188, local copies, waits for them, and re-layouts: 24.4 us -> 12.3 us
    ppermute x18 -> x9, waiting for transfers between devices: 49.2 us -> 60.5 us  [the longest x6 41.2 us: gather(): moved = lax.ppermute(moved, 'z', self.cycle)]
    convert_element_type x7 -> x1, other arithmetic: 10.6 us -> 0.92 us  [output(): v.output = clock.run(lambda hidden, *terms: (grid.turn_back(sum((term[:,...]
  transfers between devices with their start and end apart: 84 -> 78, of which waited for: 33 -> 31; matrix products, arithmetic and copies ran while one was open for 31% -> 24% of each run, Pallas kernels for 11% -> 17%
where the time goes in v3:
time: 626 us; the launch traced here: 616 us
  waiting for transfers between devices  193 us (31%)
  starting transfers between devices  123 us (20%)
  Pallas kernels  115 us (18%)
  local copies, waits for them, and re-layouts  72.9 us (12%)
  other arithmetic  54.5 us (9%)
  matrix products  53.8 us (9%)
    pallas_call x5, Pallas kernels, over_rows(): pl.pallas_call(kernel, grid_spec=pltpu.PrefetchScalarGridSpec(num_scalar_...  50.1 us
    ppermute x6, waiting for transfers between devices, gather(): moved = lax.ppermute(moved, 'z', self.cycle)  41.2 us
    ppermute x16, waiting for transfers between devices, send(): lax.ppermute(values, GROUP, self.forward if forward else self.backward)  39.2 us
    all_to_all x7, starting transfers between devices, all_to_all(): return lax.all_to_all(values, axes, split_axis=0, concat_axis=0, tiled=True)  35.2 us
    ppermute x15, waiting for transfers between devices, to_axis(): lax.ppermute(lax.dynamic_index_in_dim(values, lax.rem(me + step, count),...  32.4 us
    pallas_call x7, Pallas kernels, assemble(): pl.pallas_call(kernel, grid_spec=pltpu.PrefetchScalarGridSpec(num_scalar_...  28.9 us
    all_to_all x7, waiting for transfers between devices, all_to_all(): return lax.all_to_all(values, axes, split_axis=0, concat_axis=0, tiled=True)  28.9 us
    dot_general x2, matrix products, dot_nn(): lax.dot_general(left, right, (((1,), (0,)), ((), ())), preferred_element_...  20.6 us
  transfers between devices with their start and end apart: 78, of which 31 were waited for; matrix products, arithmetic and copies ran while one was open for 24% of the time, Pallas kernels for 17%

profile of v3, /device:TPU:0, one launch (start us, length us, event | category | flops | bytes accessed | tf_op | source)
XLA Modules:
  0.0 615.9 jit_solution(8927150535685007963)
XLA Ops:
  7.1 6.4 %all-to-all-start = ((bf16[8,64,768]{2,1,0:T(8,128)(2,1)}), bf16[8,64,768]{2,1,0:T(8,128)(2,1)S(1)}, u32[]{:S(2)}, u32[]{:S(2)}) async-start(bf16[8,64,768]{2,1,0:T(8,128)(2,1)} %reshape.200), calls=%async_computation | async-start | bytes 1572864 | tf_op jit(solution)/shard_map/qkv_in/all_to_all | solution.py:794
  24.1 14.9 %collective-permute-done.2 = bf16[128,2048]{1,0:T(8,128)(2,1)} collective-permute-done((bf16[128,2048]{1,0:T(8,128)(2,1)S(1)}, bf16[128,2048]{1,0:T(8,128)(2,1)}, u32[]{:S(2)}, u32[]{:S(2)}) %collective-permute-start.2) | collective-permute-done | bytes 524320 | tf_op jit(solution)/shard_map/tokens_in/ppermute | solution.py:192
  41.3 5.8 collective-permute-start.4
  58.4 5.1 collective-permute-done.5
  84.8 7.2 %all-to-all-start.2 = ((bf16[8,64,1536]{2,1,0:T(8,128)(2,1)}), bf16[8,64,1536]{2,1,0:T(8,128)(2,1)}, u32[]{:S(2)}, u32[]{:S(2)}) async-start(bf16[8,64,1536]{2,1,0:T(8,128)(2,1)} %pad_maximum_fusion.5), calls=%async_computation.2 | async-start | bytes 3145728 | tf_op jit(solution)/shard_map/gate_up_in/all_to_all | solution.py:794
  97.1 12.0 %project.1 = (bf16[1024,2048]{1,0:T(8,128)(2,1)}, bf16[1024,768]{1,0:T(8,128)(2,1)}) custom-call(s32[4]{0:T(128)} %pad_add_fusion.1.places_ref, bf16[1024,2048]{1,0:T(8,128)(2,1)} %constant_dynamic-update-slice_fusion.9.refs_0_.refs_3_, f32[1024,128]{1,0:T(8,128)} %pad_maximum_fusion.6.refs_1_.cos_ref.all_cos_ref, ...), custom_call_target="tpu_custom_call" | custom-call | tf_op jit(solution)/shard_map/project/project/pallas_call | solution.py:648
  113.2 9.5 %attend_forward.1 = (bf16[1024,256]{1,0:T(8,128)(2,1)}, f32[2,1024,1]{2,1,0:T(8,128)}) custom-call(bf16[1024,768]{1,0:T(8,128)(2,1)} %get-tuple-element.470.q_ref.k_ref.v_ref, bf16[1024,768]{1,0:T(8,128)(2,1)} %get-tuple-element.470.q_ref.k_ref.v_ref, bf16[1024,768]{1,0:T(8,128)(2,1)} %get-tuple-element.470.q_ref.k_ref.v_ref, s32[1024,1]{1,0:T(8,128)} %copy.63.low_ref, ...), custom_call_target="tpu_custom_call" | custom-call | tf_op jit(solution)/shard_map/attend/attend_forward/pallas_call | solution.py:587
  124.0 7.5 %collective-permute-done.12.refs_1_ = bf16[128,2048]{1,0:T(8,128)(2,1)} collective-permute-done((bf16[128,2048]{1,0:T(8,128)(2,1)S(1)}, bf16[128,2048]{1,0:T(8,128)(2,1)}, u32[]{:S(2)}, u32[]{:S(2)}) %collective-permute-start.12) | collective-permute-done | bytes 524320 | tf_op jit(solution)/shard_map/out_grad_in/ppermute | solution.py:265
  143.1 6.1 collective-permute-done.13.refs_1_
  152.8 10.4 %all-to-all-done.2.refs_0_ = bf16[8,64,1536]{2,1,0:T(8,128)(2,1)} async-done(((bf16[8,64,1536]{2,1,0:T(8,128)(2,1)}), bf16[8,64,1536]{2,1,0:T(8,128)(2,1)}, u32[]{:S(2)}, u32[]{:S(2)}) %all-to-all-start.2) | async-done | bytes 1572896 | tf_op jit(solution)/shard_map/gate_up_in/all_to_all | solution.py:794
  171.7 12.7 %collective-permute-done.16.refs_2_ = bf16[512,512]{1,0:T(8,128)(2,1)S(1)} collective-permute-done((bf16[512,512]{1,0:T(8,128)(2,1)S(1)}, bf16[512,512]{1,0:T(8,128)(2,1)S(1)}, u32[]{:S(2)}, u32[]{:S(2)}) %collective-permute-start.16) | collective-permute-done | bytes 524320 | tf_op jit(solution)/shard_map/attended_in/ppermute | solution.py:265
  187.3 4.1 all-to-all-start.3
  192.0 7.4 %collective-permute-done.20.refs_3_ = bf16[512,512]{1,0:T(8,128)(2,1)} collective-permute-done((bf16[512,512]{1,0:T(8,128)(2,1)S(1)}, bf16[512,512]{1,0:T(8,128)(2,1)}, u32[]{:S(2)}, u32[]{:S(2)}) %collective-permute-start.20) | collective-permute-done | bytes 524320 | tf_op jit(solution)/shard_map/attended_in/ppermute | solution.py:265
  199.4 3.6 assemble.9.refs_1_
  203.0 7.5 %collective-permute-done.25.refs_3_ = bf16[128,2048]{1,0:T(8,128)(2,1)S(1)} collective-permute-done((bf16[128,2048]{1,0:T(8,128)(2,1)}, bf16[128,2048]{1,0:T(8,128)(2,1)S(1)}, u32[]{:S(2)}, u32[]{:S(2)}) %collective-permute-start.25) | collective-permute-done | bytes 524320 | tf_op jit(solution)/shard_map/out_grad_in/ppermute | solution.py:265
  220.5 12.3 %second_norm.1 = (f32[512,2048]{1,0:T(8,128)}, bf16[512,512]{1,0:T(8,128)(2,1)}, bf16[512,512]{1,0:T(8,128)(2,1)}, bf16[512,512]{1,0:T(8,128)(2,1)}, bf16[512,512]{1,0:T(8,128)(2,1)}) custom-call(s32[7]{0:T(128)} %concatenate.59.places_ref, bf16[1024,2048]{1,0:T(8,128)(2,1)} %constant_dynamic-update-slice_fusion.9.refs_0_.refs_3_, ...), custom_call_target="tpu_custom_call" | custom-call | tf_op jit(solution)/shard_map/second_norm/second_norm/pallas_call | solution.py:648
  235.4 6.1 assemble.11
  244.9 4.3 assemble.12
  249.2 11.7 %convolution_add_fusion = f32[1024,1536]{1,0:T(8,128)} fusion(bf16[1024,2048]{1,0:T(8,128)(2,1)} %assemble.12, bf16[2048,1536]{1,0:T(8,128)(2,1)} %bitcast.261, f32[1536]{0:T(1024)S(1)} %pad_maximum_fusion.9), kind=kOutput, calls=%fused_computation.8 | convolution fusion | flops 6444023808 | bytes 16783360 | tf_op jit(solution)/shard_map/gate_up/dot_general | solution.py:95
  267.4 5.8 collective-permute-done.35.refs_3_
  275.5 4.2 assemble.13
  279.8 8.9 %fusion.4 = (bf16[1024,768]{1,0:T(8,128)(2,1)S(1)}, bf16[1024,768]{1,0:T(8,128)(2,1)S(1)}, bf16[1024,768]{1,0:T(8,128)(2,1)S(1)}) fusion(f32[1024,1536]{1,0:T(8,128)} %convolution_add_fusion, bf16[1024,2048]{1,0:T(8,128)(2,1)S(1)} %pad_maximum_fusion, bf16[2048,768]{1,0:T(8,128)(2,1)} %bitcast.274), kind=kOutput, calls=%fused_computation.17 | convolution fusion | flops 3244818432 | bytes 18350080 | tf_op jit(solution)/shard_map/act/dot_general | solution.py:95
  295.2 4.1 convolution_convert_fusion.7
  301.5 4.1 convolution_convert_fusion.4
  306.0 3.7 convolution_convert_fusion.5
  315.4 5.9 convolution_convert_fusion
  321.3 5.0 convolution_convert_fusion.2
  333.8 4.7 collective-permute-done.38
  352.8 14.5 %collective-permute-done.39 = bf16[128,4096]{1,0:T(8,128)(2,1)} collective-permute-done((bf16[128,4096]{1,0:T(8,128)(2,1)}, bf16[128,4096]{1,0:T(8,128)(2,1)}, u32[]{:S(2)}, u32[]{:S(2)}) %collective-permute-start.39) | collective-permute-done | bytes 1048608 | tf_op jit(solution)/shard_map/parts_out/ppermute | solution.py:283
  372.8 14.1 %collective-permute-done.41 = bf16[8,2,64,1152]{3,2,0,1:T(8,128)(2,1)} collective-permute-done((bf16[8,2,64,1152]{3,2,0,1:T(8,128)(2,1)}, bf16[8,2,64,1152]{3,2,0,1:T(8,128)(2,1)}, u32[]{:S(2)}, u32[]{:S(2)}) %collective-permute-start.41) | collective-permute-done | bytes 2359328 | tf_op jit(solution)/shard_map/ffn_grad/ppermute | solution.py:416
  389.8 11.8 %collective-permute-done.43 = bf16[2,8,64,768]{3,2,1,0:T(8,128)(2,1)S(1)} collective-permute-done((bf16[2,8,64,768]{3,2,1,0:T(8,128)(2,1)S(1)}, bf16[2,8,64,768]{3,2,1,0:T(8,128)(2,1)S(1)}, u32[]{:S(2)}, u32[]{:S(2)}) %collective-permute-start.43) | collective-permute-done | bytes 1572896 | tf_op jit(solution)/shard_map/ffn_grad/ppermute | solution.py:306
  411.8 10.2 %second_norm_back.1 = (f32[128,2048]{1,0:T(8,128)}, bf16[128,2048]{1,0:T(8,128)(2,1)}, bf16[128,2048]{1,0:T(8,128)(2,1)}, f32[1,2048]{1,0:T(1,128)}, f32[1,2048]...) custom-call(s32[6]{0:T(128)} %pad_add_fusion.4.places_ref, bf16[128,4096]{1,0:T(8,128)(2,1)} %copy-done.31, ...), custom_call_target="tpu_custom_call" | custom-call | tf_op jit(solution)/shard_map/second_back/second_norm_back/pallas_call | solution.py:648
  423.8 4.1 all-to-all-start.4
  428.0 4.2 collective-permute-done.44
  440.6 4.6 all-to-all-start.5
  447.0 11.9 %attend_backward.1 = (bf16[1024,256]{1,0:T(8,128)(2,1)}, bf16[1024,256]{1,0:T(8,128)(2,1)}, bf16[1024,256]{1,0:T(8,128)(2,1)}) custom-call(bf16[1024,768]{1,0:T(8,128)(2,1)} %get-tuple-element.470.q_ref.k_ref.v_ref, bf16[1024,768]{1,0:T(8,128)(2,1)} %get-tuple-element.470.q_ref.k_ref.v_ref, bf16[1024,768]{1,0:T(8,128)(2,1)} %get-tuple-element.470.q_ref.k_ref.v_ref, ...), custom_call_target="tpu_custom_call" | custom-call | tf_op jit(solution)/shard_map/attend_back/attend_backward/pallas_call | solution.py:609
  459.0 11.9 %first_norm_back.1 = (bf16[1024,2048]{1,0:T(8,128)(2,1)}, f32[1,2048]{1,0:T(1,128)}, f32[1,2048]{1,0:T(1,128)}, f32[1,768]{1,0:T(1,128)}) custom-call(s32[4]{0:T(128)} %pad_add_fusion.1.places_ref, bf16[1024,256]{1,0:T(8,128)(2,1)} %get-tuple-element.509.refs_0_, bf16[1024,256]{1,0:T(8,128)(2,1)} %get-tuple-element.510.refs_1_, ...), custom_call_target="tpu_custom_call" | custom-call | tf_op jit(solution)/shard_map/first_back/first_norm_back/pallas_call | solution.py:648
  474.8 3.8 convolution_convert_fusion.1
  482.9 16.6 %all-to-all-done.5.refs_0_ = bf16[8,64,2304]{2,1,0:T(8,128)(2,1)} async-done(((bf16[8,64,2304]{2,1,0:T(8,128)(2,1)}), bf16[8,64,2304]{2,1,0:T(8,128)(2,1)}, u32[]{:S(2)}, u32[]{:S(2)}) %all-to-all-start.5) | async-done | bytes 2359328 | tf_op jit(solution)/shard_map/ffn_back/all_to_all | solution.py:794
  499.5 6.0 collective-permute-done.50
  539.6 7.1 %collective-permute-done.51 = f32[1,29696]{1,0:T(1,128)} collective-permute-done((f32[1,29696]{1,0:T(1,128)S(1)}, f32[1,29696]{1,0:T(1,128)}, u32[]{:S(2)}, u32[]{:S(2)}) %collective-permute-start.51) | collective-permute-done | bytes 118816 | tf_op jit(solution)/shard_map/small/ppermute | solution.py:443
  551.1 5.3 all-to-all-start.6
  558.1 8.3 %collective-permute-done.59 = bf16[128,2048]{1,0:T(8,128)(2,1)} collective-permute-done((bf16[128,2048]{1,0:T(8,128)(2,1)}, bf16[128,2048]{1,0:T(8,128)(2,1)}, u32[]{:S(2)}, u32[]{:S(2)}) %collective-permute-start.59) | collective-permute-done | bytes 524320 | tf_op jit(solution)/shard_map/normed_out/ppermute | solution.py:192
  573.1 5.9 collective-permute-done.64
  587.8 4.6 collective-permute-start.67
  592.5 3.6 first_norm_tokens.1
  597.7 6.7 %collective-permute-start.68 = (bf16[64,512]{1,0:T(8,128)(2,1)S(1)}, bf16[64,512]{1,0:T(8,128)(2,1)S(1)}, u32[]{:S(2)}, u32[]{:S(2)}) collective-permute-start(bf16[64,512]{1,0:T(8,128)(2,1)S(1)} %get-tuple-element.616), channel_id=1, source_target_pairs={{0,6},{2,0},{4,2},{6,4},{1,7},{3,1},{5,3},{7,5},{8,14},{10,8},{12,... | collective-permute-start | bytes 196616 | tf_op jit(solution)/shard_map/out_back/ppermute | solution.py:306
  605.7 4.8 collective-permute-done.70
  (446 shorter events, 251.3 us)
Async XLA Ops:
  7.1 44.3 %all-to-all-start = ((bf16[8,64,768]{2,1,0:T(8,128)(2,1)}), bf16[8,64,768]{2,1,0:T(8,128)(2,1)S(1)}, u32[]{:S(2)}, u32[]{:S(2)}) async-start(bf16[8,64,768]{2,1,0:T(8,128)(2,1)} %reshape.200), calls=%async_computation | async-start | bytes 1572864 | tf_op jit(solution)/shard_map/qkv_in/all_to_all | solution.py:794
  18.8 20.2 %collective-permute-start.2 = (bf16[128,2048]{1,0:T(8,128)(2,1)S(1)}, bf16[128,2048]{1,0:T(8,128)(2,1)}, u32[]{:S(2)}, u32[]{:S(2)}) collective-permute-start(bf16[128,2048]{1,0:T(8,128)(2,1)S(1)} %collective-permute-done), channel_id=1, source_target_pairs={{0,2},{2,4},{4,6},{6,7},{7,5},{5,3},{3,1},{1,0},{8,10},{10,12},{12... | collective-permute-start | bytes 1572872 | tf_op jit(solution)/shard_map/tokens_in/ppermute | solution.py:192
  20.4 20.9 %collective-permute-start.3 = (bf16[128,2048]{1,0:T(8,128)(2,1)S(1)}, bf16[128,2048]{1,0:T(8,128)(2,1)}, u32[]{:S(2)}, u32[]{:S(2)}) collective-permute-start(bf16[128,2048]{1,0:T(8,128)(2,1)S(1)} %collective-permute-done.1), channel_id=1, source_target_pairs={{2,0},{4,2},{6,4},{7,6},{5,7},{3,5},{1,3},{0,1},{10,8},{12,10},{14... | collective-permute-start | bytes 1572872 | tf_op jit(solution)/shard_map/tokens_in/ppermute | solution.py:192
  41.3 17.1 %collective-permute-start.4 = (bf16[128,2048]{1,0:T(8,128)(2,1)}, bf16[128,2048]{1,0:T(8,128)(2,1)}, u32[]{:S(2)}, u32[]{:S(2)}) collective-permute-start(bf16[128,2048]{1,0:T(8,128)(2,1)} %collective-permute-done.2), channel_id=1, source_target_pairs={{0,2},{2,4},{4,6},{6,7},{7,5},{5,3},{3,1},{1,0},{8,10},{10,12},{12... | collective-permute-start | bytes 1572872 | tf_op jit(solution)/shard_map/tokens_in/ppermute | solution.py:192
  51.4 30.8 %collective-permute-start.8 = (bf16[512,768]{1,0:T(8,128)(2,1)S(1)}, bf16[512,768]{1,0:T(8,128)(2,1)S(1)}, u32[]{:S(2)}, u32[]{:S(2)}) collective-permute-start(bf16[512,768]{1,0:T(8,128)(2,1)S(1)} %bitcast.257), channel_id=1, source_target_pairs={{0,16},{16,0},{1,17},{17,1},{2,18},{18,2},{3,19},{19,3},{4,20},{20... | collective-permute-start | bytes 2359304 | tf_op jit(solution)/shard_map/qkv_in/ppermute | solution.py:298
  54.0 30.8 %all-to-all-start.1 = ((bf16[4,64,2048]{2,1,0:T(8,128)(2,1)}), bf16[4,64,2048]{2,1,0:T(8,128)(2,1)S(1)}, u32[]{:S(2)}, u32[]{:S(2)}) async-start(bf16[4,64,2048]{2,1,0:T(8,128)(2,1)} %broadcast_in_dim.7), calls=%async_computation.1 | async-start | bytes 2097152 | tf_op jit(solution)/shard_map/out_in/all_to_all | solution.py:794
  84.8 78.5 %all-to-all-start.2 = ((bf16[8,64,1536]{2,1,0:T(8,128)(2,1)}), bf16[8,64,1536]{2,1,0:T(8,128)(2,1)}, u32[]{:S(2)}, u32[]{:S(2)}) async-start(bf16[8,64,1536]{2,1,0:T(8,128)(2,1)} %pad_maximum_fusion.5), calls=%async_computation.2 | async-start | bytes 3145728 | tf_op jit(solution)/shard_map/gate_up_in/all_to_all | solution.py:794
  92.6 43.0 %collective-permute-start.14 = (bf16[4,64,2048]{2,1,0:T(8,128)(2,1)S(1)}, bf16[4,64,2048]{2,1,0:T(8,128)(2,1)}, u32[]{:S(2)}, u32[]{:S(2)}) collective-permute-start(bf16[4,64,2048]{2,1,0:T(8,128)(2,1)S(1)} %all-to-all-done.1.refs_0_), channel_id=1, source_target_pairs={{0,16},{16,0},{1,17},{17,1},{2,18},{18,2},{3,19},{19,3},{4,20},{20... | collective-permute-start | bytes 3145736 | tf_op jit(solution)/shard_map/out_in/ppermute | solution.py:298
  94.1 41.5 %collective-permute-start.15 = (bf16[4,64,2048]{2,1,0:T(8,128)(2,1)S(1)}, bf16[4,64,2048]{2,1,0:T(8,128)(2,1)}, u32[]{:S(2)}, u32[]{:S(2)}) collective-permute-start(bf16[4,64,2048]{2,1,0:T(8,128)(2,1)S(1)} %all-to-all-done.1.refs_0_), channel_id=1, source_target_pairs={{0,1},{1,0},{2,3},{3,2},{4,5},{5,4},{6,7},{7,6},{8,9},{9,8},{10,11... | collective-permute-start | bytes 3145736 | tf_op jit(solution)/shard_map/out_in/ppermute | solution.py:298
  109.1 22.4 %collective-permute-start.12 = (bf16[128,2048]{1,0:T(8,128)(2,1)S(1)}, bf16[128,2048]{1,0:T(8,128)(2,1)}, u32[]{:S(2)}, u32[]{:S(2)}) collective-permute-start(bf16[128,2048]{1,0:T(8,128)(2,1)S(1)} %pad_maximum_fusion.8.refs_0_), channel_id=1, source_target_pairs={{0,4},{4,6},{6,2},{2,0},{1,5},{5,7},{7,3},{3,1},{8,12},{12,14},{14... | collective-permute-start | bytes 1572872 | tf_op jit(solution)/shard_map/out_grad_in/ppermute | solution.py:265
  132.5 16.8 %collective-permute-start.13 = (bf16[512,512]{1,0:T(8,128)(2,1)S(1)}, bf16[512,512]{1,0:T(8,128)(2,1)S(1)}, u32[]{:S(2)}, u32[]{:S(2)}) collective-permute-start(bf16[512,512]{1,0:T(8,128)(2,1)S(1)} %bitcast.278), channel_id=1, source_target_pairs={{0,4},{4,6},{6,2},{2,0},{1,5},{5,7},{7,3},{3,1},{8,12},{12,14},{14... | collective-permute-start | bytes 1572872 | tf_op jit(solution)/shard_map/attended_in/ppermute | solution.py:265
  134.3 29.0 %collective-permute-start.19 = (bf16[128,2048]{1,0:T(8,128)(2,1)}, bf16[128,2048]{1,0:T(8,128)(2,1)}, u32[]{:S(2)}, u32[]{:S(2)}) collective-permute-start(bf16[128,2048]{1,0:T(8,128)(2,1)} %collective-permute-done.12.refs_1_), channel_id=1, source_target_pairs={{0,4},{4,6},{6,2},{2,0},{1,5},{5,7},{7,3},{3,1},{8,12},{12,14},{14... | collective-permute-start | bytes 1572872 | tf_op jit(solution)/shard_map/out_grad_in/ppermute | solution.py:265
  137.5 25.7 %collective-permute-start.17 = (bf16[2,64,2048]{2,1,0:T(8,128)(2,1)}, bf16[2,64,2048]{2,1,0:T(8,128)(2,1)}, u32[]{:S(2)}, u32[]{:S(2)}) collective-permute-start(bf16[2,64,2048]{2,1,0:T(8,128)(2,1)} %slice.260), channel_id=1, source_target_pairs={{0,1},{1,0},{2,3},{3,2},{4,5},{5,4},{6,7},{7,6},{8,9},{9,8},{10,11... | collective-permute-start | bytes 1572872 | tf_op jit(solution)/shard_map/out_in/ppermute | solution.py:298
  141.0 22.2 %collective-permute-start.18 = (bf16[2,64,2048]{2,1,0:T(8,128)(2,1)}, bf16[2,64,2048]{2,1,0:T(8,128)(2,1)}, u32[]{:S(2)}, u32[]{:S(2)}) collective-permute-start(bf16[2,64,2048]{2,1,0:T(8,128)(2,1)} %slice.261), channel_id=1, source_target_pairs={{0,16},{16,0},{1,17},{17,1},{2,18},{18,2},{3,19},{19,3},{4,20},{20... | collective-permute-start | bytes 1572872 | tf_op jit(solution)/shard_map/out_in/ppermute | solution.py:298
  166.8 19.1 %collective-permute-start.22 = (bf16[512,2048]{1,0:T(8,128)(2,1)S(1)}, bf16[512,2048]{1,0:T(8,128)(2,1)S(1)}, u32[]{:S(2)}, u32[]{:S(2)}) collective-permute-start(bf16[512,2048]{1,0:T(8,128)(2,1)S(1)} %bitcast.251), channel_id=1, source_target_pairs={{0,8},{8,0},{1,9},{9,1},{2,10},{10,2},{3,11},{11,3},{4,12},{12,4},... | collective-permute-start | bytes 6291464 | tf_op jit(solution)/shard_map/out_in/ppermute | solution.py:797
  167.2 20.1 %collective-permute-start.21 = (bf16[512,2048]{1,0:T(8,128)(2,1)}, bf16[512,2048]{1,0:T(8,128)(2,1)}, u32[]{:S(2)}, u32[]{:S(2)}) collective-permute-start(bf16[512,2048]{1,0:T(8,128)(2,1)} %bitcast.252), channel_id=1, source_target_pairs={{0,8},{8,0},{1,9},{9,1},{2,10},{10,2},{3,11},{11,3},{4,12},{12,4},... | collective-permute-start | bytes 6291464 | tf_op jit(solution)/shard_map/out_in/ppermute | solution.py:797
  167.4 47.5 %collective-permute-start.23 = (bf16[8,64,1536]{2,1,0:T(8,128)(2,1)}, bf16[8,64,1536]{2,1,0:T(8,128)(2,1)}, u32[]{:S(2)}, u32[]{:S(2)}) collective-permute-start(bf16[8,64,1536]{2,1,0:T(8,128)(2,1)} %all-to-all-done.2.refs_0_), channel_id=1, source_target_pairs={{0,16},{16,0},{1,17},{17,1},{2,18},{18,2},{3,19},{19,3},{4,20},{20... | collective-permute-start | bytes 4718600 | tf_op jit(solution)/shard_map/gate_up_in/ppermute | solution.py:298
  168.9 46.0 %collective-permute-start.24 = (bf16[8,64,1536]{2,1,0:T(8,128)(2,1)}, bf16[8,64,1536]{2,1,0:T(8,128)(2,1)}, u32[]{:S(2)}, u32[]{:S(2)}) collective-permute-start(bf16[8,64,1536]{2,1,0:T(8,128)(2,1)} %all-to-all-done.2.refs_0_), channel_id=1, source_target_pairs={{0,1},{1,0},{2,3},{3,2},{4,5},{5,4},{6,7},{7,6},{8,9},{9,8},{10,11... | collective-permute-start | bytes 4718600 | tf_op jit(solution)/shard_map/gate_up_in/ppermute | solution.py:298
  187.2 23.3 %collective-permute-start.25 = (bf16[128,2048]{1,0:T(8,128)(2,1)}, bf16[128,2048]{1,0:T(8,128)(2,1)S(1)}, u32[]{:S(2)}, u32[]{:S(2)}) collective-permute-start(bf16[128,2048]{1,0:T(8,128)(2,1)} %collective-permute-done.19.refs_2_), channel_id=1, source_target_pairs={{0,4},{4,6},{6,2},{2,0},{1,5},{5,7},{7,3},{3,1},{8,12},{12,14},{14... | collective-permute-start | bytes 1572872 | tf_op jit(solution)/shard_map/out_grad_in/ppermute | solution.py:265
  187.3 54.3 %all-to-all-start.3 = ((bf16[8,64,768]{2,1,0:T(8,128)(2,1)}), bf16[8,64,768]{2,1,0:T(8,128)(2,1)S(1)}, u32[]{:S(2)}, u32[]{:S(2)}) async-start(bf16[8,64,768]{2,1,0:T(8,128)(2,1)} %copy-done.44), calls=%async_computation.3 | async-start | bytes 1572864 | tf_op jit(solution)/shard_map/down_in/all_to_all | solution.py:794
  217.0 16.5 %collective-permute-start.27 = (bf16[4,64,1536]{2,1,0:T(8,128)(2,1)}, bf16[4,64,1536]{2,1,0:T(8,128)(2,1)}, u32[]{:S(2)}, u32[]{:S(2)}) collective-permute-start(bf16[4,64,1536]{2,1,0:T(8,128)(2,1)} %slice.262), channel_id=1, source_target_pairs={{0,1},{1,0},{2,3},{3,2},{4,5},{5,4},{6,7},{7,6},{8,9},{9,8},{10,11... | collective-permute-start | bytes 2359304 | tf_op jit(solution)/shard_map/gate_up_in/ppermute | solution.py:298
  235.3 30.0 %collective-permute-start.26 = (bf16[512,2048]{1,0:T(8,128)(2,1)S(1)}, bf16[512,2048]{1,0:T(8,128)(2,1)}, u32[]{:S(2)}, u32[]{:S(2)}) collective-permute-start(bf16[512,2048]{1,0:T(8,128)(2,1)S(1)} %copy-done.11), channel_id=1, source_target_pairs={{0,8},{8,0},{1,9},{9,1},{2,10},{10,2},{3,11},{11,3},{4,12},{12,4},... | collective-permute-start | bytes 6291464 | tf_op jit(solution)/shard_map/out_grad_core/ppermute | solution.py:797
  241.6 20.0 %collective-permute-start.29 = (bf16[8,64,768]{2,1,0:T(8,128)(2,1)S(1)}, bf16[8,64,768]{2,1,0:T(8,128)(2,1)S(1)}, u32[]{:S(2)}, u32[]{:S(2)}) collective-permute-start(bf16[8,64,768]{2,1,0:T(8,128)(2,1)S(1)} %all-to-all-done.3.refs_0_), channel_id=1, source_target_pairs={{0,16},{16,0},{1,17},{17,1},{2,18},{18,2},{3,19},{19,3},{4,20},{20... | collective-permute-start | bytes 2359304 | tf_op jit(solution)/shard_map/down_in/ppermute | solution.py:298
  243.2 19.6 %collective-permute-start.30 = (bf16[8,64,768]{2,1,0:T(8,128)(2,1)S(1)}, bf16[8,64,768]{2,1,0:T(8,128)(2,1)S(1)}, u32[]{:S(2)}, u32[]{:S(2)}) collective-permute-start(bf16[8,64,768]{2,1,0:T(8,128)(2,1)S(1)} %all-to-all-done.3.refs_0_), channel_id=1, source_target_pairs={{0,1},{1,0},{2,3},{3,2},{4,5},{5,4},{6,7},{7,6},{8,9},{9,8},{10,11... | collective-permute-start | bytes 2359304 | tf_op jit(solution)/shard_map/down_in/ppermute | solution.py:298
  312.9 25.6 %collective-permute-start.38 = (bf16[128,4096]{1,0:T(8,128)(2,1)S(1)}, bf16[128,4096]{1,0:T(8,128)(2,1)S(1)}, u32[]{:S(2)}, u32[]{:S(2)}) collective-permute-start(bf16[128,4096]{1,0:T(8,128)(2,1)S(1)} %add_convert_fusion.2), channel_id=1, source_target_pairs={{0,4},{4,6},{6,2},{2,0},{1,5},{5,7},{7,3},{3,1},{8,12},{12,14},{14... | collective-permute-start | bytes 3145736 | tf_op jit(solution)/shard_map/parts_out/ppermute | solution.py:283
  333.2 53.7 %collective-permute-start.41 = (bf16[8,2,64,1152]{3,2,0,1:T(8,128)(2,1)}, bf16[8,2,64,1152]{3,2,0,1:T(8,128)(2,1)}, u32[]{:S(2)}, u32[]{:S(2)}) collective-permute-start(bf16[8,2,64,1152]{3,2,0,1:T(8,128)(2,1)} %copy.68), channel_id=1, source_target_pairs={{0,16},{16,0},{1,17},{17,1},{2,18},{18,2},{3,19},{19,3},{4,20},{20... | collective-permute-start | bytes 7077896 | tf_op jit(solution)/shard_map/ffn_grad/ppermute | solution.py:416
  341.2 26.2 %collective-permute-start.39 = (bf16[128,4096]{1,0:T(8,128)(2,1)}, bf16[128,4096]{1,0:T(8,128)(2,1)}, u32[]{:S(2)}, u32[]{:S(2)}) collective-permute-start(bf16[128,4096]{1,0:T(8,128)(2,1)} %add_convert_fusion.1), channel_id=1, source_target_pairs={{0,4},{4,6},{6,2},{2,0},{1,5},{5,7},{7,3},{3,1},{8,12},{12,14},{14... | collective-permute-start | bytes 3145736 | tf_op jit(solution)/shard_map/parts_out/ppermute | solution.py:283
  349.0 37.9 %collective-permute-start.42 = (bf16[2,8,64,384]{3,2,1,0:T(8,128)(2,1)S(1)}, bf16[2,8,64,384]{3,2,1,0:T(8,128)(2,1)S(1)}, u32[]{:S(2)}, u32[]{:S(2)}) collective-permute-start(bf16[2,8,64,384]{3,2,1,0:T(8,128)(2,1)S(1)} %dynamic-slice_bitcast_fusion.4), channel_id=1, source_target_pairs={{0,1},{1,0},{2,3},{3,2},{4,5},{5,4},{6,7},{7,6},{8,9},{9,8},{10,11... | collective-permute-start | bytes 2359304 | tf_op jit(solution)/shard_map/ffn_grad/ppermute | solution.py:306
  351.7 50.0 %collective-permute-start.43 = (bf16[2,8,64,768]{3,2,1,0:T(8,128)(2,1)S(1)}, bf16[2,8,64,768]{3,2,1,0:T(8,128)(2,1)S(1)}, u32[]{:S(2)}, u32[]{:S(2)}) collective-permute-start(bf16[2,8,64,768]{3,2,1,0:T(8,128)(2,1)S(1)} %dynamic-slice_bitcast_fusion.1), channel_id=1, source_target_pairs={{0,1},{1,0},{2,3},{3,2},{4,5},{5,4},{6,7},{7,6},{8,9},{9,8},{10,11... | collective-permute-start | bytes 4718600 | tf_op jit(solution)/shard_map/ffn_grad/ppermute | solution.py:306
  369.4 41.4 %collective-permute-start.40 = (bf16[128,4096]{1,0:T(8,128)(2,1)S(1)}, bf16[128,4096]{1,0:T(8,128)(2,1)S(1)}, u32[]{:S(2)}, u32[]{:S(2)}) collective-permute-start(bf16[128,4096]{1,0:T(8,128)(2,1)S(1)} %add_convert_fusion), channel_id=1, source_target_pairs={{0,4},{4,6},{6,2},{2,0},{1,5},{5,7},{7,3},{3,1},{8,12},{12,14},{14... | collective-permute-start | bytes 3145736 | tf_op jit(solution)/shard_map/parts_out/ppermute | solution.py:283
  403.3 28.8 %collective-permute-start.44 = (bf16[8,64,1152]{2,1,0:T(8,128)(2,1)}, bf16[8,64,1152]{2,1,0:T(8,128)(2,1)}, u32[]{:S(2)}, u32[]{:S(2)}) collective-permute-start(bf16[8,64,1152]{2,1,0:T(8,128)(2,1)} %dynamic-slice_bitcast_fusion.2), channel_id=1, source_target_pairs={{0,1},{1,0},{2,3},{3,2},{4,5},{5,4},{6,7},{7,6},{8,9},{9,8},{10,11... | collective-permute-start | bytes 3538952 | tf_op jit(solution)/shard_map/ffn_grad/ppermute | solution.py:306
  406.3 27.7 %collective-permute-start.46 = (bf16[8,64,768]{2,1,0:T(8,128)(2,1)}, bf16[8,64,768]{2,1,0:T(8,128)(2,1)}, u32[]{:S(2)}, u32[]{:S(2)}) collective-permute-start(bf16[8,64,768]{2,1,0:T(8,128)(2,1)} %slice_bitcast_fusion), channel_id=1, source_target_pairs={{0,16},{16,0},{1,17},{17,1},{2,18},{18,2},{3,19},{19,3},{4,20},{20... | collective-permute-start | bytes 2359304 | tf_op jit(solution)/shard_map/ffn_grad/ppermute | solution.py:416
  406.9 25.8 %collective-permute-start.45 = (bf16[8,64,384]{2,1,0:T(8,128)(2,1)S(1)}, bf16[8,64,384]{2,1,0:T(8,128)(2,1)}, u32[]{:S(2)}, u32[]{:S(2)}) collective-permute-start(bf16[8,64,384]{2,1,0:T(8,128)(2,1)S(1)} %slice_bitcast_fusion.1), channel_id=1, source_target_pairs={{0,16},{16,0},{1,17},{17,1},{2,18},{18,2},{3,19},{19,3},{4,20},{20... | collective-permute-start | bytes 1179656 | tf_op jit(solution)/shard_map/ffn_grad/ppermute | solution.py:416
  423.8 16.8 %all-to-all-start.4 = ((bf16[8,128,256]{2,1,0:T(8,128)(2,1)}), bf16[8,128,256]{2,1,0:T(8,128)(2,1)}, u32[]{:S(2)}, u32[]{:S(2)}) async-start(bf16[8,128,256]{2,1,0:T(8,128)(2,1)} %bitcast.280), calls=%async_computation.4 | async-start | bytes 1048576 | tf_op jit(solution)/shard_map/heads_in/all_to_all | solution.py:794
  440.6 58.9 %all-to-all-start.5 = ((bf16[8,64,2304]{2,1,0:T(8,128)(2,1)}), bf16[8,64,2304]{2,1,0:T(8,128)(2,1)}, u32[]{:S(2)}, u32[]{:S(2)}) async-start(bf16[8,64,2304]{2,1,0:T(8,128)(2,1)} %pad_maximum_fusion.4), calls=%async_computation.5 | async-start | bytes 4718592 | tf_op jit(solution)/shard_map/ffn_back/all_to_all | solution.py:794
  480.4 28.3 %collective-permute-start.48 = (bf16[2,512,768]{2,1,0:T(8,128)(2,1)S(1)}, bf16[2,512,768]{2,1,0:T(8,128)(2,1)S(1)}, u32[]{:S(2)}, u32[]{:S(2)}) collective-permute-start(bf16[2,512,768]{2,1,0:T(8,128)(2,1)S(1)} %dynamic-slice_bitcast_fusion), channel_id=1, source_target_pairs={{0,8},{8,0},{1,9},{9,1},{2,10},{10,2},{3,11},{11,3},{4,12},{12,4},... | collective-permute-start | bytes 4718600 | tf_op jit(solution)/shard_map/qkv_back/ppermute | solution.py:306
  480.9 18.6 %collective-permute-start.49 = (bf16[64,2048]{1,0:T(8,128)(2,1)}, bf16[64,2048]{1,0:T(8,128)(2,1)}, u32[]{:S(2)}, u32[]{:S(2)}) collective-permute-start(bf16[64,2048]{1,0:T(8,128)(2,1)} %get-tuple-element.496), channel_id=1, source_target_pairs={{0,2},{2,4},{4,6},{6,7},{7,5},{5,3},{3,1},{1,0},{8,10},{10,12},{12... | collective-permute-start | bytes 786440 | tf_op jit(solution)/shard_map/normed_out/ppermute | solution.py:192
  482.5 23.0 %collective-permute-start.50 = (bf16[64,2048]{1,0:T(8,128)(2,1)S(1)}, bf16[64,2048]{1,0:T(8,128)(2,1)}, u32[]{:S(2)}, u32[]{:S(2)}) collective-permute-start(bf16[64,2048]{1,0:T(8,128)(2,1)S(1)} %get-tuple-element.514), channel_id=1, source_target_pairs={{2,0},{4,2},{6,4},{7,6},{5,7},{3,5},{1,3},{0,1},{10,8},{12,10},{14... | collective-permute-start | bytes 786440 | tf_op jit(solution)/shard_map/normed_out/ppermute | solution.py:192
  482.9 37.5 %collective-permute-start.47 = (f32[1,29696]{1,0:T(1,128)S(1)}, f32[1,29696]{1,0:T(1,128)}, u32[]{:S(2)}, u32[]{:S(2)}) collective-permute-start(f32[1,29696]{1,0:T(1,128)S(1)} %copy-done.56), channel_id=1, source_target_pairs={{0,8},{8,0},{1,9},{9,1},{2,10},{10,2},{3,11},{11,3},{4,12},{12,4},... | collective-permute-start | bytes 356360 | tf_op jit(solution)/shard_map/small/ppermute | solution.py:443
  508.0 17.8 %collective-permute-start.55 = (bf16[128,2048]{1,0:T(8,128)(2,1)}, bf16[128,2048]{1,0:T(8,128)(2,1)}, u32[]{:S(2)}, u32[]{:S(2)}) collective-permute-start(bf16[128,2048]{1,0:T(8,128)(2,1)} %get-tuple-element.517), channel_id=1, source_target_pairs={{0,2},{2,4},{4,6},{6,7},{7,5},{5,3},{3,1},{1,0},{8,10},{10,12},{12... | collective-permute-start | bytes 1572872 | tf_op jit(solution)/shard_map/normed_out/ppermute | solution.py:192
  508.6 17.8 %collective-permute-start.56 = (bf16[128,2048]{1,0:T(8,128)(2,1)}, bf16[128,2048]{1,0:T(8,128)(2,1)}, u32[]{:S(2)}, u32[]{:S(2)}) collective-permute-start(bf16[128,2048]{1,0:T(8,128)(2,1)} %get-tuple-element.525), channel_id=1, source_target_pairs={{2,0},{4,2},{6,4},{7,6},{5,7},{3,5},{1,3},{0,1},{10,8},{12,10},{14... | collective-permute-start | bytes 1572872 | tf_op jit(solution)/shard_map/normed_out/ppermute | solution.py:192
  525.8 24.2 %collective-permute-start.61 = (bf16[512,768]{1,0:T(8,128)(2,1)}, bf16[512,768]{1,0:T(8,128)(2,1)S(1)}, u32[]{:S(2)}, u32[]{:S(2)}) collective-permute-start(bf16[512,768]{1,0:T(8,128)(2,1)} %dynamic-slice_bitcast_fusion.3), channel_id=1, source_target_pairs={{0,16},{16,0},{1,17},{17,1},{2,18},{18,2},{3,19},{19,3},{4,20},{20... | collective-permute-start | bytes 2359304 | tf_op jit(solution)/shard_map/qkv_back/ppermute | solution.py:306
  537.9 18.4 %collective-permute-start.60 = (bf16[2,4,2,64,512]{4,3,1,2,0:T(8,128)(2,1)}, bf16[2,4,2,64,512]{4,3,1,2,0:T(8,128)(2,1)}, u32[]{:S(2)}, u32[]{:S(2)}) collective-permute-start(bf16[2,4,2,64,512]{4,3,1,2,0:T(8,128)(2,1)} %bitcast.242), channel_id=1, source_target_pairs={{0,8},{8,0},{1,9},{9,1},{2,10},{10,2},{3,11},{11,3},{4,12},{12,4},... | collective-permute-start | bytes 3145736 | tf_op jit(solution)/shard_map/out_back/ppermute | solution.py:306
  539.6 18.4 %collective-permute-start.58 = (bf16[128,2048]{1,0:T(8,128)(2,1)}, bf16[128,2048]{1,0:T(8,128)(2,1)}, u32[]{:S(2)}, u32[]{:S(2)}) collective-permute-start(bf16[128,2048]{1,0:T(8,128)(2,1)} %get-tuple-element.528), channel_id=1, source_target_pairs={{0,2},{2,4},{4,6},{6,7},{7,5},{5,3},{3,1},{1,0},{8,10},{10,12},{12... | collective-permute-start | bytes 1572872 | tf_op jit(solution)/shard_map/normed_out/ppermute | solution.py:192
  547.9 21.8 %collective-permute-start.57 = (f32[1,29696]{1,0:T(1,128)S(1)}, f32[1,29696]{1,0:T(1,128)}, u32[]{:S(2)}, u32[]{:S(2)}) collective-permute-start(f32[1,29696]{1,0:T(1,128)S(1)} %add.517), channel_id=1, source_target_pairs={{0,1},{1,0},{2,3},{3,2},{4,5},{5,4},{6,7},{7,6},{8,9},{9,8},{10,11... | collective-permute-start | bytes 356360 | tf_op jit(solution)/shard_map/small/ppermute | solution.py:443
  549.4 17.0 %collective-permute-start.59 = (bf16[128,2048]{1,0:T(8,128)(2,1)}, bf16[128,2048]{1,0:T(8,128)(2,1)}, u32[]{:S(2)}, u32[]{:S(2)}) collective-permute-start(bf16[128,2048]{1,0:T(8,128)(2,1)} %get-tuple-element.537), channel_id=1, source_target_pairs={{2,0},{4,2},{6,4},{7,6},{5,7},{3,5},{1,3},{0,1},{10,8},{12,10},{14... | collective-permute-start | bytes 1572872 | tf_op jit(solution)/shard_map/normed_out/ppermute | solution.py:192
  551.1 45.1 %all-to-all-start.6 = ((bf16[8,64,768]{2,1,0:T(8,128)(2,1)}), bf16[8,64,768]{2,1,0:T(8,128)(2,1)S(1)}, u32[]{:S(2)}, u32[]{:S(2)}) async-start(bf16[8,64,768]{2,1,0:T(8,128)(2,1)} %bitcast.94), calls=%async_computation.6 | async-start | bytes 1572864 | tf_op jit(solution)/shard_map/qkv_back/all_to_all | solution.py:794
  568.3 18.4 %collective-permute-start.62 = (bf16[128,2048]{1,0:T(8,128)(2,1)S(1)}, bf16[128,2048]{1,0:T(8,128)(2,1)S(1)}, u32[]{:S(2)}, u32[]{:S(2)}) collective-permute-start(bf16[128,2048]{1,0:T(8,128)(2,1)S(1)} %get-tuple-element.544), channel_id=1, source_target_pairs={{0,2},{2,4},{4,6},{6,7},{7,5},{5,3},{3,1},{1,0},{8,10},{10,12},{12... | collective-permute-start | bytes 1572872 | tf_op jit(solution)/shard_map/normed_out/ppermute | solution.py:192
  (104 other events, 1177.7 us)

commit v4 on v3

--- a/solution.py
+++ b/solution.py
@@ -323,13 +323,6 @@
     yield
     found = [own_part(values, axis, dim)] + [clock(value) for value in arrived]
     return in_order(found, axis, count, dim)
-
-
-def team_exchange(values, nz, clock):
-    values = clock.hold(values).reshape(2, nz, *values.shape[1:])
-    both = yield from exchange(values, "core", 2, 0, clock)
-    out = yield from exchange(both, "z", nz, 1, clock)
-    return out.reshape(2 * nz, *values.shape[2:])
 
 
 def own_part(values, axis, dim):
@@ -390,6 +383,13 @@
             owners,
         ).reshape(self.nx * size, width)
 
+    def send(self, values, i, j):
+        nx, ny = self.nx, self.ny
+        pairs = [
+            (x * ny + y, (x + i) % nx * ny + (y + j) % ny) for x in range(nx) for y in range(ny)
+        ]
+        return lax.ppermute(values, ("x", "y"), pairs)
+
     def place(self, k):
         return lax.rem(self.x - k + self.nx, self.nx)
 
@@ -411,24 +411,45 @@
         values = [v.reshape(nx, rows, ny, -1, v.shape[1]) for v in values]
         one, two = values[:count], values[count:]
 
-        def send_x(values):
+        def x_blocks(values):
+            return [values[k] for k in range(1, nx)]
+
+        def send_x(blocks):
             return [
-                lax.ppermute(values[k], "x", [(i, (i - k) % nx) for i in range(nx)])
-                for k in range(1, nx)
+                lax.ppermute(block, "x", [(i, (i - k) % nx) for i in range(nx)])
+                for k, block in enumerate(blocks, 1)
             ]
 
-        sent = [send_x(v) for v in one] + [to_axis(v, "y", ny, 2) for v in two]
+        def y_blocks(values, dim):
+            return [
+                lax.dynamic_index_in_dim(values, lax.rem(self.y + step, ny), dim, False)
+                for step in range(1, ny)
+            ]
+
+        def send_y(blocks):
+            return [lax.ppermute(block, "y", pairs) for block, pairs in zip(blocks, shifts(ny))]
+
+        def exchange_all(x_arrays, y_arrays, dim):
+            groups = [x_blocks(v) for v in x_arrays] + [y_blocks(v, dim) for v in y_arrays]
+            flat = self.clock(*[block for group in groups for block in group])
+            flat = list(flat) if isinstance(flat, (tuple, list)) else [flat]
+            groups = [[flat.pop(0) for _ in group] for group in groups]
+            count = len(x_arrays)
+            return [send_x(g) for g in groups[:count]] + [send_y(g) for g in groups[count:]]
+
+        sent = exchange_all(one, two, 2)
         yield
         sent = [[self.clock(v) for v in group] for group in sent]
         one = [add_up(v[0], *group) for v, group in zip(one, sent)]
         two = [add_up(own_part(v, "y", 2), *group) for v, group in zip(two, sent[count:])]
         values = self.clock(*one, *two)
         one, two = values[:count], values[count:]
-        sent = [to_axis(v, "y", ny, 1) for v in one] + [send_x(v) for v in two]
+        sent = exchange_all(two, one, 1)
         yield
         sent = [[self.clock(v) for v in group] for group in sent]
-        one = [add_up(own_part(v, "y", 1), *group) for v, group in zip(one, sent)]
-        two = [add_up(v[0], *group) for v, group in zip(two, sent[count:])]
+        back = len(two)
+        one = [add_up(own_part(v, "y", 1), *group) for v, group in zip(one, sent[back:])]
+        two = [add_up(v[0], *group) for v, group in zip(two, sent[:back])]
         return jnp.concatenate([*one, *two], axis=2)
 
 
@@ -680,51 +701,6 @@
     return total
 
 
-def transposed_sums(name, lefts, rights, block=256):
-    rights = [r if isinstance(r, (tuple, list)) else [r] for r in rights]
-    depth = lefts[0].shape[1]
-    block = min(block, depth)
-    width = sum(r.shape[1] for r in rights[0])
-    flat = [r for group in rights for r in group]
-
-    def kernel(*refs):
-        left_refs, right_refs, out_ref = refs[: len(lefts)], refs[len(lefts) : -1], refs[-1]
-        per = len(rights[0])
-        start = 0
-        for j in range(per):
-            size = rights[0][j].shape[1]
-            total = None
-            for i, left in enumerate(left_refs):
-                term = dot_tn(left[...], right_refs[i * per + j][...])
-                total = term if total is None else total + term
-            out_ref[:, start : start + size] = total.astype(bf16)
-            start += size
-
-    return pl.pallas_call(
-        kernel,
-        grid=(depth // block,),
-        in_specs=[pl.BlockSpec((a.shape[0], block), lambda i: (0, i)) for a in lefts]
-        + [pl.BlockSpec(a.shape, lambda i: (0, 0)) for a in flat],
-        out_specs=pl.BlockSpec((block, width), lambda i: (i, 0)),
-        out_shape=jax.ShapeDtypeStruct((depth, width), bf16),
-        compiler_params=params,
-        cost_estimate=cost,
-        name=name,
-    )(*lefts, *flat)
-
-
-def times_transposed(name, left, pieces, places, width):
-    def body(rows, whole, places_ref, outs, sums):
-        for i, piece in enumerate(whole):
-            part = dot_nt(rows[0][...], piece[...]).astype(bf16)
-            columns_of(outs[0], places_ref[i], piece.shape[0])[...] = part
-
-    (out,) = over_rows(
-        name, body, min(256, left.shape[0]), [left], pieces, [(width, bf16)], places=places
-    )
-    return out
-
-
 def tile_split(width, count):
     tiles = -(-width // LANES)
     least, extra = divmod(tiles, count)
@@ -746,10 +722,10 @@
     "out_grad_core", "gate_up", "down_in", "out_grad_core", "down_in", "act", "other_parts", "own_parts",
     "other_parts", "parts_out", "first_share", "second_share", "ffn_grad", "parts_out", "parts_out",
     "ffn_grad", "parts_out", "second_back", "heads_in", "ffn_grad", "heads_in", "ffn_back", "attend_back",
-    "first_back", "normed_out", "small", "qkv_back", "ffn_back", "normed_out", "grad_attn_in", "qkv_back",
-    "ffn_rows", "small", "normed_out", "grad_attn_in", "out_back", "small", "qkv_back", "out_back",
-    "normed_out", "small", "output", "out_back", "normed_out", "small", "out_back", "first_norm_tokens",
-    "qkv_back", "small", "out_back", "out_rows", "qkv_rows",
+    "qkv_back", "first_back", "normed_out", "qkv_back", "small", "grad_attn_in", "ffn_back", "normed_out",
+    "qkv_back", "small", "ffn_rows", "normed_out", "grad_attn_in", "out_back", "small", "normed_out",
+    "out_back", "small", "qkv_back", "qkv_rows", "normed_out", "out_back", "small", "output",
+    "first_norm_tokens", "small", "out_back", "out_rows",
 )
 
 
@@ -1227,10 +1203,19 @@
     def out_back():
         share = clock.run(low_tn, v.attended, v.grad_attn_block)
         share = share.reshape(nx, 2, nz, ny, weight_rows, width // nz)
-        for axis, size, dim in (("core", 2, 1), ("x", nx, 0), ("y", ny, 1)):
-            arrived = to_axis(share, axis, size, dim)
-            yield
-            share = clock(add_up(own_part(share, axis, dim), *[clock(a) for a in arrived]))
+        arrived = to_axis(share, "core", 2, 1)
+        yield
+        share = clock(add_up(own_part(share, "core", 1), *[clock(a) for a in arrived]))
+
+        def part_of(i, j):
+            where = (lax.rem(x + i, nx), 0, lax.rem(y + j, ny), 0, 0)
+            found = cut(share, where, (1, nz, 1, weight_rows, width // nz))
+            return found.reshape(nz, weight_rows, width // nz)
+
+        others = [(i, j) for i in range(nx) for j in range(ny) if i or j]
+        arrived = [grid.send(part_of(i, j), i, j) for i, j in others]
+        yield
+        share = clock(add_up(part_of(0, 0), *[clock(a) for a in arrived]))
         v.out_back = yield from exchange(share, "z", nz, 0, clock)
 
     @plan.step

time: 626 us -> 613 us (0.979)
  starting transfers between devices: 123 us -> 115 us
  waiting for transfers between devices: 193 us -> 186 us
    ppermute x15 -> x10, waiting for transfers between devices: 32.4 us -> 8.01 us  [to_axis(): lax.ppermute(lax.dynamic_index_in_dim(values, lax.rem(me + step, count),...]
    ppermute x3 -> x9, waiting for transfers between devices: 14.6 us -> 29.4 us  [the longest x3 17.9 us: send_x(): lax.ppermute(block, 'x', [(i, (i - k) % nx) for i in range(nx)])]
    ppermute x5, starting transfers between devices: 9.9 us -> 2.51 us  [sum_everywhere(): other = lax.ppermute(values, axis, [(i, i ^ step) for i in range(count)])]
    ppermute x15 -> x10, starting transfers between devices: 16.5 us -> 9.77 us  [to_axis(): lax.ppermute(lax.dynamic_index_in_dim(values, lax.rem(me + step, count),...]
    ppermute x3 -> x9, starting transfers between devices: 2.7 us -> 9.21 us  [the longest x3 3.55 us: send(): return lax.ppermute(values, ('x', 'y'), pairs)]
    unnamed x188 -> x180, local copies, waits for them, and re-layouts: 12.3 us -> 15.3 us
    convert_element_type x14 -> x13, other arithmetic: 20 us -> 20 us  [add_up(): return total.astype(bf16)]
  transfers between devices with their start and end apart: 78 -> 79, of which waited for: 31 -> 33; matrix products, arithmetic and copies ran while one was open for 24% -> 24% of each run, Pallas kernels for 17% -> 18%
where the time goes in v4:
time: 613 us; the launch traced here: 603 us
  waiting for transfers between devices  186 us (30%)
  starting transfers between devices  115 us (19%)
  Pallas kernels  115 us (19%)
  local copies, waits for them, and re-layouts  78 us (13%)
  matrix products  52.8 us (9%)
  other arithmetic  52.5 us (9%)
    pallas_call x5, Pallas kernels, over_rows(): pl.pallas_call(kernel, grid_spec=pltpu.PrefetchScalarGridSpec(num_scalar_...  49.8 us
    ppermute x16, waiting for transfers between devices, send(): lax.ppermute(values, GROUP, self.forward if forward else self.backward)  44.6 us
    ppermute x6, waiting for transfers between devices, gather(): moved = lax.ppermute(moved, 'z', self.cycle)  41.2 us
    all_to_all x7, starting transfers between devices, all_to_all(): return lax.all_to_all(values, axes, split_axis=0, concat_axis=0, tiled=True)  33.4 us
    pallas_call x7, Pallas kernels, assemble(): pl.pallas_call(kernel, grid_spec=pltpu.PrefetchScalarGridSpec(num_scalar_...  28.9 us
    all_to_all x7, waiting for transfers between devices, all_to_all(): return lax.all_to_all(values, axes, split_axis=0, concat_axis=0, tiled=True)  28 us
    ppermute x16, starting transfers between devices, send(): lax.ppermute(values, GROUP, self.forward if forward else self.backward)  21.7 us
    ppermute x3, waiting for transfers between devices, scatter(): moved = lax.ppermute(moved, 'z', self.cycle)  20.9 us
  transfers between devices with their start and end apart: 79, of which 33 were waited for; matrix products, arithmetic and copies ran while one was open for 24% of the time, Pallas kernels for 18%

profile of v4, /device:TPU:0, one launch (start us, length us, event | category | flops | bytes accessed | tf_op | source)
XLA Modules:
  0.0 602.7 jit_solution(9347909562702139582)
XLA Ops:
  7.1 6.4 %all-to-all-start = ((bf16[8,64,768]{2,1,0:T(8,128)(2,1)}), bf16[8,64,768]{2,1,0:T(8,128)(2,1)S(1)}, u32[]{:S(2)}, u32[]{:S(2)}) async-start(bf16[8,64,768]{2,1,0:T(8,128)(2,1)} %reshape.208), calls=%async_computation | async-start | bytes 1572864 | tf_op jit(solution)/shard_map/qkv_in/all_to_all | solution.py:770
  24.1 14.9 %collective-permute-done.2 = bf16[128,2048]{1,0:T(8,128)(2,1)} collective-permute-done((bf16[128,2048]{1,0:T(8,128)(2,1)S(1)}, bf16[128,2048]{1,0:T(8,128)(2,1)}, u32[]{:S(2)}, u32[]{:S(2)}) %collective-permute-start.2) | collective-permute-done | bytes 524320 | tf_op jit(solution)/shard_map/tokens_in/ppermute | solution.py:192
  41.3 5.8 collective-permute-start.4
  58.4 5.1 collective-permute-done.5
  84.8 7.2 %all-to-all-start.2 = ((bf16[8,64,1536]{2,1,0:T(8,128)(2,1)}), bf16[8,64,1536]{2,1,0:T(8,128)(2,1)}, u32[]{:S(2)}, u32[]{:S(2)}) async-start(bf16[8,64,1536]{2,1,0:T(8,128)(2,1)} %pad_maximum_fusion.5), calls=%async_computation.2 | async-start | bytes 3145728 | tf_op jit(solution)/shard_map/gate_up_in/all_to_all | solution.py:770
  97.2 12.0 %project.1 = (bf16[1024,2048]{1,0:T(8,128)(2,1)}, bf16[1024,768]{1,0:T(8,128)(2,1)}) custom-call(s32[4]{0:T(128)} %pad_add_fusion.1.places_ref, bf16[1024,2048]{1,0:T(8,128)(2,1)} %constant_dynamic-update-slice_fusion.9.refs_0_.refs_3_, f32[1024,128]{1,0:T(8,128)} %pad_maximum_fusion.6.refs_1_.cos_ref.all_cos_ref, ...), custom_call_target="tpu_custom_call" | custom-call | tf_op jit(solution)/shard_map/project/project/pallas_call | solution.py:669
  113.3 9.5 %attend_forward.1 = (bf16[1024,256]{1,0:T(8,128)(2,1)}, f32[2,1024,1]{2,1,0:T(8,128)}) custom-call(bf16[1024,768]{1,0:T(8,128)(2,1)} %get-tuple-element.482.q_ref.k_ref.v_ref, bf16[1024,768]{1,0:T(8,128)(2,1)} %get-tuple-element.482.q_ref.k_ref.v_ref, bf16[1024,768]{1,0:T(8,128)(2,1)} %get-tuple-element.482.q_ref.k_ref.v_ref, s32[1024,1]{1,0:T(8,128)} %copy.63.low_ref, ...), custom_call_target="tpu_custom_call" | custom-call | tf_op jit(solution)/shard_map/attend/attend_forward/pallas_call | solution.py:608
  124.1 7.5 %collective-permute-done.12.refs_1_ = bf16[128,2048]{1,0:T(8,128)(2,1)} collective-permute-done((bf16[128,2048]{1,0:T(8,128)(2,1)S(1)}, bf16[128,2048]{1,0:T(8,128)(2,1)}, u32[]{:S(2)}, u32[]{:S(2)}) %collective-permute-start.12) | collective-permute-done | bytes 524320 | tf_op jit(solution)/shard_map/out_grad_in/ppermute | solution.py:265
  143.2 6.1 %collective-permute-done.13.refs_1_ = bf16[512,512]{1,0:T(8,128)(2,1)S(1)} collective-permute-done((bf16[512,512]{1,0:T(8,128)(2,1)S(1)}, bf16[512,512]{1,0:T(8,128)(2,1)S(1)}, u32[]{:S(2)}, u32[]{:S(2)}) %collective-permute-start.13) | collective-permute-done | bytes 524320 | tf_op jit(solution)/shard_map/attended_in/ppermute | solution.py:265
  149.2 3.6 assemble.7
  152.8 10.4 %all-to-all-done.2.refs_0_ = bf16[8,64,1536]{2,1,0:T(8,128)(2,1)} async-done(((bf16[8,64,1536]{2,1,0:T(8,128)(2,1)}), bf16[8,64,1536]{2,1,0:T(8,128)(2,1)}, u32[]{:S(2)}, u32[]{:S(2)}) %all-to-all-start.2) | async-done | bytes 1572896 | tf_op jit(solution)/shard_map/gate_up_in/all_to_all | solution.py:770
  171.7 12.7 %collective-permute-done.16.refs_2_ = bf16[512,512]{1,0:T(8,128)(2,1)S(1)} collective-permute-done((bf16[512,512]{1,0:T(8,128)(2,1)S(1)}, bf16[512,512]{1,0:T(8,128)(2,1)S(1)}, u32[]{:S(2)}, u32[]{:S(2)}) %collective-permute-start.16) | collective-permute-done | bytes 524320 | tf_op jit(solution)/shard_map/attended_in/ppermute | solution.py:265
  187.3 4.1 all-to-all-start.3
  192.0 7.4 %collective-permute-done.20.refs_3_ = bf16[512,512]{1,0:T(8,128)(2,1)} collective-permute-done((bf16[512,512]{1,0:T(8,128)(2,1)S(1)}, bf16[512,512]{1,0:T(8,128)(2,1)}, u32[]{:S(2)}, u32[]{:S(2)}) %collective-permute-start.20) | collective-permute-done | bytes 524320 | tf_op jit(solution)/shard_map/attended_in/ppermute | solution.py:265
  199.4 3.6 assemble.9.refs_1_
  203.0 7.5 %collective-permute-done.25.refs_3_ = bf16[128,2048]{1,0:T(8,128)(2,1)S(1)} collective-permute-done((bf16[128,2048]{1,0:T(8,128)(2,1)}, bf16[128,2048]{1,0:T(8,128)(2,1)S(1)}, u32[]{:S(2)}, u32[]{:S(2)}) %collective-permute-start.25) | collective-permute-done | bytes 524320 | tf_op jit(solution)/shard_map/out_grad_in/ppermute | solution.py:265
  211.3 3.6 assemble.10
  220.5 12.3 %second_norm.1 = (f32[512,2048]{1,0:T(8,128)}, bf16[512,512]{1,0:T(8,128)(2,1)}, bf16[512,512]{1,0:T(8,128)(2,1)}, bf16[512,512]{1,0:T(8,128)(2,1)}, bf16[512,512]{1,0:T(8,128)(2,1)}) custom-call(s32[7]{0:T(128)} %concatenate.59.places_ref, bf16[1024,2048]{1,0:T(8,128)(2,1)} %constant_dynamic-update-slice_fusion.9.refs_0_.refs_3_, ...), custom_call_target="tpu_custom_call" | custom-call | tf_op jit(solution)/shard_map/second_norm/second_norm/pallas_call | solution.py:669
  235.4 6.1 %assemble.11 = bf16[2,8,2,64,1536]{4,3,2,1,0:T(8,128)(2,1)} custom-call(s32[2]{0:T(128)} %pad_add_fusion.2.places_ref, bf16[8,64,1536]{2,1,0:T(8,128)(2,1)} %all-to-all-done.2.refs_0_, bf16[8,64,1536]{2,1,0:T(8,128)(2,1)} %collective-permute-done.24.refs_1_, bf16[8,64,1536]{2,1,0:T(8,128)(2,1)} %collective-permute-done.23.refs_2_, ...), custom_call_target="tpu_custom_call" | custom-call | tf_op jit(solution)/shard_map/gate_up_in/assemble/pallas_call | solution.py:543
  244.9 4.3 assemble.12
  249.2 11.8 %convolution_add_fusion = f32[1024,1536]{1,0:T(8,128)} fusion(bf16[1024,2048]{1,0:T(8,128)(2,1)} %assemble.12, bf16[2048,1536]{1,0:T(8,128)(2,1)} %bitcast.260, f32[1536]{0:T(1024)S(1)} %pad_maximum_fusion.9), kind=kOutput, calls=%fused_computation.8 | convolution fusion | flops 6444023808 | bytes 16783360 | tf_op jit(solution)/shard_map/gate_up/dot_general | solution.py:95
  267.4 5.8 collective-permute-done.35.refs_3_
  275.5 4.2 assemble.13
  279.8 8.9 %fusion.4 = (bf16[1024,768]{1,0:T(8,128)(2,1)S(1)}, bf16[1024,768]{1,0:T(8,128)(2,1)S(1)}, bf16[1024,768]{1,0:T(8,128)(2,1)S(1)}) fusion(f32[1024,1536]{1,0:T(8,128)} %convolution_add_fusion, bf16[1024,2048]{1,0:T(8,128)(2,1)S(1)} %pad_maximum_fusion, bf16[2048,768]{1,0:T(8,128)(2,1)} %bitcast.271), kind=kOutput, calls=%fused_computation.17 | convolution fusion | flops 3244818432 | bytes 18350080 | tf_op jit(solution)/shard_map/act/dot_general | solution.py:95
  295.2 4.1 convolution_convert_fusion.7
  301.5 4.1 convolution_convert_fusion.4
  306.0 3.7 convolution_convert_fusion.5
  315.4 5.9 convolution_convert_fusion
  324.0 3.7 convolution_convert_fusion.2
  340.2 3.6 collective-permute-start.39
  348.8 17.3 %collective-permute-done.39 = bf16[128,4096]{1,0:T(8,128)(2,1)} collective-permute-done((bf16[128,4096]{1,0:T(8,128)(2,1)S(1)}, bf16[128,4096]{1,0:T(8,128)(2,1)}, u32[]{:S(2)}, u32[]{:S(2)}) %collective-permute-start.39) | collective-permute-done | bytes 1048608 | tf_op jit(solution)/shard_map/parts_out/ppermute | solution.py:283
  372.0 15.9 %collective-permute-done.41 = bf16[8,2,64,1152]{3,2,0,1:T(8,128)(2,1)S(1)} collective-permute-done((bf16[8,2,64,1152]{3,2,0,1:T(8,128)(2,1)}, bf16[8,2,64,1152]{3,2,0,1:T(8,128)(2,1)S(1)}, u32[]{:S(2)}, u32[]{:S(2)}) %collective-permute-start.41) | collective-permute-done | bytes 2359328 | tf_op jit(solution)/shard_map/ffn_grad/ppermute | solution.py:419
  391.9 7.7 %collective-permute-done.43 = bf16[2,8,64,768]{3,2,1,0:T(8,128)(2,1)S(1)} collective-permute-done((bf16[2,8,64,768]{3,2,1,0:T(8,128)(2,1)}, bf16[2,8,64,768]{3,2,1,0:T(8,128)(2,1)S(1)}, u32[]{:S(2)}, u32[]{:S(2)}) %collective-permute-start.43) | collective-permute-done | bytes 1572896 | tf_op jit(solution)/shard_map/ffn_grad/ppermute | solution.py:430
  410.9 10.2 %second_norm_back.1 = (f32[128,2048]{1,0:T(8,128)}, bf16[128,2048]{1,0:T(8,128)(2,1)}, bf16[128,2048]{1,0:T(8,128)(2,1)}, f32[1,2048]{1,0:T(1,128)}, f32[1,2048]...) custom-call(s32[6]{0:T(128)} %pad_add_fusion.4.places_ref, bf16[128,4096]{1,0:T(8,128)(2,1)} %copy-done.33, ...), custom_call_target="tpu_custom_call" | custom-call | tf_op jit(solution)/shard_map/second_back/second_norm_back/pallas_call | solution.py:669
  423.0 4.1 all-to-all-start.4
  434.9 4.9 all-to-all-done.4
  439.8 3.8 all-to-all-start.5
  443.6 12.0 %attend_backward.1 = (bf16[1024,256]{1,0:T(8,128)(2,1)}, bf16[1024,256]{1,0:T(8,128)(2,1)}, bf16[1024,256]{1,0:T(8,128)(2,1)}) custom-call(bf16[1024,768]{1,0:T(8,128)(2,1)} %get-tuple-element.482.q_ref.k_ref.v_ref, bf16[1024,768]{1,0:T(8,128)(2,1)} %get-tuple-element.482.q_ref.k_ref.v_ref, bf16[1024,768]{1,0:T(8,128)(2,1)} %get-tuple-element.482.q_ref.k_ref.v_ref, ...), custom_call_target="tpu_custom_call" | custom-call | tf_op jit(solution)/shard_map/attend_back/attend_backward/pallas_call | solution.py:630
  455.6 5.2 convolution_convert_fusion.1
  464.2 11.6 %first_norm_back.1 = (bf16[1024,2048]{1,0:T(8,128)(2,1)}, f32[1,2048]{1,0:T(1,128)}, f32[1,2048]{1,0:T(1,128)}, f32[1,768]{1,0:T(1,128)}) custom-call(s32[4]{0:T(128)} %pad_add_fusion.1.places_ref, bf16[1024,256]{1,0:T(8,128)(2,1)} %get-tuple-element.496.refs_0_, bf16[1024,256]{1,0:T(8,128)(2,1)} %get-tuple-element.497.refs_1_, ...), custom_call_target="tpu_custom_call" | custom-call | tf_op jit(solution)/shard_map/first_back/first_norm_back/pallas_call | solution.py:669
  486.4 11.5 %all-to-all-done.5.refs_0_ = bf16[8,64,2304]{2,1,0:T(8,128)(2,1)S(1)} async-done(((bf16[8,64,2304]{2,1,0:T(8,128)(2,1)}), bf16[8,64,2304]{2,1,0:T(8,128)(2,1)S(1)}, u32[]{:S(2)}, u32[]{:S(2)}) %all-to-all-start.5) | async-done | bytes 2359328 | tf_op jit(solution)/shard_map/ffn_back/all_to_all | solution.py:770
  498.6 5.3 collective-permute-done.51
  536.1 4.2 all-to-all-start.6
  541.2 4.4 collective-permute-done.52
  569.1 8.9 %collective-permute-done.64.refs_0_ = bf16[128,2048]{1,0:T(8,128)(2,1)} collective-permute-done((bf16[128,2048]{1,0:T(8,128)(2,1)}, bf16[128,2048]{1,0:T(8,128)(2,1)}, u32[]{:S(2)}, u32[]{:S(2)}) %collective-permute-start.64) | collective-permute-done | bytes 524320 | tf_op jit(solution)/shard_map/normed_out/ppermute | solution.py:192
  578.2 3.8 collective-permute-done.63
  584.9 3.6 first_norm_tokens.1
  594.9 4.0 collective-permute-done.71
  (438 shorter events, 254.7 us)
Async XLA Ops:
  7.1 44.3 %all-to-all-start = ((bf16[8,64,768]{2,1,0:T(8,128)(2,1)}), bf16[8,64,768]{2,1,0:T(8,128)(2,1)S(1)}, u32[]{:S(2)}, u32[]{:S(2)}) async-start(bf16[8,64,768]{2,1,0:T(8,128)(2,1)} %reshape.208), calls=%async_computation | async-start | bytes 1572864 | tf_op jit(solution)/shard_map/qkv_in/all_to_all | solution.py:770
  18.8 20.2 %collective-permute-start.2 = (bf16[128,2048]{1,0:T(8,128)(2,1)S(1)}, bf16[128,2048]{1,0:T(8,128)(2,1)}, u32[]{:S(2)}, u32[]{:S(2)}) collective-permute-start(bf16[128,2048]{1,0:T(8,128)(2,1)S(1)} %collective-permute-done), channel_id=1, source_target_pairs={{0,2},{2,4},{4,6},{6,7},{7,5},{5,3},{3,1},{1,0},{8,10},{10,12},{12... | collective-permute-start | bytes 1572872 | tf_op jit(solution)/shard_map/tokens_in/ppermute | solution.py:192
  20.4 20.9 %collective-permute-start.3 = (bf16[128,2048]{1,0:T(8,128)(2,1)S(1)}, bf16[128,2048]{1,0:T(8,128)(2,1)}, u32[]{:S(2)}, u32[]{:S(2)}) collective-permute-start(bf16[128,2048]{1,0:T(8,128)(2,1)S(1)} %collective-permute-done.1), channel_id=1, source_target_pairs={{2,0},{4,2},{6,4},{7,6},{5,7},{3,5},{1,3},{0,1},{10,8},{12,10},{14... | collective-permute-start | bytes 1572872 | tf_op jit(solution)/shard_map/tokens_in/ppermute | solution.py:192
  41.3 17.1 %collective-permute-start.4 = (bf16[128,2048]{1,0:T(8,128)(2,1)}, bf16[128,2048]{1,0:T(8,128)(2,1)}, u32[]{:S(2)}, u32[]{:S(2)}) collective-permute-start(bf16[128,2048]{1,0:T(8,128)(2,1)} %collective-permute-done.2), channel_id=1, source_target_pairs={{0,2},{2,4},{4,6},{6,7},{7,5},{5,3},{3,1},{1,0},{8,10},{10,12},{12... | collective-permute-start | bytes 1572872 | tf_op jit(solution)/shard_map/tokens_in/ppermute | solution.py:192
  51.4 30.9 %collective-permute-start.8 = (bf16[512,768]{1,0:T(8,128)(2,1)S(1)}, bf16[512,768]{1,0:T(8,128)(2,1)S(1)}, u32[]{:S(2)}, u32[]{:S(2)}) collective-permute-start(bf16[512,768]{1,0:T(8,128)(2,1)S(1)} %bitcast.256), channel_id=1, source_target_pairs={{0,16},{16,0},{1,17},{17,1},{2,18},{18,2},{3,19},{19,3},{4,20},{20... | collective-permute-start | bytes 2359304 | tf_op jit(solution)/shard_map/qkv_in/ppermute | solution.py:298
  54.0 30.8 %all-to-all-start.1 = ((bf16[4,64,2048]{2,1,0:T(8,128)(2,1)}), bf16[4,64,2048]{2,1,0:T(8,128)(2,1)S(1)}, u32[]{:S(2)}, u32[]{:S(2)}) async-start(bf16[4,64,2048]{2,1,0:T(8,128)(2,1)} %broadcast_in_dim.7), calls=%async_computation.1 | async-start | bytes 2097152 | tf_op jit(solution)/shard_map/out_in/all_to_all | solution.py:770
  84.8 78.4 %all-to-all-start.2 = ((bf16[8,64,1536]{2,1,0:T(8,128)(2,1)}), bf16[8,64,1536]{2,1,0:T(8,128)(2,1)}, u32[]{:S(2)}, u32[]{:S(2)}) async-start(bf16[8,64,1536]{2,1,0:T(8,128)(2,1)} %pad_maximum_fusion.5), calls=%async_computation.2 | async-start | bytes 3145728 | tf_op jit(solution)/shard_map/gate_up_in/all_to_all | solution.py:770
  92.6 43.0 %collective-permute-start.14 = (bf16[4,64,2048]{2,1,0:T(8,128)(2,1)S(1)}, bf16[4,64,2048]{2,1,0:T(8,128)(2,1)}, u32[]{:S(2)}, u32[]{:S(2)}) collective-permute-start(bf16[4,64,2048]{2,1,0:T(8,128)(2,1)S(1)} %all-to-all-done.1.refs_0_), channel_id=1, source_target_pairs={{0,16},{16,0},{1,17},{17,1},{2,18},{18,2},{3,19},{19,3},{4,20},{20... | collective-permute-start | bytes 3145736 | tf_op jit(solution)/shard_map/out_in/ppermute | solution.py:298
  94.1 41.5 %collective-permute-start.15 = (bf16[4,64,2048]{2,1,0:T(8,128)(2,1)S(1)}, bf16[4,64,2048]{2,1,0:T(8,128)(2,1)}, u32[]{:S(2)}, u32[]{:S(2)}) collective-permute-start(bf16[4,64,2048]{2,1,0:T(8,128)(2,1)S(1)} %all-to-all-done.1.refs_0_), channel_id=1, source_target_pairs={{0,1},{1,0},{2,3},{3,2},{4,5},{5,4},{6,7},{7,6},{8,9},{9,8},{10,11... | collective-permute-start | bytes 3145736 | tf_op jit(solution)/shard_map/out_in/ppermute | solution.py:298
  109.2 22.3 %collective-permute-start.12 = (bf16[128,2048]{1,0:T(8,128)(2,1)S(1)}, bf16[128,2048]{1,0:T(8,128)(2,1)}, u32[]{:S(2)}, u32[]{:S(2)}) collective-permute-start(bf16[128,2048]{1,0:T(8,128)(2,1)S(1)} %pad_maximum_fusion.8.refs_0_), channel_id=1, source_target_pairs={{0,4},{4,6},{6,2},{2,0},{1,5},{5,7},{7,3},{3,1},{8,12},{12,14},{14... | collective-permute-start | bytes 1572872 | tf_op jit(solution)/shard_map/out_grad_in/ppermute | solution.py:265
  132.5 16.8 %collective-permute-start.13 = (bf16[512,512]{1,0:T(8,128)(2,1)S(1)}, bf16[512,512]{1,0:T(8,128)(2,1)S(1)}, u32[]{:S(2)}, u32[]{:S(2)}) collective-permute-start(bf16[512,512]{1,0:T(8,128)(2,1)S(1)} %bitcast.277), channel_id=1, source_target_pairs={{0,4},{4,6},{6,2},{2,0},{1,5},{5,7},{7,3},{3,1},{8,12},{12,14},{14... | collective-permute-start | bytes 1572872 | tf_op jit(solution)/shard_map/attended_in/ppermute | solution.py:265
  134.3 29.0 %collective-permute-start.19 = (bf16[128,2048]{1,0:T(8,128)(2,1)}, bf16[128,2048]{1,0:T(8,128)(2,1)}, u32[]{:S(2)}, u32[]{:S(2)}) collective-permute-start(bf16[128,2048]{1,0:T(8,128)(2,1)} %collective-permute-done.12.refs_1_), channel_id=1, source_target_pairs={{0,4},{4,6},{6,2},{2,0},{1,5},{5,7},{7,3},{3,1},{8,12},{12,14},{14... | collective-permute-start | bytes 1572872 | tf_op jit(solution)/shard_map/out_grad_in/ppermute | solution.py:265
  137.5 25.7 %collective-permute-start.17 = (bf16[2,64,2048]{2,1,0:T(8,128)(2,1)}, bf16[2,64,2048]{2,1,0:T(8,128)(2,1)}, u32[]{:S(2)}, u32[]{:S(2)}) collective-permute-start(bf16[2,64,2048]{2,1,0:T(8,128)(2,1)} %slice.260), channel_id=1, source_target_pairs={{0,1},{1,0},{2,3},{3,2},{4,5},{5,4},{6,7},{7,6},{8,9},{9,8},{10,11... | collective-permute-start | bytes 1572872 | tf_op jit(solution)/shard_map/out_in/ppermute | solution.py:298
  141.1 22.2 %collective-permute-start.18 = (bf16[2,64,2048]{2,1,0:T(8,128)(2,1)}, bf16[2,64,2048]{2,1,0:T(8,128)(2,1)}, u32[]{:S(2)}, u32[]{:S(2)}) collective-permute-start(bf16[2,64,2048]{2,1,0:T(8,128)(2,1)} %slice.261), channel_id=1, source_target_pairs={{0,16},{16,0},{1,17},{17,1},{2,18},{18,2},{3,19},{19,3},{4,20},{20... | collective-permute-start | bytes 1572872 | tf_op jit(solution)/shard_map/out_in/ppermute | solution.py:298
  166.8 19.1 %collective-permute-start.22 = (bf16[512,2048]{1,0:T(8,128)(2,1)S(1)}, bf16[512,2048]{1,0:T(8,128)(2,1)S(1)}, u32[]{:S(2)}, u32[]{:S(2)}) collective-permute-start(bf16[512,2048]{1,0:T(8,128)(2,1)S(1)} %bitcast.250), channel_id=1, source_target_pairs={{0,8},{8,0},{1,9},{9,1},{2,10},{10,2},{3,11},{11,3},{4,12},{12,4},... | collective-permute-start | bytes 6291464 | tf_op jit(solution)/shard_map/out_in/ppermute | solution.py:773
  167.2 20.1 %collective-permute-start.21 = (bf16[512,2048]{1,0:T(8,128)(2,1)}, bf16[512,2048]{1,0:T(8,128)(2,1)}, u32[]{:S(2)}, u32[]{:S(2)}) collective-permute-start(bf16[512,2048]{1,0:T(8,128)(2,1)} %bitcast.251), channel_id=1, source_target_pairs={{0,8},{8,0},{1,9},{9,1},{2,10},{10,2},{3,11},{11,3},{4,12},{12,4},... | collective-permute-start | bytes 6291464 | tf_op jit(solution)/shard_map/out_in/ppermute | solution.py:773
  167.4 47.5 %collective-permute-start.23 = (bf16[8,64,1536]{2,1,0:T(8,128)(2,1)}, bf16[8,64,1536]{2,1,0:T(8,128)(2,1)}, u32[]{:S(2)}, u32[]{:S(2)}) collective-permute-start(bf16[8,64,1536]{2,1,0:T(8,128)(2,1)} %all-to-all-done.2.refs_0_), channel_id=1, source_target_pairs={{0,16},{16,0},{1,17},{17,1},{2,18},{18,2},{3,19},{19,3},{4,20},{20... | collective-permute-start | bytes 4718600 | tf_op jit(solution)/shard_map/gate_up_in/ppermute | solution.py:298
  168.9 46.0 %collective-permute-start.24 = (bf16[8,64,1536]{2,1,0:T(8,128)(2,1)}, bf16[8,64,1536]{2,1,0:T(8,128)(2,1)}, u32[]{:S(2)}, u32[]{:S(2)}) collective-permute-start(bf16[8,64,1536]{2,1,0:T(8,128)(2,1)} %all-to-all-done.2.refs_0_), channel_id=1, source_target_pairs={{0,1},{1,0},{2,3},{3,2},{4,5},{5,4},{6,7},{7,6},{8,9},{9,8},{10,11... | collective-permute-start | bytes 4718600 | tf_op jit(solution)/shard_map/gate_up_in/ppermute | solution.py:298
  187.3 23.2 %collective-permute-start.25 = (bf16[128,2048]{1,0:T(8,128)(2,1)}, bf16[128,2048]{1,0:T(8,128)(2,1)S(1)}, u32[]{:S(2)}, u32[]{:S(2)}) collective-permute-start(bf16[128,2048]{1,0:T(8,128)(2,1)} %collective-permute-done.19.refs_2_), channel_id=1, source_target_pairs={{0,4},{4,6},{6,2},{2,0},{1,5},{5,7},{7,3},{3,1},{8,12},{12,14},{14... | collective-permute-start | bytes 1572872 | tf_op jit(solution)/shard_map/out_grad_in/ppermute | solution.py:265
  187.3 54.3 %all-to-all-start.3 = ((bf16[8,64,768]{2,1,0:T(8,128)(2,1)}), bf16[8,64,768]{2,1,0:T(8,128)(2,1)S(1)}, u32[]{:S(2)}, u32[]{:S(2)}) async-start(bf16[8,64,768]{2,1,0:T(8,128)(2,1)} %copy-done.47), calls=%async_computation.3 | async-start | bytes 1572864 | tf_op jit(solution)/shard_map/down_in/all_to_all | solution.py:770
  235.3 30.0 %collective-permute-start.26 = (bf16[512,2048]{1,0:T(8,128)(2,1)S(1)}, bf16[512,2048]{1,0:T(8,128)(2,1)}, u32[]{:S(2)}, u32[]{:S(2)}) collective-permute-start(bf16[512,2048]{1,0:T(8,128)(2,1)S(1)} %copy-done.10), channel_id=1, source_target_pairs={{0,8},{8,0},{1,9},{9,1},{2,10},{10,2},{3,11},{11,3},{4,12},{12,4},... | collective-permute-start | bytes 6291464 | tf_op jit(solution)/shard_map/out_grad_core/ppermute | solution.py:773
  241.6 20.0 %collective-permute-start.29 = (bf16[8,64,768]{2,1,0:T(8,128)(2,1)S(1)}, bf16[8,64,768]{2,1,0:T(8,128)(2,1)S(1)}, u32[]{:S(2)}, u32[]{:S(2)}) collective-permute-start(bf16[8,64,768]{2,1,0:T(8,128)(2,1)S(1)} %all-to-all-done.3.refs_0_), channel_id=1, source_target_pairs={{0,16},{16,0},{1,17},{17,1},{2,18},{18,2},{3,19},{19,3},{4,20},{20... | collective-permute-start | bytes 2359304 | tf_op jit(solution)/shard_map/down_in/ppermute | solution.py:298
  243.2 19.6 %collective-permute-start.30 = (bf16[8,64,768]{2,1,0:T(8,128)(2,1)S(1)}, bf16[8,64,768]{2,1,0:T(8,128)(2,1)S(1)}, u32[]{:S(2)}, u32[]{:S(2)}) collective-permute-start(bf16[8,64,768]{2,1,0:T(8,128)(2,1)S(1)} %all-to-all-done.3.refs_0_), channel_id=1, source_target_pairs={{0,1},{1,0},{2,3},{3,2},{4,5},{5,4},{6,7},{7,6},{8,9},{9,8},{10,11... | collective-permute-start | bytes 2359304 | tf_op jit(solution)/shard_map/down_in/ppermute | solution.py:298
  312.9 25.7 %collective-permute-start.38 = (bf16[128,4096]{1,0:T(8,128)(2,1)S(1)}, bf16[128,4096]{1,0:T(8,128)(2,1)S(1)}, u32[]{:S(2)}, u32[]{:S(2)}) collective-permute-start(bf16[128,4096]{1,0:T(8,128)(2,1)S(1)} %add_convert_fusion.2), channel_id=1, source_target_pairs={{0,4},{4,6},{6,2},{2,0},{1,5},{5,7},{7,3},{3,1},{8,12},{12,14},{14... | collective-permute-start | bytes 3145736 | tf_op jit(solution)/shard_map/parts_out/ppermute | solution.py:283
  334.3 53.6 %collective-permute-start.41 = (bf16[8,2,64,1152]{3,2,0,1:T(8,128)(2,1)}, bf16[8,2,64,1152]{3,2,0,1:T(8,128)(2,1)S(1)}, u32[]{:S(2)}, u32[]{:S(2)}) collective-permute-start(bf16[8,2,64,1152]{3,2,0,1:T(8,128)(2,1)} %copy.68), channel_id=1, source_target_pairs={{0,16},{16,0},{1,17},{17,1},{2,18},{18,2},{3,19},{19,3},{4,20},{20... | collective-permute-start | bytes 7077896 | tf_op jit(solution)/shard_map/ffn_grad/ppermute | solution.py:419
  340.2 25.9 %collective-permute-start.39 = (bf16[128,4096]{1,0:T(8,128)(2,1)S(1)}, bf16[128,4096]{1,0:T(8,128)(2,1)}, u32[]{:S(2)}, u32[]{:S(2)}) collective-permute-start(bf16[128,4096]{1,0:T(8,128)(2,1)S(1)} %add_convert_fusion.1), channel_id=1, source_target_pairs={{0,4},{4,6},{6,2},{2,0},{1,5},{5,7},{7,3},{3,1},{8,12},{12,14},{14... | collective-permute-start | bytes 3145736 | tf_op jit(solution)/shard_map/parts_out/ppermute | solution.py:283
  346.8 41.1 %collective-permute-start.42 = (bf16[2,8,64,384]{3,2,1,0:T(8,128)(2,1)}, bf16[2,8,64,384]{3,2,1,0:T(8,128)(2,1)S(1)}, u32[]{:S(2)}, u32[]{:S(2)}) collective-permute-start(bf16[2,8,64,384]{3,2,1,0:T(8,128)(2,1)} %dynamic-slice_bitcast_fusion.4), channel_id=1, source_target_pairs={{0,1},{1,0},{2,3},{3,2},{4,5},{5,4},{6,7},{7,6},{8,9},{9,8},{10,11... | collective-permute-start | bytes 2359304 | tf_op jit(solution)/shard_map/ffn_grad/ppermute | solution.py:430
  347.7 51.9 %collective-permute-start.43 = (bf16[2,8,64,768]{3,2,1,0:T(8,128)(2,1)}, bf16[2,8,64,768]{3,2,1,0:T(8,128)(2,1)S(1)}, u32[]{:S(2)}, u32[]{:S(2)}) collective-permute-start(bf16[2,8,64,768]{3,2,1,0:T(8,128)(2,1)} %dynamic-slice_bitcast_fusion.1), channel_id=1, source_target_pairs={{0,1},{1,0},{2,3},{3,2},{4,5},{5,4},{6,7},{7,6},{8,9},{9,8},{10,11... | collective-permute-start | bytes 4718600 | tf_op jit(solution)/shard_map/ffn_grad/ppermute | solution.py:430
  368.5 41.5 %collective-permute-start.40 = (bf16[128,4096]{1,0:T(8,128)(2,1)S(1)}, bf16[128,4096]{1,0:T(8,128)(2,1)S(1)}, u32[]{:S(2)}, u32[]{:S(2)}) collective-permute-start(bf16[128,4096]{1,0:T(8,128)(2,1)S(1)} %add_convert_fusion), channel_id=1, source_target_pairs={{0,4},{4,6},{6,2},{2,0},{1,5},{5,7},{7,3},{3,1},{8,12},{12,14},{14... | collective-permute-start | bytes 3145736 | tf_op jit(solution)/shard_map/parts_out/ppermute | solution.py:283
  402.3 26.8 %collective-permute-start.45 = (bf16[8,64,768]{2,1,0:T(8,128)(2,1)}, bf16[8,64,768]{2,1,0:T(8,128)(2,1)}, u32[]{:S(2)}, u32[]{:S(2)}) collective-permute-start(bf16[8,64,768]{2,1,0:T(8,128)(2,1)} %slice_bitcast_fusion), channel_id=1, source_target_pairs={{0,16},{16,0},{1,17},{17,1},{2,18},{18,2},{3,19},{19,3},{4,20},{20... | collective-permute-start | bytes 2359304 | tf_op jit(solution)/shard_map/ffn_grad/ppermute | solution.py:419
  403.0 28.8 %collective-permute-start.44 = (bf16[8,64,1152]{2,1,0:T(8,128)(2,1)}, bf16[8,64,1152]{2,1,0:T(8,128)(2,1)}, u32[]{:S(2)}, u32[]{:S(2)}) collective-permute-start(bf16[8,64,1152]{2,1,0:T(8,128)(2,1)} %dynamic-slice_bitcast_fusion.2), channel_id=1, source_target_pairs={{0,1},{1,0},{2,3},{3,2},{4,5},{5,4},{6,7},{7,6},{8,9},{9,8},{10,11... | collective-permute-start | bytes 3538952 | tf_op jit(solution)/shard_map/ffn_grad/ppermute | solution.py:430
  406.2 22.9 %collective-permute-start.46 = (bf16[8,64,384]{2,1,0:T(8,128)(2,1)S(1)}, bf16[8,64,384]{2,1,0:T(8,128)(2,1)}, u32[]{:S(2)}, u32[]{:S(2)}) collective-permute-start(bf16[8,64,384]{2,1,0:T(8,128)(2,1)S(1)} %slice_bitcast_fusion.1), channel_id=1, source_target_pairs={{0,16},{16,0},{1,17},{17,1},{2,18},{18,2},{3,19},{19,3},{4,20},{20... | collective-permute-start | bytes 1179656 | tf_op jit(solution)/shard_map/ffn_grad/ppermute | solution.py:419
  423.0 16.8 %all-to-all-start.4 = ((bf16[8,128,256]{2,1,0:T(8,128)(2,1)}), bf16[8,128,256]{2,1,0:T(8,128)(2,1)}, u32[]{:S(2)}, u32[]{:S(2)}) async-start(bf16[8,128,256]{2,1,0:T(8,128)(2,1)} %bitcast.279), calls=%async_computation.4 | async-start | bytes 1048576 | tf_op jit(solution)/shard_map/heads_in/all_to_all | solution.py:770
  439.8 58.0 %all-to-all-start.5 = ((bf16[8,64,2304]{2,1,0:T(8,128)(2,1)}), bf16[8,64,2304]{2,1,0:T(8,128)(2,1)S(1)}, u32[]{:S(2)}, u32[]{:S(2)}) async-start(bf16[8,64,2304]{2,1,0:T(8,128)(2,1)} %pad_maximum_fusion.4), calls=%async_computation.5 | async-start | bytes 4718592 | tf_op jit(solution)/shard_map/ffn_back/all_to_all | solution.py:770
  479.9 31.5 %collective-permute-start.49 = (bf16[512,768]{1,0:T(8,128)(2,1)}, bf16[512,768]{1,0:T(8,128)(2,1)}, u32[]{:S(2)}, u32[]{:S(2)}) collective-permute-start(bf16[512,768]{1,0:T(8,128)(2,1)} %dynamic-slice_bitcast_fusion.3), channel_id=1, source_target_pairs={{0,16},{16,0},{1,17},{17,1},{2,18},{18,2},{3,19},{19,3},{4,20},{20... | collective-permute-start | bytes 2359304 | tf_op jit(solution)/shard_map/qkv_back/ppermute | solution.py:306
  482.8 21.2 %collective-permute-start.51 = (bf16[64,2048]{1,0:T(8,128)(2,1)S(1)}, bf16[64,2048]{1,0:T(8,128)(2,1)}, u32[]{:S(2)}, u32[]{:S(2)}) collective-permute-start(bf16[64,2048]{1,0:T(8,128)(2,1)S(1)} %get-tuple-element.526), channel_id=1, source_target_pairs={{2,0},{4,2},{6,4},{7,6},{5,7},{3,5},{1,3},{0,1},{10,8},{12,10},{14... | collective-permute-start | bytes 786440 | tf_op jit(solution)/shard_map/normed_out/ppermute | solution.py:192
  506.3 18.8 %collective-permute-start.56 = (bf16[128,2048]{1,0:T(8,128)(2,1)}, bf16[128,2048]{1,0:T(8,128)(2,1)}, u32[]{:S(2)}, u32[]{:S(2)}) collective-permute-start(bf16[128,2048]{1,0:T(8,128)(2,1)} %get-tuple-element.531), channel_id=1, source_target_pairs={{0,2},{2,4},{4,6},{6,7},{7,5},{5,3},{3,1},{1,0},{8,10},{10,12},{12... | collective-permute-start | bytes 1572872 | tf_op jit(solution)/shard_map/normed_out/ppermute | solution.py:192
  506.9 18.2 %collective-permute-start.57 = (bf16[128,2048]{1,0:T(8,128)(2,1)S(1)}, bf16[128,2048]{1,0:T(8,128)(2,1)}, u32[]{:S(2)}, u32[]{:S(2)}) collective-permute-start(bf16[128,2048]{1,0:T(8,128)(2,1)S(1)} %get-tuple-element.537), channel_id=1, source_target_pairs={{2,0},{4,2},{6,4},{7,6},{5,7},{3,5},{1,3},{0,1},{10,8},{12,10},{14... | collective-permute-start | bytes 1572872 | tf_op jit(solution)/shard_map/normed_out/ppermute | solution.py:192
  510.9 21.3 %collective-permute-start.53 = (bf16[128,512]{1,0:T(8,128)(2,1)S(1)}, bf16[128,512]{1,0:T(8,128)(2,1)S(1)}, u32[]{:S(2)}, u32[]{:S(2)}) collective-permute-start(bf16[128,512]{1,0:T(8,128)(2,1)S(1)} %bitcast.289), channel_id=1, source_target_pairs={{0,6},{2,0},{4,2},{6,4},{1,7},{3,1},{5,3},{7,5},{8,14},{10,8},{12,... | collective-permute-start | bytes 393224 | tf_op jit(solution)/shard_map/grad_attn_in/ppermute | solution.py:306
  511.4 20.7 %collective-permute-start.54 = (bf16[128,512]{1,0:T(8,128)(2,1)S(1)}, bf16[128,512]{1,0:T(8,128)(2,1)S(1)}, u32[]{:S(2)}, u32[]{:S(2)}) collective-permute-start(bf16[128,512]{1,0:T(8,128)(2,1)S(1)} %bitcast.290), channel_id=1, source_target_pairs={{0,4},{2,6},{4,0},{6,2},{1,5},{3,7},{5,1},{7,3},{8,12},{10,14},{12... | collective-permute-start | bytes 393224 | tf_op jit(solution)/shard_map/grad_attn_in/ppermute | solution.py:306
  534.0 24.3 %collective-permute-start.59 = (bf16[2,4,2,64,512]{4,3,1,2,0:T(8,128)(2,1)S(1)}, bf16[2,4,2,64,512]{4,3,1,2,0:T(8,128)(2,1)S(1)}, u32[]{:S(2)}, u32[]{:S(2)}) collective-permute-start(bf16[2,4,2,64,512]{4,3,1,2,0:T(8,128)(2,1)S(1)} %bitcast.283), channel_id=1, source_target_pairs={{0,8},{8,0},{1,9},{9,1},{2,10},{10,2},{3,11},{11,3},{4,12},{12,4},... | collective-permute-start | bytes 3145736 | tf_op jit(solution)/shard_map/out_back/ppermute | solution.py:306
  534.1 18.6 %collective-permute-start.61 = (bf16[128,2048]{1,0:T(8,128)(2,1)}, bf16[128,2048]{1,0:T(8,128)(2,1)}, u32[]{:S(2)}, u32[]{:S(2)}) collective-permute-start(bf16[128,2048]{1,0:T(8,128)(2,1)} %get-tuple-element.551), channel_id=1, source_target_pairs={{2,0},{4,2},{6,4},{7,6},{5,7},{3,5},{1,3},{0,1},{10,8},{12,10},{14... | collective-permute-start | bytes 1572872 | tf_op jit(solution)/shard_map/normed_out/ppermute | solution.py:192
  536.1 30.5 %all-to-all-start.6 = ((bf16[8,64,768]{2,1,0:T(8,128)(2,1)}), bf16[8,64,768]{2,1,0:T(8,128)(2,1)}, u32[]{:S(2)}, u32[]{:S(2)}) async-start(bf16[8,64,768]{2,1,0:T(8,128)(2,1)} %bitcast.92), calls=%async_computation.6 | async-start | bytes 1572864 | tf_op jit(solution)/shard_map/qkv_back/all_to_all | solution.py:770
  555.6 22.4 %collective-permute-start.64 = (bf16[128,2048]{1,0:T(8,128)(2,1)}, bf16[128,2048]{1,0:T(8,128)(2,1)}, u32[]{:S(2)}, u32[]{:S(2)}) collective-permute-start(bf16[128,2048]{1,0:T(8,128)(2,1)} %get-tuple-element.554), channel_id=1, source_target_pairs={{0,2},{2,4},{4,6},{6,7},{7,5},{5,3},{3,1},{1,0},{8,10},{10,12},{12... | collective-permute-start | bytes 1572872 | tf_op jit(solution)/shard_map/normed_out/ppermute | solution.py:192
  555.6 22.6 %collective-permute-start.65 = (bf16[128,2048]{1,0:T(8,128)(2,1)}, bf16[128,2048]{1,0:T(8,128)(2,1)}, u32[]{:S(2)}, u32[]{:S(2)}) collective-permute-start(bf16[128,2048]{1,0:T(8,128)(2,1)} %get-tuple-element.558), channel_id=1, source_target_pairs={{2,0},{4,2},{6,4},{7,6},{5,7},{3,5},{1,3},{0,1},{10,8},{12,10},{14... | collective-permute-start | bytes 1572872 | tf_op jit(solution)/shard_map/normed_out/ppermute | solution.py:192
  559.6 22.5 %collective-permute-start.63 = (bf16[4,64,512]{2,1,0:T(8,128)(2,1)}, bf16[4,64,512]{2,1,0:T(8,128)(2,1)S(1)}, u32[]{:S(2)}, u32[]{:S(2)}) collective-permute-start(bf16[4,64,512]{2,1,0:T(8,128)(2,1)} %get-tuple-element.613), channel_id=1, source_target_pairs={{0,1},{1,0},{16,17},{17,16},{2,3},{3,2},{18,19},{19,18},{4,5},{5,4... | collective-permute-start | bytes 786440 | tf_op jit(solution)/shard_map/out_back/ppermute | solution.py:391
  561.6 20.5 %collective-permute-start.66 = (bf16[4,64,512]{2,1,0:T(8,128)(2,1)}, bf16[4,64,512]{2,1,0:T(8,128)(2,1)}, u32[]{:S(2)}, u32[]{:S(2)}) collective-permute-start(bf16[4,64,512]{2,1,0:T(8,128)(2,1)} %get-tuple-element.615), channel_id=1, source_target_pairs={{0,16},{1,17},{16,0},{17,1},{2,18},{3,19},{18,2},{19,3},{4,20},{5,... | collective-permute-start | bytes 786440 | tf_op jit(solution)/shard_map/out_back/ppermute | solution.py:391
  562.2 19.8 %collective-permute-start.67 = (bf16[4,64,512]{2,1,0:T(8,128)(2,1)}, bf16[4,64,512]{2,1,0:T(8,128)(2,1)}, u32[]{:S(2)}, u32[]{:S(2)}) collective-permute-start(bf16[4,64,512]{2,1,0:T(8,128)(2,1)} %get-tuple-element.614), channel_id=1, source_target_pairs={{0,17},{1,16},{16,1},{17,0},{2,19},{3,18},{18,3},{19,2},{4,21},{5,... | collective-permute-start | bytes 786440 | tf_op jit(solution)/shard_map/out_back/ppermute | solution.py:391
  (101 other events, 1150.1 us)

commit v5 on v4

--- a/solution.py
+++ b/solution.py
@@ -721,8 +721,8 @@
     "gate_up_in", "second_norm", "normed_core", "gate_up_in", "down_in", "down_in", "normed_core",
     "out_grad_core", "gate_up", "down_in", "out_grad_core", "down_in", "act", "other_parts", "own_parts",
     "other_parts", "parts_out", "first_share", "second_share", "ffn_grad", "parts_out", "parts_out",
-    "ffn_grad", "parts_out", "second_back", "heads_in", "ffn_grad", "heads_in", "ffn_back", "attend_back",
-    "qkv_back", "first_back", "normed_out", "qkv_back", "small", "grad_attn_in", "ffn_back", "normed_out",
+    "ffn_grad", "parts_out", "second_back", "heads_in", "ffn_grad", "heads_in", "ffn_back", "grad_attn_in",
+    "attend_back", "qkv_back", "first_back", "normed_out", "qkv_back", "small", "ffn_back", "normed_out",
     "qkv_back", "small", "ffn_rows", "normed_out", "grad_attn_in", "out_back", "small", "normed_out",
     "out_back", "small", "qkv_back", "qkv_rows", "normed_out", "out_back", "small", "output",
     "first_norm_tokens", "small", "out_back", "out_rows",

time: 613 us -> 613 us (level)
    unnamed x180 -> x184, local copies, waits for them, and re-layouts: 15.3 us -> 15.3 us
where the time goes in v5:
time: 613 us; the launch traced here: 603 us
  waiting for transfers between devices  186 us (30%)
  starting transfers between devices  115 us (19%)
  Pallas kernels  115 us (19%)
  local copies, waits for them, and re-layouts  77.9 us (13%)
  matrix products  52.8 us (9%)
  other arithmetic  52.5 us (9%)
    pallas_call x5, Pallas kernels, over_rows(): pl.pallas_call(kernel, grid_spec=pltpu.PrefetchScalarGridSpec(num_scalar_...  49.8 us
    ppermute x16, waiting for transfers between devices, send(): lax.ppermute(values, GROUP, self.forward if forward else self.backward)  44.6 us
    ppermute x6, waiting for transfers between devices, gather(): moved = lax.ppermute(moved, 'z', self.cycle)  41.2 us
    all_to_all x7, starting transfers between devices, all_to_all(): return lax.all_to_all(values, axes, split_axis=0, concat_axis=0, tiled=True)  33.4 us
    pallas_call x7, Pallas kernels, assemble(): pl.pallas_call(kernel, grid_spec=pltpu.PrefetchScalarGridSpec(num_scalar_...  28.9 us
    all_to_all x7, waiting for transfers between devices, all_to_all(): return lax.all_to_all(values, axes, split_axis=0, concat_axis=0, tiled=True)  28.1 us
    ppermute x16, starting transfers between devices, send(): lax.ppermute(values, GROUP, self.forward if forward else self.backward)  21.7 us
    ppermute x3, waiting for transfers between devices, scatter(): moved = lax.ppermute(moved, 'z', self.cycle)  20.9 us
  transfers between devices with their start and end apart: 79, of which 33 were waited for; matrix products, arithmetic and copies ran while one was open for 24% of the time, Pallas kernels for 18%

profile of v5, /device:TPU:0, one launch (start us, length us, event | category | flops | bytes accessed | tf_op | source)
XLA Modules:
  0.0 602.6 jit_solution(15500412935302313000)
XLA Ops:
  7.1 6.4 %all-to-all-start = ((bf16[8,64,768]{2,1,0:T(8,128)(2,1)}), bf16[8,64,768]{2,1,0:T(8,128)(2,1)S(1)}, u32[]{:S(2)}, u32[]{:S(2)}) async-start(bf16[8,64,768]{2,1,0:T(8,128)(2,1)} %reshape.208), calls=%async_computation | async-start | bytes 1572864 | tf_op jit(solution)/shard_map/qkv_in/all_to_all | solution.py:770
  24.1 14.9 %collective-permute-done.2 = bf16[128,2048]{1,0:T(8,128)(2,1)} collective-permute-done((bf16[128,2048]{1,0:T(8,128)(2,1)S(1)}, bf16[128,2048]{1,0:T(8,128)(2,1)}, u32[]{:S(2)}, u32[]{:S(2)}) %collective-permute-start.2) | collective-permute-done | bytes 524320 | tf_op jit(solution)/shard_map/tokens_in/ppermute | solution.py:192
  41.3 5.8 collective-permute-start.4
  58.4 5.1 collective-permute-done.5
  84.8 7.2 %all-to-all-start.2 = ((bf16[8,64,1536]{2,1,0:T(8,128)(2,1)}), bf16[8,64,1536]{2,1,0:T(8,128)(2,1)}, u32[]{:S(2)}, u32[]{:S(2)}) async-start(bf16[8,64,1536]{2,1,0:T(8,128)(2,1)} %pad_maximum_fusion.5), calls=%async_computation.2 | async-start | bytes 3145728 | tf_op jit(solution)/shard_map/gate_up_in/all_to_all | solution.py:770
  97.1 12.0 %project.1 = (bf16[1024,2048]{1,0:T(8,128)(2,1)}, bf16[1024,768]{1,0:T(8,128)(2,1)}) custom-call(s32[4]{0:T(128)} %pad_add_fusion.1.places_ref, bf16[1024,2048]{1,0:T(8,128)(2,1)} %constant_dynamic-update-slice_fusion.9.refs_0_.refs_3_, f32[1024,128]{1,0:T(8,128)} %pad_maximum_fusion.6.refs_1_.cos_ref.all_cos_ref, ...), custom_call_target="tpu_custom_call" | custom-call | tf_op jit(solution)/shard_map/project/project/pallas_call | solution.py:669
  113.2 9.5 %attend_forward.1 = (bf16[1024,256]{1,0:T(8,128)(2,1)}, f32[2,1024,1]{2,1,0:T(8,128)}) custom-call(bf16[1024,768]{1,0:T(8,128)(2,1)} %get-tuple-element.482.q_ref.k_ref.v_ref, bf16[1024,768]{1,0:T(8,128)(2,1)} %get-tuple-element.482.q_ref.k_ref.v_ref, bf16[1024,768]{1,0:T(8,128)(2,1)} %get-tuple-element.482.q_ref.k_ref.v_ref, s32[1024,1]{1,0:T(8,128)} %copy.63.low_ref, ...), custom_call_target="tpu_custom_call" | custom-call | tf_op jit(solution)/shard_map/attend/attend_forward/pallas_call | solution.py:608
  124.0 7.5 %collective-permute-done.12.refs_1_ = bf16[128,2048]{1,0:T(8,128)(2,1)} collective-permute-done((bf16[128,2048]{1,0:T(8,128)(2,1)S(1)}, bf16[128,2048]{1,0:T(8,128)(2,1)}, u32[]{:S(2)}, u32[]{:S(2)}) %collective-permute-start.12) | collective-permute-done | bytes 524320 | tf_op jit(solution)/shard_map/out_grad_in/ppermute | solution.py:265
  143.1 6.1 %collective-permute-done.13.refs_1_ = bf16[512,512]{1,0:T(8,128)(2,1)S(1)} collective-permute-done((bf16[512,512]{1,0:T(8,128)(2,1)S(1)}, bf16[512,512]{1,0:T(8,128)(2,1)S(1)}, u32[]{:S(2)}, u32[]{:S(2)}) %collective-permute-start.13) | collective-permute-done | bytes 524320 | tf_op jit(solution)/shard_map/attended_in/ppermute | solution.py:265
  149.2 3.6 assemble.7
  152.8 10.4 %all-to-all-done.2.refs_0_ = bf16[8,64,1536]{2,1,0:T(8,128)(2,1)} async-done(((bf16[8,64,1536]{2,1,0:T(8,128)(2,1)}), bf16[8,64,1536]{2,1,0:T(8,128)(2,1)}, u32[]{:S(2)}, u32[]{:S(2)}) %all-to-all-start.2) | async-done | bytes 1572896 | tf_op jit(solution)/shard_map/gate_up_in/all_to_all | solution.py:770
  171.7 12.7 %collective-permute-done.16.refs_2_ = bf16[512,512]{1,0:T(8,128)(2,1)S(1)} collective-permute-done((bf16[512,512]{1,0:T(8,128)(2,1)S(1)}, bf16[512,512]{1,0:T(8,128)(2,1)S(1)}, u32[]{:S(2)}, u32[]{:S(2)}) %collective-permute-start.16) | collective-permute-done | bytes 524320 | tf_op jit(solution)/shard_map/attended_in/ppermute | solution.py:265
  187.3 4.1 all-to-all-start.3
  192.0 7.4 %collective-permute-done.20.refs_3_ = bf16[512,512]{1,0:T(8,128)(2,1)} collective-permute-done((bf16[512,512]{1,0:T(8,128)(2,1)S(1)}, bf16[512,512]{1,0:T(8,128)(2,1)}, u32[]{:S(2)}, u32[]{:S(2)}) %collective-permute-start.20) | collective-permute-done | bytes 524320 | tf_op jit(solution)/shard_map/attended_in/ppermute | solution.py:265
  199.4 3.6 assemble.9.refs_1_
  203.0 7.5 %collective-permute-done.25.refs_3_ = bf16[128,2048]{1,0:T(8,128)(2,1)S(1)} collective-permute-done((bf16[128,2048]{1,0:T(8,128)(2,1)}, bf16[128,2048]{1,0:T(8,128)(2,1)S(1)}, u32[]{:S(2)}, u32[]{:S(2)}) %collective-permute-start.25) | collective-permute-done | bytes 524320 | tf_op jit(solution)/shard_map/out_grad_in/ppermute | solution.py:265
  211.3 3.6 assemble.10
  220.5 12.3 %second_norm.1 = (f32[512,2048]{1,0:T(8,128)}, bf16[512,512]{1,0:T(8,128)(2,1)}, bf16[512,512]{1,0:T(8,128)(2,1)}, bf16[512,512]{1,0:T(8,128)(2,1)}, bf16[512,512]{1,0:T(8,128)(2,1)}) custom-call(s32[7]{0:T(128)} %concatenate.59.places_ref, bf16[1024,2048]{1,0:T(8,128)(2,1)} %constant_dynamic-update-slice_fusion.9.refs_0_.refs_3_, ...), custom_call_target="tpu_custom_call" | custom-call | tf_op jit(solution)/shard_map/second_norm/second_norm/pallas_call | solution.py:669
  235.4 6.1 %assemble.11 = bf16[2,8,2,64,1536]{4,3,2,1,0:T(8,128)(2,1)} custom-call(s32[2]{0:T(128)} %pad_add_fusion.2.places_ref, bf16[8,64,1536]{2,1,0:T(8,128)(2,1)} %all-to-all-done.2.refs_0_, bf16[8,64,1536]{2,1,0:T(8,128)(2,1)} %collective-permute-done.24.refs_1_, bf16[8,64,1536]{2,1,0:T(8,128)(2,1)} %collective-permute-done.23.refs_2_, ...), custom_call_target="tpu_custom_call" | custom-call | tf_op jit(solution)/shard_map/gate_up_in/assemble/pallas_call | solution.py:543
  244.9 4.3 assemble.12
  249.2 11.7 %convolution_add_fusion = f32[1024,1536]{1,0:T(8,128)} fusion(bf16[1024,2048]{1,0:T(8,128)(2,1)} %assemble.12, bf16[2048,1536]{1,0:T(8,128)(2,1)} %bitcast.260, f32[1536]{0:T(1024)S(1)} %pad_maximum_fusion.9), kind=kOutput, calls=%fused_computation.8 | convolution fusion | flops 6444023808 | bytes 16783360 | tf_op jit(solution)/shard_map/gate_up/dot_general | solution.py:95
  267.4 5.9 collective-permute-done.35.refs_3_
  275.5 4.2 assemble.13
  279.8 8.9 %fusion.4 = (bf16[1024,768]{1,0:T(8,128)(2,1)S(1)}, bf16[1024,768]{1,0:T(8,128)(2,1)S(1)}, bf16[1024,768]{1,0:T(8,128)(2,1)S(1)}) fusion(f32[1024,1536]{1,0:T(8,128)} %convolution_add_fusion, bf16[1024,2048]{1,0:T(8,128)(2,1)S(1)} %pad_maximum_fusion, bf16[2048,768]{1,0:T(8,128)(2,1)} %bitcast.271), kind=kOutput, calls=%fused_computation.17 | convolution fusion | flops 3244818432 | bytes 18350080 | tf_op jit(solution)/shard_map/act/dot_general | solution.py:95
  295.2 4.1 convolution_convert_fusion.7
  301.5 4.1 convolution_convert_fusion.4
  306.0 3.7 convolution_convert_fusion.5
  315.4 5.9 convolution_convert_fusion
  324.0 3.7 convolution_convert_fusion.2
  340.2 3.6 collective-permute-start.39
  348.8 17.3 %collective-permute-done.39 = bf16[128,4096]{1,0:T(8,128)(2,1)} collective-permute-done((bf16[128,4096]{1,0:T(8,128)(2,1)S(1)}, bf16[128,4096]{1,0:T(8,128)(2,1)}, u32[]{:S(2)}, u32[]{:S(2)}) %collective-permute-start.39) | collective-permute-done | bytes 1048608 | tf_op jit(solution)/shard_map/parts_out/ppermute | solution.py:283
  372.0 15.9 %collective-permute-done.41 = bf16[8,2,64,1152]{3,2,0,1:T(8,128)(2,1)S(1)} collective-permute-done((bf16[8,2,64,1152]{3,2,0,1:T(8,128)(2,1)}, bf16[8,2,64,1152]{3,2,0,1:T(8,128)(2,1)S(1)}, u32[]{:S(2)}, u32[]{:S(2)}) %collective-permute-start.41) | collective-permute-done | bytes 2359328 | tf_op jit(solution)/shard_map/ffn_grad/ppermute | solution.py:419
  391.9 7.7 %collective-permute-done.43 = bf16[2,8,64,768]{3,2,1,0:T(8,128)(2,1)S(1)} collective-permute-done((bf16[2,8,64,768]{3,2,1,0:T(8,128)(2,1)}, bf16[2,8,64,768]{3,2,1,0:T(8,128)(2,1)S(1)}, u32[]{:S(2)}, u32[]{:S(2)}) %collective-permute-start.43) | collective-permute-done | bytes 1572896 | tf_op jit(solution)/shard_map/ffn_grad/ppermute | solution.py:430
  410.8 10.2 %second_norm_back.1 = (f32[128,2048]{1,0:T(8,128)}, bf16[128,2048]{1,0:T(8,128)(2,1)}, bf16[128,2048]{1,0:T(8,128)(2,1)}, f32[1,2048]{1,0:T(1,128)}, f32[1,2048]...) custom-call(s32[6]{0:T(128)} %pad_add_fusion.4.places_ref, bf16[128,4096]{1,0:T(8,128)(2,1)} %copy-done.33, ...), custom_call_target="tpu_custom_call" | custom-call | tf_op jit(solution)/shard_map/second_back/second_norm_back/pallas_call | solution.py:669
  422.9 4.1 all-to-all-start.4
  434.8 4.9 all-to-all-done.4
  439.7 3.8 all-to-all-start.5
  443.6 11.9 %attend_backward.1 = (bf16[1024,256]{1,0:T(8,128)(2,1)}, bf16[1024,256]{1,0:T(8,128)(2,1)}, bf16[1024,256]{1,0:T(8,128)(2,1)}) custom-call(bf16[1024,768]{1,0:T(8,128)(2,1)} %get-tuple-element.482.q_ref.k_ref.v_ref, bf16[1024,768]{1,0:T(8,128)(2,1)} %get-tuple-element.482.q_ref.k_ref.v_ref, bf16[1024,768]{1,0:T(8,128)(2,1)} %get-tuple-element.482.q_ref.k_ref.v_ref, ...), custom_call_target="tpu_custom_call" | custom-call | tf_op jit(solution)/shard_map/attend_back/attend_backward/pallas_call | solution.py:630
  455.5 5.1 convolution_convert_fusion.1
  464.1 11.6 %first_norm_back.1 = (bf16[1024,2048]{1,0:T(8,128)(2,1)}, f32[1,2048]{1,0:T(1,128)}, f32[1,2048]{1,0:T(1,128)}, f32[1,768]{1,0:T(1,128)}) custom-call(s32[4]{0:T(128)} %pad_add_fusion.1.places_ref, bf16[1024,256]{1,0:T(8,128)(2,1)} %get-tuple-element.496.refs_0_, bf16[1024,256]{1,0:T(8,128)(2,1)} %get-tuple-element.497.refs_1_, ...), custom_call_target="tpu_custom_call" | custom-call | tf_op jit(solution)/shard_map/first_back/first_norm_back/pallas_call | solution.py:669
  486.2 11.5 %all-to-all-done.5.refs_0_ = bf16[8,64,2304]{2,1,0:T(8,128)(2,1)S(1)} async-done(((bf16[8,64,2304]{2,1,0:T(8,128)(2,1)}), bf16[8,64,2304]{2,1,0:T(8,128)(2,1)S(1)}, u32[]{:S(2)}, u32[]{:S(2)}) %all-to-all-start.5) | async-done | bytes 2359328 | tf_op jit(solution)/shard_map/ffn_back/all_to_all | solution.py:770
  498.5 5.3 collective-permute-done.51
  536.1 4.2 all-to-all-start.6
  541.1 4.4 collective-permute-done.52
  569.0 8.9 %collective-permute-done.64.refs_0_ = bf16[128,2048]{1,0:T(8,128)(2,1)} collective-permute-done((bf16[128,2048]{1,0:T(8,128)(2,1)}, bf16[128,2048]{1,0:T(8,128)(2,1)}, u32[]{:S(2)}, u32[]{:S(2)}) %collective-permute-start.64) | collective-permute-done | bytes 524320 | tf_op jit(solution)/shard_map/normed_out/ppermute | solution.py:192
  578.2 3.8 collective-permute-done.63
  584.8 3.6 first_norm_tokens.1
  594.8 4.0 collective-permute-done.71
  (442 shorter events, 254.6 us)
Async XLA Ops:
  7.1 44.3 %all-to-all-start = ((bf16[8,64,768]{2,1,0:T(8,128)(2,1)}), bf16[8,64,768]{2,1,0:T(8,128)(2,1)S(1)}, u32[]{:S(2)}, u32[]{:S(2)}) async-start(bf16[8,64,768]{2,1,0:T(8,128)(2,1)} %reshape.208), calls=%async_computation | async-start | bytes 1572864 | tf_op jit(solution)/shard_map/qkv_in/all_to_all | solution.py:770
  18.8 20.2 %collective-permute-start.2 = (bf16[128,2048]{1,0:T(8,128)(2,1)S(1)}, bf16[128,2048]{1,0:T(8,128)(2,1)}, u32[]{:S(2)}, u32[]{:S(2)}) collective-permute-start(bf16[128,2048]{1,0:T(8,128)(2,1)S(1)} %collective-permute-done), channel_id=1, source_target_pairs={{0,2},{2,4},{4,6},{6,7},{7,5},{5,3},{3,1},{1,0},{8,10},{10,12},{12... | collective-permute-start | bytes 1572872 | tf_op jit(solution)/shard_map/tokens_in/ppermute | solution.py:192
  20.4 20.9 %collective-permute-start.3 = (bf16[128,2048]{1,0:T(8,128)(2,1)S(1)}, bf16[128,2048]{1,0:T(8,128)(2,1)}, u32[]{:S(2)}, u32[]{:S(2)}) collective-permute-start(bf16[128,2048]{1,0:T(8,128)(2,1)S(1)} %collective-permute-done.1), channel_id=1, source_target_pairs={{2,0},{4,2},{6,4},{7,6},{5,7},{3,5},{1,3},{0,1},{10,8},{12,10},{14... | collective-permute-start | bytes 1572872 | tf_op jit(solution)/shard_map/tokens_in/ppermute | solution.py:192
  41.3 17.1 %collective-permute-start.4 = (bf16[128,2048]{1,0:T(8,128)(2,1)}, bf16[128,2048]{1,0:T(8,128)(2,1)}, u32[]{:S(2)}, u32[]{:S(2)}) collective-permute-start(bf16[128,2048]{1,0:T(8,128)(2,1)} %collective-permute-done.2), channel_id=1, source_target_pairs={{0,2},{2,4},{4,6},{6,7},{7,5},{5,3},{3,1},{1,0},{8,10},{10,12},{12... | collective-permute-start | bytes 1572872 | tf_op jit(solution)/shard_map/tokens_in/ppermute | solution.py:192
  51.4 30.8 %collective-permute-start.8 = (bf16[512,768]{1,0:T(8,128)(2,1)S(1)}, bf16[512,768]{1,0:T(8,128)(2,1)S(1)}, u32[]{:S(2)}, u32[]{:S(2)}) collective-permute-start(bf16[512,768]{1,0:T(8,128)(2,1)S(1)} %bitcast.256), channel_id=1, source_target_pairs={{0,16},{16,0},{1,17},{17,1},{2,18},{18,2},{3,19},{19,3},{4,20},{20... | collective-permute-start | bytes 2359304 | tf_op jit(solution)/shard_map/qkv_in/ppermute | solution.py:298
  54.0 30.8 %all-to-all-start.1 = ((bf16[4,64,2048]{2,1,0:T(8,128)(2,1)}), bf16[4,64,2048]{2,1,0:T(8,128)(2,1)S(1)}, u32[]{:S(2)}, u32[]{:S(2)}) async-start(bf16[4,64,2048]{2,1,0:T(8,128)(2,1)} %broadcast_in_dim.7), calls=%async_computation.1 | async-start | bytes 2097152 | tf_op jit(solution)/shard_map/out_in/all_to_all | solution.py:770
  84.8 78.5 %all-to-all-start.2 = ((bf16[8,64,1536]{2,1,0:T(8,128)(2,1)}), bf16[8,64,1536]{2,1,0:T(8,128)(2,1)}, u32[]{:S(2)}, u32[]{:S(2)}) async-start(bf16[8,64,1536]{2,1,0:T(8,128)(2,1)} %pad_maximum_fusion.5), calls=%async_computation.2 | async-start | bytes 3145728 | tf_op jit(solution)/shard_map/gate_up_in/all_to_all | solution.py:770
  92.6 43.0 %collective-permute-start.14 = (bf16[4,64,2048]{2,1,0:T(8,128)(2,1)S(1)}, bf16[4,64,2048]{2,1,0:T(8,128)(2,1)}, u32[]{:S(2)}, u32[]{:S(2)}) collective-permute-start(bf16[4,64,2048]{2,1,0:T(8,128)(2,1)S(1)} %all-to-all-done.1.refs_0_), channel_id=1, source_target_pairs={{0,16},{16,0},{1,17},{17,1},{2,18},{18,2},{3,19},{19,3},{4,20},{20... | collective-permute-start | bytes 3145736 | tf_op jit(solution)/shard_map/out_in/ppermute | solution.py:298
  94.1 41.5 %collective-permute-start.15 = (bf16[4,64,2048]{2,1,0:T(8,128)(2,1)S(1)}, bf16[4,64,2048]{2,1,0:T(8,128)(2,1)}, u32[]{:S(2)}, u32[]{:S(2)}) collective-permute-start(bf16[4,64,2048]{2,1,0:T(8,128)(2,1)S(1)} %all-to-all-done.1.refs_0_), channel_id=1, source_target_pairs={{0,1},{1,0},{2,3},{3,2},{4,5},{5,4},{6,7},{7,6},{8,9},{9,8},{10,11... | collective-permute-start | bytes 3145736 | tf_op jit(solution)/shard_map/out_in/ppermute | solution.py:298
  109.2 22.3 %collective-permute-start.12 = (bf16[128,2048]{1,0:T(8,128)(2,1)S(1)}, bf16[128,2048]{1,0:T(8,128)(2,1)}, u32[]{:S(2)}, u32[]{:S(2)}) collective-permute-start(bf16[128,2048]{1,0:T(8,128)(2,1)S(1)} %pad_maximum_fusion.8.refs_0_), channel_id=1, source_target_pairs={{0,4},{4,6},{6,2},{2,0},{1,5},{5,7},{7,3},{3,1},{8,12},{12,14},{14... | collective-permute-start | bytes 1572872 | tf_op jit(solution)/shard_map/out_grad_in/ppermute | solution.py:265
  134.3 29.0 %collective-permute-start.19 = (bf16[128,2048]{1,0:T(8,128)(2,1)}, bf16[128,2048]{1,0:T(8,128)(2,1)}, u32[]{:S(2)}, u32[]{:S(2)}) collective-permute-start(bf16[128,2048]{1,0:T(8,128)(2,1)} %collective-permute-done.12.refs_1_), channel_id=1, source_target_pairs={{0,4},{4,6},{6,2},{2,0},{1,5},{5,7},{7,3},{3,1},{8,12},{12,14},{14... | collective-permute-start | bytes 1572872 | tf_op jit(solution)/shard_map/out_grad_in/ppermute | solution.py:265
  137.5 25.7 %collective-permute-start.17 = (bf16[2,64,2048]{2,1,0:T(8,128)(2,1)}, bf16[2,64,2048]{2,1,0:T(8,128)(2,1)}, u32[]{:S(2)}, u32[]{:S(2)}) collective-permute-start(bf16[2,64,2048]{2,1,0:T(8,128)(2,1)} %slice.260), channel_id=1, source_target_pairs={{0,1},{1,0},{2,3},{3,2},{4,5},{5,4},{6,7},{7,6},{8,9},{9,8},{10,11... | collective-permute-start | bytes 1572872 | tf_op jit(solution)/shard_map/out_in/ppermute | solution.py:298
  141.0 22.2 %collective-permute-start.18 = (bf16[2,64,2048]{2,1,0:T(8,128)(2,1)}, bf16[2,64,2048]{2,1,0:T(8,128)(2,1)}, u32[]{:S(2)}, u32[]{:S(2)}) collective-permute-start(bf16[2,64,2048]{2,1,0:T(8,128)(2,1)} %slice.261), channel_id=1, source_target_pairs={{0,16},{16,0},{1,17},{17,1},{2,18},{18,2},{3,19},{19,3},{4,20},{20... | collective-permute-start | bytes 1572872 | tf_op jit(solution)/shard_map/out_in/ppermute | solution.py:298
  166.8 19.1 %collective-permute-start.22 = (bf16[512,2048]{1,0:T(8,128)(2,1)S(1)}, bf16[512,2048]{1,0:T(8,128)(2,1)S(1)}, u32[]{:S(2)}, u32[]{:S(2)}) collective-permute-start(bf16[512,2048]{1,0:T(8,128)(2,1)S(1)} %bitcast.250), channel_id=1, source_target_pairs={{0,8},{8,0},{1,9},{9,1},{2,10},{10,2},{3,11},{11,3},{4,12},{12,4},... | collective-permute-start | bytes 6291464 | tf_op jit(solution)/shard_map/out_in/ppermute | solution.py:773
  167.2 20.1 %collective-permute-start.21 = (bf16[512,2048]{1,0:T(8,128)(2,1)}, bf16[512,2048]{1,0:T(8,128)(2,1)}, u32[]{:S(2)}, u32[]{:S(2)}) collective-permute-start(bf16[512,2048]{1,0:T(8,128)(2,1)} %bitcast.251), channel_id=1, source_target_pairs={{0,8},{8,0},{1,9},{9,1},{2,10},{10,2},{3,11},{11,3},{4,12},{12,4},... | collective-permute-start | bytes 6291464 | tf_op jit(solution)/shard_map/out_in/ppermute | solution.py:773
  167.4 47.5 %collective-permute-start.23 = (bf16[8,64,1536]{2,1,0:T(8,128)(2,1)}, bf16[8,64,1536]{2,1,0:T(8,128)(2,1)}, u32[]{:S(2)}, u32[]{:S(2)}) collective-permute-start(bf16[8,64,1536]{2,1,0:T(8,128)(2,1)} %all-to-all-done.2.refs_0_), channel_id=1, source_target_pairs={{0,16},{16,0},{1,17},{17,1},{2,18},{18,2},{3,19},{19,3},{4,20},{20... | collective-permute-start | bytes 4718600 | tf_op jit(solution)/shard_map/gate_up_in/ppermute | solution.py:298
  168.9 46.0 %collective-permute-start.24 = (bf16[8,64,1536]{2,1,0:T(8,128)(2,1)}, bf16[8,64,1536]{2,1,0:T(8,128)(2,1)}, u32[]{:S(2)}, u32[]{:S(2)}) collective-permute-start(bf16[8,64,1536]{2,1,0:T(8,128)(2,1)} %all-to-all-done.2.refs_0_), channel_id=1, source_target_pairs={{0,1},{1,0},{2,3},{3,2},{4,5},{5,4},{6,7},{7,6},{8,9},{9,8},{10,11... | collective-permute-start | bytes 4718600 | tf_op jit(solution)/shard_map/gate_up_in/ppermute | solution.py:298
  187.2 23.3 %collective-permute-start.25 = (bf16[128,2048]{1,0:T(8,128)(2,1)}, bf16[128,2048]{1,0:T(8,128)(2,1)S(1)}, u32[]{:S(2)}, u32[]{:S(2)}) collective-permute-start(bf16[128,2048]{1,0:T(8,128)(2,1)} %collective-permute-done.19.refs_2_), channel_id=1, source_target_pairs={{0,4},{4,6},{6,2},{2,0},{1,5},{5,7},{7,3},{3,1},{8,12},{12,14},{14... | collective-permute-start | bytes 1572872 | tf_op jit(solution)/shard_map/out_grad_in/ppermute | solution.py:265
  187.3 54.3 %all-to-all-start.3 = ((bf16[8,64,768]{2,1,0:T(8,128)(2,1)}), bf16[8,64,768]{2,1,0:T(8,128)(2,1)S(1)}, u32[]{:S(2)}, u32[]{:S(2)}) async-start(bf16[8,64,768]{2,1,0:T(8,128)(2,1)} %copy-done.47), calls=%async_computation.3 | async-start | bytes 1572864 | tf_op jit(solution)/shard_map/down_in/all_to_all | solution.py:770
  235.3 30.0 %collective-permute-start.26 = (bf16[512,2048]{1,0:T(8,128)(2,1)S(1)}, bf16[512,2048]{1,0:T(8,128)(2,1)}, u32[]{:S(2)}, u32[]{:S(2)}) collective-permute-start(bf16[512,2048]{1,0:T(8,128)(2,1)S(1)} %copy-done.10), channel_id=1, source_target_pairs={{0,8},{8,0},{1,9},{9,1},{2,10},{10,2},{3,11},{11,3},{4,12},{12,4},... | collective-permute-start | bytes 6291464 | tf_op jit(solution)/shard_map/out_grad_core/ppermute | solution.py:773
  241.6 20.0 %collective-permute-start.29 = (bf16[8,64,768]{2,1,0:T(8,128)(2,1)S(1)}, bf16[8,64,768]{2,1,0:T(8,128)(2,1)S(1)}, u32[]{:S(2)}, u32[]{:S(2)}) collective-permute-start(bf16[8,64,768]{2,1,0:T(8,128)(2,1)S(1)} %all-to-all-done.3.refs_0_), channel_id=1, source_target_pairs={{0,16},{16,0},{1,17},{17,1},{2,18},{18,2},{3,19},{19,3},{4,20},{20... | collective-permute-start | bytes 2359304 | tf_op jit(solution)/shard_map/down_in/ppermute | solution.py:298
  243.2 19.6 %collective-permute-start.30 = (bf16[8,64,768]{2,1,0:T(8,128)(2,1)S(1)}, bf16[8,64,768]{2,1,0:T(8,128)(2,1)S(1)}, u32[]{:S(2)}, u32[]{:S(2)}) collective-permute-start(bf16[8,64,768]{2,1,0:T(8,128)(2,1)S(1)} %all-to-all-done.3.refs_0_), channel_id=1, source_target_pairs={{0,1},{1,0},{2,3},{3,2},{4,5},{5,4},{6,7},{7,6},{8,9},{9,8},{10,11... | collective-permute-start | bytes 2359304 | tf_op jit(solution)/shard_map/down_in/ppermute | solution.py:298
  312.8 25.6 %collective-permute-start.38 = (bf16[128,4096]{1,0:T(8,128)(2,1)S(1)}, bf16[128,4096]{1,0:T(8,128)(2,1)S(1)}, u32[]{:S(2)}, u32[]{:S(2)}) collective-permute-start(bf16[128,4096]{1,0:T(8,128)(2,1)S(1)} %add_convert_fusion.2), channel_id=1, source_target_pairs={{0,4},{4,6},{6,2},{2,0},{1,5},{5,7},{7,3},{3,1},{8,12},{12,14},{14... | collective-permute-start | bytes 3145736 | tf_op jit(solution)/shard_map/parts_out/ppermute | solution.py:283
  334.3 53.6 %collective-permute-start.41 = (bf16[8,2,64,1152]{3,2,0,1:T(8,128)(2,1)}, bf16[8,2,64,1152]{3,2,0,1:T(8,128)(2,1)S(1)}, u32[]{:S(2)}, u32[]{:S(2)}) collective-permute-start(bf16[8,2,64,1152]{3,2,0,1:T(8,128)(2,1)} %copy.68), channel_id=1, source_target_pairs={{0,16},{16,0},{1,17},{17,1},{2,18},{18,2},{3,19},{19,3},{4,20},{20... | collective-permute-start | bytes 7077896 | tf_op jit(solution)/shard_map/ffn_grad/ppermute | solution.py:419
  340.2 25.9 %collective-permute-start.39 = (bf16[128,4096]{1,0:T(8,128)(2,1)S(1)}, bf16[128,4096]{1,0:T(8,128)(2,1)}, u32[]{:S(2)}, u32[]{:S(2)}) collective-permute-start(bf16[128,4096]{1,0:T(8,128)(2,1)S(1)} %add_convert_fusion.1), channel_id=1, source_target_pairs={{0,4},{4,6},{6,2},{2,0},{1,5},{5,7},{7,3},{3,1},{8,12},{12,14},{14... | collective-permute-start | bytes 3145736 | tf_op jit(solution)/shard_map/parts_out/ppermute | solution.py:283
  346.8 41.1 %collective-permute-start.42 = (bf16[2,8,64,384]{3,2,1,0:T(8,128)(2,1)}, bf16[2,8,64,384]{3,2,1,0:T(8,128)(2,1)S(1)}, u32[]{:S(2)}, u32[]{:S(2)}) collective-permute-start(bf16[2,8,64,384]{3,2,1,0:T(8,128)(2,1)} %dynamic-slice_bitcast_fusion.4), channel_id=1, source_target_pairs={{0,1},{1,0},{2,3},{3,2},{4,5},{5,4},{6,7},{7,6},{8,9},{9,8},{10,11... | collective-permute-start | bytes 2359304 | tf_op jit(solution)/shard_map/ffn_grad/ppermute | solution.py:430
  347.7 51.9 %collective-permute-start.43 = (bf16[2,8,64,768]{3,2,1,0:T(8,128)(2,1)}, bf16[2,8,64,768]{3,2,1,0:T(8,128)(2,1)S(1)}, u32[]{:S(2)}, u32[]{:S(2)}) collective-permute-start(bf16[2,8,64,768]{3,2,1,0:T(8,128)(2,1)} %dynamic-slice_bitcast_fusion.1), channel_id=1, source_target_pairs={{0,1},{1,0},{2,3},{3,2},{4,5},{5,4},{6,7},{7,6},{8,9},{9,8},{10,11... | collective-permute-start | bytes 4718600 | tf_op jit(solution)/shard_map/ffn_grad/ppermute | solution.py:430
  368.4 41.4 %collective-permute-start.40 = (bf16[128,4096]{1,0:T(8,128)(2,1)S(1)}, bf16[128,4096]{1,0:T(8,128)(2,1)S(1)}, u32[]{:S(2)}, u32[]{:S(2)}) collective-permute-start(bf16[128,4096]{1,0:T(8,128)(2,1)S(1)} %add_convert_fusion), channel_id=1, source_target_pairs={{0,4},{4,6},{6,2},{2,0},{1,5},{5,7},{7,3},{3,1},{8,12},{12,14},{14... | collective-permute-start | bytes 3145736 | tf_op jit(solution)/shard_map/parts_out/ppermute | solution.py:283
  402.3 26.8 %collective-permute-start.45 = (bf16[8,64,768]{2,1,0:T(8,128)(2,1)}, bf16[8,64,768]{2,1,0:T(8,128)(2,1)}, u32[]{:S(2)}, u32[]{:S(2)}) collective-permute-start(bf16[8,64,768]{2,1,0:T(8,128)(2,1)} %slice_bitcast_fusion), channel_id=1, source_target_pairs={{0,16},{16,0},{1,17},{17,1},{2,18},{18,2},{3,19},{19,3},{4,20},{20... | collective-permute-start | bytes 2359304 | tf_op jit(solution)/shard_map/ffn_grad/ppermute | solution.py:419
  402.9 28.8 %collective-permute-start.44 = (bf16[8,64,1152]{2,1,0:T(8,128)(2,1)}, bf16[8,64,1152]{2,1,0:T(8,128)(2,1)}, u32[]{:S(2)}, u32[]{:S(2)}) collective-permute-start(bf16[8,64,1152]{2,1,0:T(8,128)(2,1)} %dynamic-slice_bitcast_fusion.2), channel_id=1, source_target_pairs={{0,1},{1,0},{2,3},{3,2},{4,5},{5,4},{6,7},{7,6},{8,9},{9,8},{10,11... | collective-permute-start | bytes 3538952 | tf_op jit(solution)/shard_map/ffn_grad/ppermute | solution.py:430
  406.1 22.9 %collective-permute-start.46 = (bf16[8,64,384]{2,1,0:T(8,128)(2,1)S(1)}, bf16[8,64,384]{2,1,0:T(8,128)(2,1)}, u32[]{:S(2)}, u32[]{:S(2)}) collective-permute-start(bf16[8,64,384]{2,1,0:T(8,128)(2,1)S(1)} %slice_bitcast_fusion.1), channel_id=1, source_target_pairs={{0,16},{16,0},{1,17},{17,1},{2,18},{18,2},{3,19},{19,3},{4,20},{20... | collective-permute-start | bytes 1179656 | tf_op jit(solution)/shard_map/ffn_grad/ppermute | solution.py:419
  422.9 16.8 %all-to-all-start.4 = ((bf16[8,128,256]{2,1,0:T(8,128)(2,1)}), bf16[8,128,256]{2,1,0:T(8,128)(2,1)}, u32[]{:S(2)}, u32[]{:S(2)}) async-start(bf16[8,128,256]{2,1,0:T(8,128)(2,1)} %bitcast.279), calls=%async_computation.4 | async-start | bytes 1048576 | tf_op jit(solution)/shard_map/heads_in/all_to_all | solution.py:770
  439.7 58.0 %all-to-all-start.5 = ((bf16[8,64,2304]{2,1,0:T(8,128)(2,1)}), bf16[8,64,2304]{2,1,0:T(8,128)(2,1)S(1)}, u32[]{:S(2)}, u32[]{:S(2)}) async-start(bf16[8,64,2304]{2,1,0:T(8,128)(2,1)} %pad_maximum_fusion.4), calls=%async_computation.5 | async-start | bytes 4718592 | tf_op jit(solution)/shard_map/ffn_back/all_to_all | solution.py:770
  479.8 33.3 %collective-permute-start.49 = (bf16[512,768]{1,0:T(8,128)(2,1)}, bf16[512,768]{1,0:T(8,128)(2,1)}, u32[]{:S(2)}, u32[]{:S(2)}) collective-permute-start(bf16[512,768]{1,0:T(8,128)(2,1)} %dynamic-slice_bitcast_fusion.3), channel_id=1, source_target_pairs={{0,16},{16,0},{1,17},{17,1},{2,18},{18,2},{3,19},{19,3},{4,20},{20... | collective-permute-start | bytes 2359304 | tf_op jit(solution)/shard_map/qkv_back/ppermute | solution.py:306
  481.0 16.8 %collective-permute-start.50 = (bf16[64,2048]{1,0:T(8,128)(2,1)S(1)}, bf16[64,2048]{1,0:T(8,128)(2,1)S(1)}, u32[]{:S(2)}, u32[]{:S(2)}) collective-permute-start(bf16[64,2048]{1,0:T(8,128)(2,1)S(1)} %get-tuple-element.513), channel_id=1, source_target_pairs={{0,2},{2,4},{4,6},{6,7},{7,5},{5,3},{3,1},{1,0},{8,10},{10,12},{12... | collective-permute-start | bytes 786440 | tf_op jit(solution)/shard_map/normed_out/ppermute | solution.py:192
  482.6 21.3 %collective-permute-start.51 = (bf16[64,2048]{1,0:T(8,128)(2,1)S(1)}, bf16[64,2048]{1,0:T(8,128)(2,1)}, u32[]{:S(2)}, u32[]{:S(2)}) collective-permute-start(bf16[64,2048]{1,0:T(8,128)(2,1)S(1)} %get-tuple-element.526), channel_id=1, source_target_pairs={{2,0},{4,2},{6,4},{7,6},{5,7},{3,5},{1,3},{0,1},{10,8},{12,10},{14... | collective-permute-start | bytes 786440 | tf_op jit(solution)/shard_map/normed_out/ppermute | solution.py:192
  506.2 18.9 %collective-permute-start.56 = (bf16[128,2048]{1,0:T(8,128)(2,1)}, bf16[128,2048]{1,0:T(8,128)(2,1)}, u32[]{:S(2)}, u32[]{:S(2)}) collective-permute-start(bf16[128,2048]{1,0:T(8,128)(2,1)} %get-tuple-element.531), channel_id=1, source_target_pairs={{0,2},{2,4},{4,6},{6,7},{7,5},{5,3},{3,1},{1,0},{8,10},{10,12},{12... | collective-permute-start | bytes 1572872 | tf_op jit(solution)/shard_map/normed_out/ppermute | solution.py:192
  506.8 18.3 %collective-permute-start.57 = (bf16[128,2048]{1,0:T(8,128)(2,1)S(1)}, bf16[128,2048]{1,0:T(8,128)(2,1)}, u32[]{:S(2)}, u32[]{:S(2)}) collective-permute-start(bf16[128,2048]{1,0:T(8,128)(2,1)S(1)} %get-tuple-element.537), channel_id=1, source_target_pairs={{2,0},{4,2},{6,4},{7,6},{5,7},{3,5},{1,3},{0,1},{10,8},{12,10},{14... | collective-permute-start | bytes 1572872 | tf_op jit(solution)/shard_map/normed_out/ppermute | solution.py:192
  510.8 21.3 %collective-permute-start.53 = (bf16[128,512]{1,0:T(8,128)(2,1)S(1)}, bf16[128,512]{1,0:T(8,128)(2,1)S(1)}, u32[]{:S(2)}, u32[]{:S(2)}) collective-permute-start(bf16[128,512]{1,0:T(8,128)(2,1)S(1)} %bitcast.289), channel_id=1, source_target_pairs={{0,6},{2,0},{4,2},{6,4},{1,7},{3,1},{5,3},{7,5},{8,14},{10,8},{12,... | collective-permute-start | bytes 393224 | tf_op jit(solution)/shard_map/grad_attn_in/ppermute | solution.py:306
  511.3 20.7 %collective-permute-start.54 = (bf16[128,512]{1,0:T(8,128)(2,1)S(1)}, bf16[128,512]{1,0:T(8,128)(2,1)S(1)}, u32[]{:S(2)}, u32[]{:S(2)}) collective-permute-start(bf16[128,512]{1,0:T(8,128)(2,1)S(1)} %bitcast.290), channel_id=1, source_target_pairs={{0,4},{2,6},{4,0},{6,2},{1,5},{3,7},{5,1},{7,3},{8,12},{10,14},{12... | collective-permute-start | bytes 393224 | tf_op jit(solution)/shard_map/grad_attn_in/ppermute | solution.py:306
  533.9 24.3 %collective-permute-start.59 = (bf16[2,4,2,64,512]{4,3,1,2,0:T(8,128)(2,1)S(1)}, bf16[2,4,2,64,512]{4,3,1,2,0:T(8,128)(2,1)S(1)}, u32[]{:S(2)}, u32[]{:S(2)}) collective-permute-start(bf16[2,4,2,64,512]{4,3,1,2,0:T(8,128)(2,1)S(1)} %bitcast.283), channel_id=1, source_target_pairs={{0,8},{8,0},{1,9},{9,1},{2,10},{10,2},{3,11},{11,3},{4,12},{12,4},... | collective-permute-start | bytes 3145736 | tf_op jit(solution)/shard_map/out_back/ppermute | solution.py:306
  534.1 18.6 %collective-permute-start.61 = (bf16[128,2048]{1,0:T(8,128)(2,1)}, bf16[128,2048]{1,0:T(8,128)(2,1)}, u32[]{:S(2)}, u32[]{:S(2)}) collective-permute-start(bf16[128,2048]{1,0:T(8,128)(2,1)} %get-tuple-element.551), channel_id=1, source_target_pairs={{2,0},{4,2},{6,4},{7,6},{5,7},{3,5},{1,3},{0,1},{10,8},{12,10},{14... | collective-permute-start | bytes 1572872 | tf_op jit(solution)/shard_map/normed_out/ppermute | solution.py:192
  536.1 30.5 %all-to-all-start.6 = ((bf16[8,64,768]{2,1,0:T(8,128)(2,1)}), bf16[8,64,768]{2,1,0:T(8,128)(2,1)}, u32[]{:S(2)}, u32[]{:S(2)}) async-start(bf16[8,64,768]{2,1,0:T(8,128)(2,1)} %bitcast.92), calls=%async_computation.6 | async-start | bytes 1572864 | tf_op jit(solution)/shard_map/qkv_back/all_to_all | solution.py:770
  555.5 22.4 %collective-permute-start.64 = (bf16[128,2048]{1,0:T(8,128)(2,1)}, bf16[128,2048]{1,0:T(8,128)(2,1)}, u32[]{:S(2)}, u32[]{:S(2)}) collective-permute-start(bf16[128,2048]{1,0:T(8,128)(2,1)} %get-tuple-element.554), channel_id=1, source_target_pairs={{0,2},{2,4},{4,6},{6,7},{7,5},{5,3},{3,1},{1,0},{8,10},{10,12},{12... | collective-permute-start | bytes 1572872 | tf_op jit(solution)/shard_map/normed_out/ppermute | solution.py:192
  555.5 22.6 %collective-permute-start.65 = (bf16[128,2048]{1,0:T(8,128)(2,1)}, bf16[128,2048]{1,0:T(8,128)(2,1)}, u32[]{:S(2)}, u32[]{:S(2)}) collective-permute-start(bf16[128,2048]{1,0:T(8,128)(2,1)} %get-tuple-element.558), channel_id=1, source_target_pairs={{2,0},{4,2},{6,4},{7,6},{5,7},{3,5},{1,3},{0,1},{10,8},{12,10},{14... | collective-permute-start | bytes 1572872 | tf_op jit(solution)/shard_map/normed_out/ppermute | solution.py:192
  559.5 22.5 %collective-permute-start.63 = (bf16[4,64,512]{2,1,0:T(8,128)(2,1)}, bf16[4,64,512]{2,1,0:T(8,128)(2,1)S(1)}, u32[]{:S(2)}, u32[]{:S(2)}) collective-permute-start(bf16[4,64,512]{2,1,0:T(8,128)(2,1)} %get-tuple-element.613), channel_id=1, source_target_pairs={{0,1},{1,0},{16,17},{17,16},{2,3},{3,2},{18,19},{19,18},{4,5},{5,4... | collective-permute-start | bytes 786440 | tf_op jit(solution)/shard_map/out_back/ppermute | solution.py:391
  561.5 20.4 %collective-permute-start.66 = (bf16[4,64,512]{2,1,0:T(8,128)(2,1)}, bf16[4,64,512]{2,1,0:T(8,128)(2,1)}, u32[]{:S(2)}, u32[]{:S(2)}) collective-permute-start(bf16[4,64,512]{2,1,0:T(8,128)(2,1)} %get-tuple-element.615), channel_id=1, source_target_pairs={{0,16},{1,17},{16,0},{17,1},{2,18},{3,19},{18,2},{19,3},{4,20},{5,... | collective-permute-start | bytes 786440 | tf_op jit(solution)/shard_map/out_back/ppermute | solution.py:391
  562.1 19.8 %collective-permute-start.67 = (bf16[4,64,512]{2,1,0:T(8,128)(2,1)}, bf16[4,64,512]{2,1,0:T(8,128)(2,1)}, u32[]{:S(2)}, u32[]{:S(2)}) collective-permute-start(bf16[4,64,512]{2,1,0:T(8,128)(2,1)} %get-tuple-element.614), channel_id=1, source_target_pairs={{0,17},{1,16},{16,1},{17,0},{2,19},{3,18},{18,3},{19,2},{4,21},{5,... | collective-permute-start | bytes 786440 | tf_op jit(solution)/shard_map/out_back/ppermute | solution.py:391
  (103 other events, 1178.8 us)
